TPU v7x, 256 devices: a whole 4x4x8 slice. The times are simulated.
256 devices in a mesh: dp: 8 (over z_lo, x), tensor: 32 (over y, z_hi, core).
Axes of the slice: x: 4, y: 4, z: 8 (z_hi: 4, z_lo: 2; z = z_hi * 2 + z_lo), core: 2. Of those that a mesh axis runs over, the one named last changes fastest.
Arguments:
- activations: bfloat16 [24, 256, 16384], P('dp', None, 'tensor'), may hold values from -6 to 6
- out_grads: bfloat16 [24, 256, 8192], P('dp', 'tensor'), may hold values from -0.5 to 0.5
Outputs:
- fisher: float32 [8192, 16384], P('dp', 'tensor')
All inputs are finite; a program needn't handle non-finite values.
Results may differ from a plain program's by a relative error of at most 0.0003.
Values may be sent and summed in bfloat16 or wider, within the bound.
No kernel may reach another device: no remote copies, remote signals or barrier semaphores. Data moves between devices by JAX's collectives and lax.ppermute only.
A program may use at most 128 MiB of HBM per device.

v0:
```python
import jax
import jax.numpy as jnp
from jax import lax
from jax.sharding import PartitionSpec as P


def squared_grad(grads, acts):
    grad = lax.dot_general(
        grads, acts, (((0,), (0,)), ((), ())), preferred_element_type=jnp.float32
    )
    return grad * grad


def per_device(activations, out_grads):
    seq_dev = activations.shape[0]
    n_data = lax.axis_size("dp")
    seq_all = seq_dev * n_data
    width_out = out_grads.shape[2]
    feat_dev = activations.shape[2]
    full_grads = lax.all_gather(out_grads, "tensor", axis=1, tiled=True)

    def add_seq(index, total):
        grads = lax.dynamic_index_in_dim(full_grads, index, 0, keepdims=False)
        acts = lax.dynamic_index_in_dim(activations, index, 0, keepdims=False)
        return total + squared_grad(grads, acts)

    total = lax.psum_scatter(
        lax.fori_loop(
            0,
            seq_dev,
            add_seq,
            jnp.zeros((lax.axis_size("dp") * (width_out // n_data), feat_dev), jnp.float32),
        ),
        "dp",
        scatter_dimension=0,
        tiled=True,
    )
    return total / jnp.float32(seq_all)


def solution(mesh):
    placed = (P("dp", None, "tensor"), P("dp", "tensor", None))
    return jax.shard_map(
        per_device, mesh=mesh, in_specs=placed, out_specs=P("dp", "tensor"), check_vma=False
    )
```

profile of v0, /device:TPU:1, one launch (start us, length us, event | category | flops | bytes accessed | tf_op | source)
XLA Modules:
  0.0 335.9 jit_solution(2887561907193449714)
XLA Ops:
  6.5 0.0 all-gather.2.cloned.1.call-start
  6.5 0.7 all-gather.2.cloned.1.call-update
  7.3 0.0 reduce-scatter.2.cloned.1.call-start
  7.3 99.1 %all-gather.2.cloned.1.call-done = bf16[3,256,8192]{2,1,0:T(8,128)(2,1)} async-done(((bf16[3,8,8192]{2,1,0:T(8,128)(2,1)}), bf16[3,256,8192]{2,1,0:T(8,128)(2,1)}) %all-gather.2.cloned.1.call-update) | async-done | bytes 12582928 | tf_op jit(solution)/shard_map/all_gather | solution.py:20
  106.5 40.8 %while.14 = (s32[]{:T(128)}, f32[8192,512]{1,0:T(8,128)}, bf16[3,256,8192]{2,1,0:T(8,128)(2,1)}, bf16[3,256,512]{2,1,0:T(8,128)(2,1)}, s32[]{:T(128)}, /*index=5*/s32[]{:T(128)}) while((s32[]{:T(128)}, f32[8192,512]{1,0:T(8,128)}, bf16[3,256,8192]{2,1,0:T(8,128)(2,1)}, bf16[3,256,512]{2,1,0:T(8,128)(2,1)}, s32[]{:T(128)}, ...), condition=%wide.region_1.2_spmd.clone, body=%wide.region_0.1_spmd.clone.sunk | while | flops 2160066560 | bytes 38012500 | solution.py:28
  106.5 10.3 %select_add_fusion.2 = f32[8192,512]{1,0:T(8,128)} fusion(f32[8192,512]{1,0:T(8,128)} %get-tuple-element.140, pred[]{:T(512)S(6)} %compare.3, bf16[3,256,8192]{2,1,0:T(8,128)(2,1)} %get-tuple-element.147, s32[]{:T(128)S(6)} %copy.5, bf16[3,256,512]{2,1,0:T(8,128)(2,1)} %get-tuple-element.148), kind=kOutput, calls=%fused_computation.clone.1 | convolution fusion | flops 2160066560 | bytes 38012416 | tf_op jit(solution)/shard_map/while/body/eval_jaxpr/dot_general | solution.py:8
  116.8 15.2 %select_add_fusion.2 = f32[8192,512]{1,0:T(8,128)} fusion(f32[8192,512]{1,0:T(8,128)} %get-tuple-element.140, pred[]{:T(512)S(6)} %compare.3, bf16[3,256,8192]{2,1,0:T(8,128)(2,1)} %get-tuple-element.147, s32[]{:T(128)S(6)} %copy.5, bf16[3,256,512]{2,1,0:T(8,128)(2,1)} %get-tuple-element.148), kind=kOutput, calls=%fused_computation.clone.1 | convolution fusion | flops 2160066560 | bytes 38012416 | tf_op jit(solution)/shard_map/while/body/eval_jaxpr/dot_general | solution.py:8
  132.0 15.2 %select_add_fusion.2 = f32[8192,512]{1,0:T(8,128)} fusion(f32[8192,512]{1,0:T(8,128)} %get-tuple-element.140, pred[]{:T(512)S(6)} %compare.3, bf16[3,256,8192]{2,1,0:T(8,128)(2,1)} %get-tuple-element.147, s32[]{:T(128)S(6)} %copy.5, bf16[3,256,512]{2,1,0:T(8,128)(2,1)} %get-tuple-element.148), kind=kOutput, calls=%fused_computation.clone.1 | convolution fusion | flops 2160066560 | bytes 38012416 | tf_op jit(solution)/shard_map/while/body/eval_jaxpr/dot_general | solution.py:8
  147.2 0.0 reduce-scatter.2.cloned.1.call-update
  147.3 178.7 %reduce-scatter.2.cloned.1.call-done = f32[1024,512]{1,0:T(8,128)} async-done(((f32[8192,512]{1,0:T(8,128)}), f32[1024,512]{1,0:T(8,128)}) %reduce-scatter.2.cloned.1.call-update) | async-done | bytes 2097168 | tf_op jit(solution)/shard_map/reduce_scatter | solution.py:27
  325.9 3.2 broadcast_multiply_fusion
  (1 shorter events, 0.0 us)
Async XLA Ops:
  6.5 99.9 %all-gather.2.cloned.1.call-start = ((), (), s32[]{:S(2)}) async-start(), calls=%async_computation.1 | async-start | bytes 12976128 | tf_op jit(solution)/shard_map/all_gather | solution.py:20
  7.3 318.7 %reduce-scatter.2.cloned.1.call-start = ((), (), s32[]{:S(2)}) async-start(), calls=%async_computation.2 | async-start | bytes 18874368 | tf_op jit(solution)/shard_map/reduce_scatter | solution.py:27
Sparse Core Ops, SparseCore 0:
  10.0 96.4 all-gather.1
  147.4 178.5 reduce-scatter.1
where the time goes:
time: 336 us
  waiting for transfers between devices  279 us (83%)
  matrix products  40.8 us (12%)
  between operations  13.4 us (4%)
    reduce_scatter x1, waiting for transfers between devices, per_device(): lax.psum_scatter(lax.fori_loop(0, seq_dev, add_seq, jnp.zeros((lax.axis_s...  179 us
    all_gather x1, waiting for transfers between devices, per_device(): full_grads = lax.all_gather(out_grads, 'tensor', axis=1, tiled=True)  99.1 us
    dot_general x3, matrix products, squared_grad(): lax.dot_general(grads, acts, (((0,), (0,)), ((), ())), preferred_element_...  40.8 us
  transfers between devices with their start and end apart: 2, of which 2 were waited for; matrix products, arithmetic and copies ran while one was open for 0% of the time, Pallas kernels for 0%

commit v1 on v0

v1 whole, which is shorter than its diff:
```python
import functools

import jax
import jax.numpy as jnp
from jax import lax
from jax.experimental import pallas as pl
from jax.experimental.pallas import tpu as pltpu
from jax.sharding import Mesh, PartitionSpec as P

AXES = ("zlo", "x", "y", "zhi", "core")
SIZES = (2, 4, 4, 4, 2)
SEQS_DP = 3
ROWS = 16


def shift(value, axis, by):
    n = lax.axis_size(axis)
    return lax.ppermute(value, axis, [(i, (i + by) % n) for i in range(n)])


def square_sum(first, last, seqs, *refs):
    place, acts, grads, rest = refs[0], refs[1:5], refs[5:13], refs[13:]
    before, out, total = (None, *rest) if first else rest
    step = pl.program_id(0)
    half = grads[0].shape[-1]
    for source in range(4):
        rows = [
            acts[source][0, pl.ds(pl.multiple_of(place[k], ROWS), ROWS), :]
            for k in range(16)
        ]
        act = jnp.concatenate(rows, axis=0)
        for side in range(2):
            grad = jnp.concatenate(
                [grads[4 * side + k // 4][k % 4, source, 0] for k in range(16)], axis=0
            )
            part = lax.dot_general(
                grad, act, (((0,), (0,)), ((), ())), preferred_element_type=jnp.float32
            )
            at = slice(side * half, (side + 1) * half)
            if source == 0:

                @pl.when(step == 0)
                def _():
                    total[at, :] = part * part if first else before[at, :] + part * part

                @pl.when(step > 0)
                def _():
                    total[at, :] += part * part
            else:
                total[at, :] += part * part

    @pl.when(step == SEQS_DP - 1)
    def _():
        if not last:
            out[...] = total[...]
        else:
            core = place[16]
            for side, where in enumerate((core, 1 - core)):
                at = slice(side * half, (side + 1) * half)
                out[pl.ds(pl.multiple_of(where * half, half), half), :] = (
                    total[at, :] / jnp.float32(seqs)
                )


def add_group(last, seqs, place, acts, grads, before=None):
    _, tokens, feats = acts[0].shape
    half = grads[0].shape[-1]
    shape = (2 * half, feats)
    one = pl.Buffered(1)
    specs = [pl.BlockSpec(memory_space=pltpu.SMEM)]
    specs += [pl.BlockSpec((1, tokens, feats), lambda j: (j, 0, 0))] * 4
    specs += [pl.BlockSpec((4, 4, 1, ROWS, half), lambda j: (0, 0, j, 0, 0))] * 8
    args = [place, *acts, *grads]
    if before is not None:
        specs.append(pl.BlockSpec(shape, lambda j: (0, 0), pipeline_mode=one))
        args.append(before)
    return pl.pallas_call(
        functools.partial(square_sum, before is None, last, seqs),
        grid=(SEQS_DP,),
        in_specs=specs,
        out_specs=pl.BlockSpec(shape, lambda j: (0, 0), pipeline_mode=one),
        out_shape=jax.ShapeDtypeStruct(shape, jnp.float32),
        scratch_shapes=[pltpu.VMEM(shape, jnp.float32)],
        compiler_params=pltpu.CompilerParams(vmem_limit_bytes=56 * 2**20),
        cost_estimate=pl.CostEstimate(
            flops=2 * 12 * tokens * 2 * half * feats,
            bytes_accessed=16 * 2**20,
            transcendentals=0,
        ),
    )(*args)


def to_owner(block, core):
    block = block.transpose(3, 2, 0, 1, 4)
    mine = lax.dynamic_index_in_dim(block, core, 0, keepdims=False)
    other = lax.dynamic_index_in_dim(block, 1 - core, 0, keepdims=False)
    other = shift(other, "core", 1)
    low = jnp.where(core == 0, mine, other)
    high = jnp.where(core == 0, other, mine)
    both = jnp.concatenate([low, high], axis=2)
    x = lax.axis_index("x")

    def piece(by):
        return lax.dynamic_index_in_dim(both, (x + by) % 4, 0, keepdims=False)

    return jnp.stack(
        [piece(0), shift(piece(1), "x", 1), shift(piece(-1), "x", -1), shift(piece(2), "x", 2)]
    )


def ring(block, axis, on):
    below = shift(block, axis, 1)
    above = shift(block, axis, -1)
    far = shift(below, axis, 1) if on > 0 else shift(above, axis, -1)
    return [block, below, above, far]


def per_device(activations, out_grads):
    zlo, y, zhi, core = (lax.axis_index(a) for a in ("zlo", "y", "zhi", "core"))
    seq_dev, tokens, _ = activations.shape
    width = out_grads.shape[2]
    half = width // 16
    seqs = seq_dev * 8

    by_z = out_grads.reshape(seq_dev, out_grads.shape[1], 2, 4, 2, half)
    near = lax.dynamic_index_in_dim(by_z, zlo, 2, keepdims=False)
    away = lax.dynamic_index_in_dim(by_z, 1 - zlo, 2, keepdims=False)

    offsets = (0, -1, 1, 2)
    place = [
        ROWS * (((y + dy) % 4) * 4 + (zhi + dz) % 4) for dy in offsets for dz in offsets
    ]
    place = jnp.stack([*place, core]).astype(jnp.int32)

    total = None
    for group in range(2):
        on = 1 if group == 0 else -1
        acts = activations if group == 0 else shift(activations, "zlo", 1)
        block = near if group == 0 else shift(away, "zlo", 1)
        block = to_owner(block, core)
        column = jnp.stack(ring(block, "zhi", on))
        mine = ring(column, "y", on)
        theirs = [shift(part, "core", 1) for part in mine]
        total = add_group(
            group == 1, seqs, place, ring(acts, "x", on), [*mine, *theirs], total
        )
    return total


def solution(mesh):
    fine = Mesh(mesh.devices.reshape(SIZES), AXES)
    dp, tensor = AXES[:2], AXES[2:]
    placed = (P(dp, None, tensor), P(dp, tensor, None))
    return jax.shard_map(
        per_device, mesh=fine, in_specs=placed, out_specs=P(dp, tensor), check_vma=False
    )
```

time: 336 us -> 149 us (0.44)
  waiting for transfers between devices: 279 us -> 63.1 us
  starting transfers between devices: 0.04 us -> 61.1 us
  matrix products: 40.8 us -> 0 us
  Pallas kernels: 0 us -> 18.8 us
  between operations: 13.4 us -> 0.39 us
  local copies, waits for them, and re-layouts: 0 us -> 3.47 us
    reduce_scatter x1 -> x0, waiting for transfers between devices: 179 us -> none  [per_device(): lax.psum_scatter(lax.fori_loop(0, seq_dev, add_seq, jnp.zeros((lax.axis_s...]
    all_gather x1 -> x0, waiting for transfers between devices: 99.1 us -> none  [per_device(): full_grads = lax.all_gather(out_grads, 'tensor', axis=1, tiled=True)]
    ppermute x0 -> x36, waiting for transfers between devices: none -> 63.1 us  [shift(): return lax.ppermute(value, axis, [(i, (i + by) % n) for i in range(n)])]
    ppermute x0 -> x36, starting transfers between devices: none -> 61.1 us  [shift(): return lax.ppermute(value, axis, [(i, (i + by) % n) for i in range(n)])]
    dot_general x3 -> x0, matrix products: 40.8 us -> none  [squared_grad(): lax.dot_general(grads, acts, (((0,), (0,)), ((), ())), preferred_element_...]
    pallas_call x0 -> x2, Pallas kernels: none -> 18.8 us  [add_group(): pl.pallas_call(functools.partial(square_sum, before is None, last, seqs),...]
  transfers between devices with their start and end apart: 2 -> 36, of which waited for: 2 -> 13; matrix products, arithmetic and copies ran while one was open for 0% -> 1% of each run, Pallas kernels for 0% -> 6%
where the time goes in v1:
time: 149 us; the launch traced here: 147 us
  waiting for transfers between devices  63.1 us (42%)
  starting transfers between devices  61.1 us (41%)
  Pallas kernels  18.8 us (13%)
  local copies, waits for them, and re-layouts  3.47 us (2%)
    ppermute x36, waiting for transfers between devices, shift(): return lax.ppermute(value, axis, [(i, (i + by) % n) for i in range(n)])  63.1 us
    ppermute x36, starting transfers between devices, shift(): return lax.ppermute(value, axis, [(i, (i + by) % n) for i in range(n)])  61.1 us
    pallas_call x2, Pallas kernels, add_group(): pl.pallas_call(functools.partial(square_sum, before is None, last, seqs),...  18.8 us
  transfers between devices with their start and end apart: 36, of which 13 were waited for; matrix products, arithmetic and copies ran while one was open for 1% of the time, Pallas kernels for 6%

profile of v1, /device:TPU:1, one launch (start us, length us, event | category | flops | bytes accessed | tf_op | source)
XLA Modules:
  0.0 147.2 jit_solution(17276289342074736091)
XLA Ops:
  1.0 3.3 %collective-permute-start.22 = (bf16[4,3,8,512]{3,2,1,0:T(8,128)(2,1)S(1)}, bf16[4,3,8,512]{3,2,1,0:T(8,128)(2,1)S(1)}, u32[]{:S(2)}, u32[]{:S(2)}) collective-permute-start(bf16[4,3,8,512]{3,2,1,0:T(8,128)(2,1)S(1)} %bitcast.82), channel_id=1, source_target_pairs={{0,1},{1,0},{2,3},{3,2},{4,5},{5,4},{6,7},{7,6},{8,9},{9,8},{10,11... | collective-permute-start | bytes 294920 | tf_op jit(solution)/shard_map/ppermute | solution.py:18
  6.5 5.3 %collective-permute-done.4 = bf16[3,8,4,2,512]{4,1,0,2,3:T(8,128)(2,1)S(1)} collective-permute-done((bf16[3,8,4,2,512]{4,1,0,2,3:T(8,128)(2,1)S(1)}, bf16[3,8,4,2,512]{4,1,0,2,3:T(8,128)(2,1)S(1)}, u32[]{:S(2)}, u32[]{:S(2)}) %collective-permute-start.4) | collective-permute-done | bytes 196640 | tf_op jit(solution)/shard_map/ppermute | solution.py:18
  13.7 1.9 %collective-permute-start.24 = (bf16[3,16,512]{2,1,0:T(8,128)(2,1)S(1)}, bf16[3,16,512]{2,1,0:T(8,128)(2,1)S(1)}, u32[]{:S(2)}, u32[]{:S(2)}) collective-permute-start(bf16[3,16,512]{2,1,0:T(8,128)(2,1)S(1)} %get-tuple-element.13), channel_id=1, source_target_pairs={{0,96},{32,0},{64,32},{96,64},{1,97},{33,1},{65,33},{97,65},{2,98}... | collective-permute-start | bytes 147464 | tf_op jit(solution)/shard_map/ppermute | solution.py:18
  17.7 9.0 %collective-permute-done.23 = bf16[3,16,512]{2,1,0:T(8,128)(2,1)S(1)} collective-permute-done((bf16[3,16,512]{2,1,0:T(8,128)(2,1)S(1)}, bf16[3,16,512]{2,1,0:T(8,128)(2,1)S(1)}, u32[]{:S(2)}, u32[]{:S(2)}) %collective-permute-start.23) | collective-permute-done | bytes 49184 | tf_op jit(solution)/shard_map/ppermute | solution.py:18
  26.8 2.5 %collective-permute-start.26 = (bf16[4,3,16,512]{3,2,1,0:T(8,128)(2,1)S(1)}, bf16[4,3,16,512]{3,2,1,0:T(8,128)(2,1)S(1)}, u32[]{:S(2)}, u32[]{:S(2)}) collective-permute-start(bf16[4,3,16,512]{3,2,1,0:T(8,128)(2,1)S(1)} %get-tuple-element.10), channel_id=1, source_target_pairs={{0,2},{2,4},{4,6},{6,0},{1,3},{3,5},{5,7},{7,1},{8,10},{10,12},{12... | collective-permute-start | bytes 589832 | tf_op jit(solution)/shard_map/ppermute | solution.py:18
  29.7 1.5 %collective-permute-done.8 = bf16[3,16,512]{2,1,0:T(8,128)(2,1)S(1)} collective-permute-done((bf16[3,16,512]{2,1,0:T(8,128)(2,1)S(1)}, bf16[3,16,512]{2,1,0:T(8,128)(2,1)S(1)}, u32[]{:S(2)}, u32[]{:S(2)}) %collective-permute-start.8) | collective-permute-done | bytes 49184 | tf_op jit(solution)/shard_map/ppermute | solution.py:18
  31.2 4.8 %collective-permute-start.10 = (bf16[4,3,16,512]{3,2,1,0:T(8,128)(2,1)S(1)}, bf16[4,3,16,512]{3,2,1,0:T(8,128)(2,1)S(1)}, u32[]{:S(2)}, u32[]{:S(2)}) collective-permute-start(bf16[4,3,16,512]{3,2,1,0:T(8,128)(2,1)S(1)} %get-tuple-element.18), channel_id=1, source_target_pairs={{0,6},{2,0},{4,2},{6,4},{1,7},{3,1},{5,3},{7,5},{8,14},{10,8},{12,... | collective-permute-start | bytes 589832 | tf_op jit(solution)/shard_map/ppermute | solution.py:18
  38.4 6.3 %collective-permute-start.9 = (bf16[4,3,16,512]{3,2,1,0:T(8,128)(2,1)S(1)}, bf16[4,3,16,512]{3,2,1,0:T(8,128)(2,1)S(1)}, u32[]{:S(2)}, u32[]{:S(2)}) collective-permute-start(bf16[4,3,16,512]{3,2,1,0:T(8,128)(2,1)S(1)} %get-tuple-element.18), channel_id=1, source_target_pairs={{0,2},{2,4},{4,6},{6,0},{1,3},{3,5},{5,7},{7,1},{8,10},{10,12},{12... | collective-permute-start | bytes 589832 | tf_op jit(solution)/shard_map/ppermute | solution.py:18
  44.7 1.6 %collective-permute-start.11 = (bf16[4,3,16,512]{3,2,1,0:T(8,128)(2,1)S(1)}, bf16[4,3,16,512]{3,2,1,0:T(8,128)(2,1)S(1)}, u32[]{:S(2)}, u32[]{:S(2)}) collective-permute-start(bf16[4,3,16,512]{3,2,1,0:T(8,128)(2,1)S(1)} %collective-permute-done.10), channel_id=1, source_target_pairs={{0,6},{2,0},{4,2},{6,4},{1,7},{3,1},{5,3},{7,5},{8,14},{10,8},{12,... | collective-permute-start | bytes 589832 | tf_op jit(solution)/shard_map/ppermute | solution.py:18
  46.3 6.8 %collective-permute-done.27 = bf16[4,3,16,512]{3,2,1,0:T(8,128)(2,1)S(1)} collective-permute-done((bf16[4,3,16,512]{3,2,1,0:T(8,128)(2,1)S(1)}, bf16[4,3,16,512]{3,2,1,0:T(8,128)(2,1)S(1)}, u32[]{:S(2)}, u32[]{:S(2)}) %collective-permute-start.27) | collective-permute-done | bytes 196640 | tf_op jit(solution)/shard_map/ppermute | solution.py:18
  53.1 2.4 %collective-permute-start.20 = (bf16[3,256,512]{2,1,0:T(8,128)(2,1)}, bf16[3,256,512]{2,1,0:T(8,128)(2,1)S(1)}, u32[]{:S(2)}, u32[]{:S(2)}) collective-permute-start(bf16[3,256,512]{2,1,0:T(8,128)(2,1)} %refs_1_.1), channel_id=1, source_target_pairs={{0,96},{32,0},{64,32},{96,64},{1,97},{33,1},{65,33},{97,65},{2,98}... | collective-permute-start | bytes 2359304 | tf_op jit(solution)/shard_map/ppermute | solution.py:18
  55.6 1.5 %collective-permute-start.29 = (bf16[4,4,3,16,512]{4,3,2,1,0:T(8,128)(2,1)S(1)}, bf16[4,4,3,16,512]{4,3,2,1,0:T(8,128)(2,1)S(1)}, u32[]{:S(2)}, u32[]{:S(2)}) collective-permute-start(bf16[4,4,3,16,512]{4,3,2,1,0:T(8,128)(2,1)S(1)} %pad_maximum_fusion.1.refs_5_), channel_id=1, source_target_pairs={{0,8},{8,16},{16,24},{24,0},{1,9},{9,17},{17,25},{25,1},{2,10},{10... | collective-permute-start | bytes 2359304 | tf_op jit(solution)/shard_map/ppermute | solution.py:18
  57.1 2.0 %collective-permute-done.11 = bf16[4,3,16,512]{3,2,1,0:T(8,128)(2,1)S(1)} collective-permute-done((bf16[4,3,16,512]{3,2,1,0:T(8,128)(2,1)S(1)}, bf16[4,3,16,512]{3,2,1,0:T(8,128)(2,1)S(1)}, u32[]{:S(2)}, u32[]{:S(2)}) %collective-permute-start.11) | collective-permute-done | bytes 196640 | tf_op jit(solution)/shard_map/ppermute | solution.py:18
  59.1 2.9 %collective-permute-start.30 = (bf16[4,4,3,16,512]{4,3,2,1,0:T(8,128)(2,1)S(1)}, bf16[4,4,3,16,512]{4,3,2,1,0:T(8,128)(2,1)S(1)}, u32[]{:S(2)}, u32[]{:S(2)}) collective-permute-start(bf16[4,4,3,16,512]{4,3,2,1,0:T(8,128)(2,1)S(1)} %pad_maximum_fusion.1.refs_5_), channel_id=1, source_target_pairs={{0,24},{8,0},{16,8},{24,16},{1,25},{9,1},{17,9},{25,17},{2,26},{10... | collective-permute-start | bytes 2359304 | tf_op jit(solution)/shard_map/ppermute | solution.py:18
  62.0 1.8 %collective-permute-start.32 = (bf16[4,4,3,16,512]{4,3,2,1,0:T(8,128)(2,1)S(1)}, bf16[4,4,3,16,512]{4,3,2,1,0:T(8,128)(2,1)S(1)}, u32[]{:S(2)}, u32[]{:S(2)}) collective-permute-start(bf16[4,4,3,16,512]{4,3,2,1,0:T(8,128)(2,1)S(1)} %pad_maximum_fusion.1.refs_5_), channel_id=1, source_target_pairs={{0,1},{1,0},{2,3},{3,2},{4,5},{5,4},{6,7},{7,6},{8,9},{9,8},{10,11... | collective-permute-start | bytes 2359304 | tf_op jit(solution)/shard_map/ppermute | solution.py:18
  63.9 4.7 %collective-permute-done.20.refs_3_ = bf16[3,256,512]{2,1,0:T(8,128)(2,1)S(1)} collective-permute-done((bf16[3,256,512]{2,1,0:T(8,128)(2,1)}, bf16[3,256,512]{2,1,0:T(8,128)(2,1)S(1)}, u32[]{:S(2)}, u32[]{:S(2)}) %collective-permute-start.20) | collective-permute-done | bytes 786464 | tf_op jit(solution)/shard_map/ppermute | solution.py:18
  68.6 2.9 %collective-permute-start.13 = (bf16[4,4,3,16,512]{4,3,2,1,0:T(8,128)(2,1)S(1)}, bf16[4,4,3,16,512]{4,3,2,1,0:T(8,128)(2,1)S(1)}, u32[]{:S(2)}, u32[]{:S(2)}) collective-permute-start(bf16[4,4,3,16,512]{4,3,2,1,0:T(8,128)(2,1)S(1)} %pad_maximum_fusion.refs_5_), channel_id=1, source_target_pairs={{0,24},{8,0},{16,8},{24,16},{1,25},{9,1},{17,9},{25,17},{2,26},{10... | collective-permute-start | bytes 2359304 | tf_op jit(solution)/shard_map/ppermute | solution.py:18
  71.6 5.9 %collective-permute-done.refs_1_ = bf16[3,256,512]{2,1,0:T(8,128)(2,1)S(1)} collective-permute-done((bf16[3,256,512]{2,1,0:T(8,128)(2,1)}, bf16[3,256,512]{2,1,0:T(8,128)(2,1)S(1)}, u32[]{:S(2)}, u32[]{:S(2)}) %collective-permute-start) | collective-permute-done | bytes 786464 | tf_op jit(solution)/shard_map/ppermute | solution.py:18
  78.7 2.4 %collective-permute-start.15 = (bf16[4,4,3,16,512]{4,3,2,1,0:T(8,128)(2,1)S(1)}, bf16[4,4,3,16,512]{4,3,2,1,0:T(8,128)(2,1)S(1)}, u32[]{:S(2)}, u32[]{:S(2)}) collective-permute-start(bf16[4,4,3,16,512]{4,3,2,1,0:T(8,128)(2,1)S(1)} %pad_maximum_fusion.refs_5_), channel_id=1, source_target_pairs={{0,1},{1,0},{2,3},{3,2},{4,5},{5,4},{6,7},{7,6},{8,9},{9,8},{10,11... | collective-permute-start | bytes 2359304 | tf_op jit(solution)/shard_map/ppermute | solution.py:18
  81.5 1.3 collective-permute-start.31
  82.8 11.4 %collective-permute-done.13.refs_7_ = bf16[4,4,3,16,512]{4,3,2,1,0:T(8,128)(2,1)S(1)} collective-permute-done((bf16[4,4,3,16,512]{4,3,2,1,0:T(8,128)(2,1)S(1)}, bf16[4,4,3,16,512]{4,3,2,1,0:T(8,128)(2,1)S(1)}, u32[]{:S(2)}, u32[]{:S(2)}) %collective-permute-start.13) | collective-permute-done | bytes 786464 | tf_op jit(solution)/shard_map/ppermute | solution.py:18
  94.2 2.6 %collective-permute-start.2 = (bf16[3,256,512]{2,1,0:T(8,128)(2,1)S(1)}, bf16[3,256,512]{2,1,0:T(8,128)(2,1)}, u32[]{:S(2)}, u32[]{:S(2)}) collective-permute-start(bf16[3,256,512]{2,1,0:T(8,128)(2,1)S(1)} %collective-permute-done.refs_1_), channel_id=1, source_target_pairs={{0,96},{32,0},{64,32},{96,64},{1,97},{33,1},{65,33},{97,65},{2,98}... | collective-permute-start | bytes 2359304 | tf_op jit(solution)/shard_map/ppermute | solution.py:18
  96.8 4.6 %collective-permute-start.33 = (bf16[4,4,3,16,512]{4,3,2,1,0:T(8,128)(2,1)S(1)}, bf16[4,4,3,16,512]{4,3,2,1,0:T(8,128)(2,1)S(1)}, u32[]{:S(2)}, u32[]{:S(2)}) collective-permute-start(bf16[4,4,3,16,512]{4,3,2,1,0:T(8,128)(2,1)S(1)} %collective-permute-done.29.refs_6_), channel_id=1, source_target_pairs={{0,1},{1,0},{2,3},{3,2},{4,5},{5,4},{6,7},{7,6},{8,9},{9,8},{10,11... | collective-permute-start | bytes 2359304 | tf_op jit(solution)/shard_map/ppermute | solution.py:18
  101.5 1.5 %collective-permute-start.14 = (bf16[4,4,3,16,512]{4,3,2,1,0:T(8,128)(2,1)S(1)}, bf16[4,4,3,16,512]{4,3,2,1,0:T(8,128)(2,1)}, u32[]{:S(2)}, u32[]{:S(2)}) collective-permute-start(bf16[4,4,3,16,512]{4,3,2,1,0:T(8,128)(2,1)S(1)} %collective-permute-done.13.refs_7_), channel_id=1, source_target_pairs={{0,24},{8,0},{16,8},{24,16},{1,25},{9,1},{17,9},{25,17},{2,26},{10... | collective-permute-start | bytes 2359304 | tf_op jit(solution)/shard_map/ppermute | solution.py:18
  103.0 9.5 %collective-permute-done.31.refs_8_ = bf16[4,4,3,16,512]{4,3,2,1,0:T(8,128)(2,1)S(1)} collective-permute-done((bf16[4,4,3,16,512]{4,3,2,1,0:T(8,128)(2,1)S(1)}, bf16[4,4,3,16,512]{4,3,2,1,0:T(8,128)(2,1)S(1)}, u32[]{:S(2)}, u32[]{:S(2)}) %collective-permute-start.31) | collective-permute-done | bytes 786464 | tf_op jit(solution)/shard_map/ppermute | solution.py:18
  112.5 3.0 %collective-permute-start.35 = (bf16[4,4,3,16,512]{4,3,2,1,0:T(8,128)(2,1)S(1)}, bf16[4,4,3,16,512]{4,3,2,1,0:T(8,128)(2,1)S(1)}, u32[]{:S(2)}, u32[]{:S(2)}) collective-permute-start(bf16[4,4,3,16,512]{4,3,2,1,0:T(8,128)(2,1)S(1)} %collective-permute-done.31.refs_8_), channel_id=1, source_target_pairs={{0,1},{1,0},{2,3},{3,2},{4,5},{5,4},{6,7},{7,6},{8,9},{9,8},{10,11... | collective-permute-start | bytes 2359304 | tf_op jit(solution)/shard_map/ppermute | solution.py:18
  116.9 2.7 %collective-permute-done.14.refs_8_ = bf16[4,4,3,16,512]{4,3,2,1,0:T(8,128)(2,1)} collective-permute-done((bf16[4,4,3,16,512]{4,3,2,1,0:T(8,128)(2,1)S(1)}, bf16[4,4,3,16,512]{4,3,2,1,0:T(8,128)(2,1)}, u32[]{:S(2)}, u32[]{:S(2)}) %collective-permute-start.14) | collective-permute-done | bytes 786464 | tf_op jit(solution)/shard_map/ppermute | solution.py:18
  119.6 1.6 %collective-permute-start.3 = (bf16[3,256,512]{2,1,0:T(8,128)(2,1)}, bf16[3,256,512]{2,1,0:T(8,128)(2,1)}, u32[]{:S(2)}, u32[]{:S(2)}) collective-permute-start(bf16[3,256,512]{2,1,0:T(8,128)(2,1)} %collective-permute-done.2.refs_3_), channel_id=1, source_target_pairs={{0,96},{32,0},{64,32},{96,64},{1,97},{33,1},{65,33},{97,65},{2,98}... | collective-permute-start | bytes 2359304 | tf_op jit(solution)/shard_map/ppermute | solution.py:18
  122.2 1.5 %collective-permute-start.18 = (bf16[4,4,3,16,512]{4,3,2,1,0:T(8,128)(2,1)}, bf16[4,4,3,16,512]{4,3,2,1,0:T(8,128)(2,1)}, u32[]{:S(2)}, u32[]{:S(2)}) collective-permute-start(bf16[4,4,3,16,512]{4,3,2,1,0:T(8,128)(2,1)} %collective-permute-done.14.refs_8_), channel_id=1, source_target_pairs={{0,1},{1,0},{2,3},{3,2},{4,5},{5,4},{6,7},{7,6},{8,9},{9,8},{10,11... | collective-permute-start | bytes 2359304 | tf_op jit(solution)/shard_map/ppermute | solution.py:18
  124.4 9.0 %shard_map.28.refs_13_ = f32[1024,512]{1,0:T(8,128)} custom-call(s32[17]{0:T(128)} %stack.127.refs_0_, bf16[3,256,512]{2,1,0:T(8,128)(2,1)} %refs_1_.1, bf16[3,256,512]{2,1,0:T(8,128)(2,1)} %collective-permute-done.19.refs_2_, bf16[3,256,512]{2,1,0:T(8,128)(2,1)} %copy-done.5, bf16[3,256,512]{2,1,0:T(8,128)(2,1)} %copy-done.9, ...), custom_call_target="tpu_custom_call" | custom-call | flops 3221225472 | bytes 16777216 | tf_op jit(solution)/shard_map/pallas_call | solution.py:77
  133.4 2.6 %collective-permute-done.1.refs_2_ = bf16[3,256,512]{2,1,0:T(8,128)(2,1)} collective-permute-done((bf16[3,256,512]{2,1,0:T(8,128)(2,1)S(1)}, bf16[3,256,512]{2,1,0:T(8,128)(2,1)}, u32[]{:S(2)}, u32[]{:S(2)}) %collective-permute-start.1) | collective-permute-done | bytes 786464 | tf_op jit(solution)/shard_map/ppermute | solution.py:18
  137.2 9.8 %shard_map.29 = f32[1024,512]{1,0:T(8,128)} custom-call(s32[17]{0:T(128)} %stack.127.refs_0_, bf16[3,256,512]{2,1,0:T(8,128)(2,1)} %copy-done.2, bf16[3,256,512]{2,1,0:T(8,128)(2,1)} %collective-permute-done.1.refs_2_, bf16[3,256,512]{2,1,0:T(8,128)(2,1)} %collective-permute-done.2.refs_3_, bf16[3,256,512]{2,1,0:T(8,128)(2,1)} %collective-permute-done.3.refs_4_, ...), custom_call_target="tpu_custom_call" | custom-call | flops 3221225472 | bytes 16777216 | tf_op jit(solution)/shard_map/pallas_call | solution.py:77
  (83 shorter events, 16.1 us)
Async XLA Ops:
  4.3 57.7 %collective-permute-start.19 = (bf16[3,256,512]{2,1,0:T(8,128)(2,1)}, bf16[3,256,512]{2,1,0:T(8,128)(2,1)}, u32[]{:S(2)}, u32[]{:S(2)}) collective-permute-start(bf16[3,256,512]{2,1,0:T(8,128)(2,1)} %refs_1_.1), channel_id=1, source_target_pairs={{0,32},{32,64},{64,96},{96,0},{1,33},{33,65},{65,97},{97,1},{2,34}... | collective-permute-start | bytes 2359304 | tf_op jit(solution)/shard_map/ppermute | solution.py:18
  5.3 6.6 %collective-permute-start.4 = (bf16[3,8,4,2,512]{4,1,0,2,3:T(8,128)(2,1)S(1)}, bf16[3,8,4,2,512]{4,1,0,2,3:T(8,128)(2,1)S(1)}, u32[]{:S(2)}, u32[]{:S(2)}) collective-permute-start(bf16[3,8,4,2,512]{4,1,0,2,3:T(8,128)(2,1)S(1)} %copy_bitcast_fusion), channel_id=1, source_target_pairs={{0,128},{128,0},{1,129},{129,1},{2,130},{130,2},{3,131},{131,3},{4... | collective-permute-start | bytes 589832 | tf_op jit(solution)/shard_map/ppermute | solution.py:18
  12.8 14.0 %collective-permute-start.23 = (bf16[3,16,512]{2,1,0:T(8,128)(2,1)S(1)}, bf16[3,16,512]{2,1,0:T(8,128)(2,1)S(1)}, u32[]{:S(2)}, u32[]{:S(2)}) collective-permute-start(bf16[3,16,512]{2,1,0:T(8,128)(2,1)S(1)} %get-tuple-element.12), channel_id=1, source_target_pairs={{0,32},{32,64},{64,96},{96,0},{1,33},{33,65},{65,97},{97,1},{2,34}... | collective-permute-start | bytes 147464 | tf_op jit(solution)/shard_map/ppermute | solution.py:18
  13.7 13.0 %collective-permute-start.24 = (bf16[3,16,512]{2,1,0:T(8,128)(2,1)S(1)}, bf16[3,16,512]{2,1,0:T(8,128)(2,1)S(1)}, u32[]{:S(2)}, u32[]{:S(2)}) collective-permute-start(bf16[3,16,512]{2,1,0:T(8,128)(2,1)S(1)} %get-tuple-element.13), channel_id=1, source_target_pairs={{0,96},{32,0},{64,32},{96,64},{1,97},{33,1},{65,33},{97,65},{2,98}... | collective-permute-start | bytes 147464 | tf_op jit(solution)/shard_map/ppermute | solution.py:18
  15.6 11.1 %collective-permute-start.25 = (bf16[3,16,512]{2,1,0:T(8,128)(2,1)S(1)}, bf16[3,16,512]{2,1,0:T(8,128)(2,1)S(1)}, u32[]{:S(2)}, u32[]{:S(2)}) collective-permute-start(bf16[3,16,512]{2,1,0:T(8,128)(2,1)S(1)} %get-tuple-element.14), channel_id=1, source_target_pairs={{0,64},{32,96},{64,0},{96,32},{1,65},{33,97},{65,1},{97,33},{2,66}... | collective-permute-start | bytes 147464 | tf_op jit(solution)/shard_map/ppermute | solution.py:18
  16.8 12.5 %collective-permute-start.6 = (bf16[3,16,512]{2,1,0:T(8,128)(2,1)S(1)}, bf16[3,16,512]{2,1,0:T(8,128)(2,1)S(1)}, u32[]{:S(2)}, u32[]{:S(2)}) collective-permute-start(bf16[3,16,512]{2,1,0:T(8,128)(2,1)S(1)} %get-tuple-element.20), channel_id=1, source_target_pairs={{0,32},{32,64},{64,96},{96,0},{1,33},{33,65},{65,97},{97,1},{2,34}... | collective-permute-start | bytes 147464 | tf_op jit(solution)/shard_map/ppermute | solution.py:18
  26.8 10.4 %collective-permute-start.26 = (bf16[4,3,16,512]{3,2,1,0:T(8,128)(2,1)S(1)}, bf16[4,3,16,512]{3,2,1,0:T(8,128)(2,1)S(1)}, u32[]{:S(2)}, u32[]{:S(2)}) collective-permute-start(bf16[4,3,16,512]{3,2,1,0:T(8,128)(2,1)S(1)} %get-tuple-element.10), channel_id=1, source_target_pairs={{0,2},{2,4},{4,6},{6,0},{1,3},{3,5},{5,7},{7,1},{8,10},{10,12},{12... | collective-permute-start | bytes 589832 | tf_op jit(solution)/shard_map/ppermute | solution.py:18
  31.2 13.5 %collective-permute-start.10 = (bf16[4,3,16,512]{3,2,1,0:T(8,128)(2,1)S(1)}, bf16[4,3,16,512]{3,2,1,0:T(8,128)(2,1)S(1)}, u32[]{:S(2)}, u32[]{:S(2)}) collective-permute-start(bf16[4,3,16,512]{3,2,1,0:T(8,128)(2,1)S(1)} %get-tuple-element.18), channel_id=1, source_target_pairs={{0,6},{2,0},{4,2},{6,4},{1,7},{3,1},{5,3},{7,5},{8,14},{10,8},{12,... | collective-permute-start | bytes 589832 | tf_op jit(solution)/shard_map/ppermute | solution.py:18
  36.0 17.1 %collective-permute-start.27 = (bf16[4,3,16,512]{3,2,1,0:T(8,128)(2,1)S(1)}, bf16[4,3,16,512]{3,2,1,0:T(8,128)(2,1)S(1)}, u32[]{:S(2)}, u32[]{:S(2)}) collective-permute-start(bf16[4,3,16,512]{3,2,1,0:T(8,128)(2,1)S(1)} %get-tuple-element.10), channel_id=1, source_target_pairs={{0,6},{2,0},{4,2},{6,4},{1,7},{3,1},{5,3},{7,5},{8,14},{10,8},{12,... | collective-permute-start | bytes 589832 | tf_op jit(solution)/shard_map/ppermute | solution.py:18
  37.2 18.3 %collective-permute-start.28 = (bf16[4,3,16,512]{3,2,1,0:T(8,128)(2,1)S(1)}, bf16[4,3,16,512]{3,2,1,0:T(8,128)(2,1)S(1)}, u32[]{:S(2)}, u32[]{:S(2)}) collective-permute-start(bf16[4,3,16,512]{3,2,1,0:T(8,128)(2,1)S(1)} %collective-permute-done.26), channel_id=1, source_target_pairs={{0,2},{2,4},{4,6},{6,0},{1,3},{3,5},{5,7},{7,1},{8,10},{10,12},{12... | collective-permute-start | bytes 589832 | tf_op jit(solution)/shard_map/ppermute | solution.py:18
  38.4 17.3 %collective-permute-start.9 = (bf16[4,3,16,512]{3,2,1,0:T(8,128)(2,1)S(1)}, bf16[4,3,16,512]{3,2,1,0:T(8,128)(2,1)S(1)}, u32[]{:S(2)}, u32[]{:S(2)}) collective-permute-start(bf16[4,3,16,512]{3,2,1,0:T(8,128)(2,1)S(1)} %get-tuple-element.18), channel_id=1, source_target_pairs={{0,2},{2,4},{4,6},{6,0},{1,3},{3,5},{5,7},{7,1},{8,10},{10,12},{12... | collective-permute-start | bytes 589832 | tf_op jit(solution)/shard_map/ppermute | solution.py:18
  44.7 14.4 %collective-permute-start.11 = (bf16[4,3,16,512]{3,2,1,0:T(8,128)(2,1)S(1)}, bf16[4,3,16,512]{3,2,1,0:T(8,128)(2,1)S(1)}, u32[]{:S(2)}, u32[]{:S(2)}) collective-permute-start(bf16[4,3,16,512]{3,2,1,0:T(8,128)(2,1)S(1)} %collective-permute-done.10), channel_id=1, source_target_pairs={{0,6},{2,0},{4,2},{6,4},{1,7},{3,1},{5,3},{7,5},{8,14},{10,8},{12,... | collective-permute-start | bytes 589832 | tf_op jit(solution)/shard_map/ppermute | solution.py:18
  53.1 15.5 %collective-permute-start.20 = (bf16[3,256,512]{2,1,0:T(8,128)(2,1)}, bf16[3,256,512]{2,1,0:T(8,128)(2,1)S(1)}, u32[]{:S(2)}, u32[]{:S(2)}) collective-permute-start(bf16[3,256,512]{2,1,0:T(8,128)(2,1)} %refs_1_.1), channel_id=1, source_target_pairs={{0,96},{32,0},{64,32},{96,64},{1,97},{33,1},{65,33},{97,65},{2,98}... | collective-permute-start | bytes 2359304 | tf_op jit(solution)/shard_map/ppermute | solution.py:18
  55.5 22.0 %collective-permute-start = (bf16[3,256,512]{2,1,0:T(8,128)(2,1)}, bf16[3,256,512]{2,1,0:T(8,128)(2,1)S(1)}, u32[]{:S(2)}, u32[]{:S(2)}) collective-permute-start(bf16[3,256,512]{2,1,0:T(8,128)(2,1)} %refs_1_.1), channel_id=1, source_target_pairs={{0,128},{128,0},{1,129},{129,1},{2,130},{130,2},{3,131},{131,3},{4... | collective-permute-start | bytes 2359304 | tf_op jit(solution)/shard_map/ppermute | solution.py:18
  55.6 23.1 %collective-permute-start.29 = (bf16[4,4,3,16,512]{4,3,2,1,0:T(8,128)(2,1)S(1)}, bf16[4,4,3,16,512]{4,3,2,1,0:T(8,128)(2,1)S(1)}, u32[]{:S(2)}, u32[]{:S(2)}) collective-permute-start(bf16[4,4,3,16,512]{4,3,2,1,0:T(8,128)(2,1)S(1)} %pad_maximum_fusion.1.refs_5_), channel_id=1, source_target_pairs={{0,8},{8,16},{16,24},{24,0},{1,9},{9,17},{17,25},{25,1},{2,10},{10... | collective-permute-start | bytes 2359304 | tf_op jit(solution)/shard_map/ppermute | solution.py:18
  59.1 22.1 %collective-permute-start.30 = (bf16[4,4,3,16,512]{4,3,2,1,0:T(8,128)(2,1)S(1)}, bf16[4,4,3,16,512]{4,3,2,1,0:T(8,128)(2,1)S(1)}, u32[]{:S(2)}, u32[]{:S(2)}) collective-permute-start(bf16[4,4,3,16,512]{4,3,2,1,0:T(8,128)(2,1)S(1)} %pad_maximum_fusion.1.refs_5_), channel_id=1, source_target_pairs={{0,24},{8,0},{16,8},{24,16},{1,25},{9,1},{17,9},{25,17},{2,26},{10... | collective-permute-start | bytes 2359304 | tf_op jit(solution)/shard_map/ppermute | solution.py:18
  62.0 19.5 %collective-permute-start.32 = (bf16[4,4,3,16,512]{4,3,2,1,0:T(8,128)(2,1)S(1)}, bf16[4,4,3,16,512]{4,3,2,1,0:T(8,128)(2,1)S(1)}, u32[]{:S(2)}, u32[]{:S(2)}) collective-permute-start(bf16[4,4,3,16,512]{4,3,2,1,0:T(8,128)(2,1)S(1)} %pad_maximum_fusion.1.refs_5_), channel_id=1, source_target_pairs={{0,1},{1,0},{2,3},{3,2},{4,5},{5,4},{6,7},{7,6},{8,9},{9,8},{10,11... | collective-permute-start | bytes 2359304 | tf_op jit(solution)/shard_map/ppermute | solution.py:18
  68.6 25.6 %collective-permute-start.13 = (bf16[4,4,3,16,512]{4,3,2,1,0:T(8,128)(2,1)S(1)}, bf16[4,4,3,16,512]{4,3,2,1,0:T(8,128)(2,1)S(1)}, u32[]{:S(2)}, u32[]{:S(2)}) collective-permute-start(bf16[4,4,3,16,512]{4,3,2,1,0:T(8,128)(2,1)S(1)} %pad_maximum_fusion.refs_5_), channel_id=1, source_target_pairs={{0,24},{8,0},{16,8},{24,16},{1,25},{9,1},{17,9},{25,17},{2,26},{10... | collective-permute-start | bytes 2359304 | tf_op jit(solution)/shard_map/ppermute | solution.py:18
  77.5 19.3 %collective-permute-start.12 = (bf16[4,4,3,16,512]{4,3,2,1,0:T(8,128)(2,1)S(1)}, bf16[4,4,3,16,512]{4,3,2,1,0:T(8,128)(2,1)}, u32[]{:S(2)}, u32[]{:S(2)}) collective-permute-start(bf16[4,4,3,16,512]{4,3,2,1,0:T(8,128)(2,1)S(1)} %pad_maximum_fusion.refs_5_), channel_id=1, source_target_pairs={{0,8},{8,16},{16,24},{24,0},{1,9},{9,17},{17,25},{25,1},{2,10},{10... | collective-permute-start | bytes 2359304 | tf_op jit(solution)/shard_map/ppermute | solution.py:18
  78.7 22.7 %collective-permute-start.15 = (bf16[4,4,3,16,512]{4,3,2,1,0:T(8,128)(2,1)S(1)}, bf16[4,4,3,16,512]{4,3,2,1,0:T(8,128)(2,1)S(1)}, u32[]{:S(2)}, u32[]{:S(2)}) collective-permute-start(bf16[4,4,3,16,512]{4,3,2,1,0:T(8,128)(2,1)S(1)} %pad_maximum_fusion.refs_5_), channel_id=1, source_target_pairs={{0,1},{1,0},{2,3},{3,2},{4,5},{5,4},{6,7},{7,6},{8,9},{9,8},{10,11... | collective-permute-start | bytes 2359304 | tf_op jit(solution)/shard_map/ppermute | solution.py:18
  81.2 20.3 %collective-permute-start.21 = (bf16[3,256,512]{2,1,0:T(8,128)(2,1)}, bf16[3,256,512]{2,1,0:T(8,128)(2,1)S(1)}, u32[]{:S(2)}, u32[]{:S(2)}) collective-permute-start(bf16[3,256,512]{2,1,0:T(8,128)(2,1)} %collective-permute-done.19.refs_2_), channel_id=1, source_target_pairs={{0,32},{32,64},{64,96},{96,0},{1,33},{33,65},{65,97},{97,1},{2,34}... | collective-permute-start | bytes 2359304 | tf_op jit(solution)/shard_map/ppermute | solution.py:18
  81.5 31.0 %collective-permute-start.31 = (bf16[4,4,3,16,512]{4,3,2,1,0:T(8,128)(2,1)S(1)}, bf16[4,4,3,16,512]{4,3,2,1,0:T(8,128)(2,1)S(1)}, u32[]{:S(2)}, u32[]{:S(2)}) collective-permute-start(bf16[4,4,3,16,512]{4,3,2,1,0:T(8,128)(2,1)S(1)} %collective-permute-done.29.refs_6_), channel_id=1, source_target_pairs={{0,8},{8,16},{16,24},{24,0},{1,9},{9,17},{17,25},{25,1},{2,10},{10... | collective-permute-start | bytes 2359304 | tf_op jit(solution)/shard_map/ppermute | solution.py:18
  94.2 21.3 %collective-permute-start.2 = (bf16[3,256,512]{2,1,0:T(8,128)(2,1)S(1)}, bf16[3,256,512]{2,1,0:T(8,128)(2,1)}, u32[]{:S(2)}, u32[]{:S(2)}) collective-permute-start(bf16[3,256,512]{2,1,0:T(8,128)(2,1)S(1)} %collective-permute-done.refs_1_), channel_id=1, source_target_pairs={{0,96},{32,0},{64,32},{96,64},{1,97},{33,1},{65,33},{97,65},{2,98}... | collective-permute-start | bytes 2359304 | tf_op jit(solution)/shard_map/ppermute | solution.py:18
  96.8 19.6 %collective-permute-start.33 = (bf16[4,4,3,16,512]{4,3,2,1,0:T(8,128)(2,1)S(1)}, bf16[4,4,3,16,512]{4,3,2,1,0:T(8,128)(2,1)S(1)}, u32[]{:S(2)}, u32[]{:S(2)}) collective-permute-start(bf16[4,4,3,16,512]{4,3,2,1,0:T(8,128)(2,1)S(1)} %collective-permute-done.29.refs_6_), channel_id=1, source_target_pairs={{0,1},{1,0},{2,3},{3,2},{4,5},{5,4},{6,7},{7,6},{8,9},{9,8},{10,11... | collective-permute-start | bytes 2359304 | tf_op jit(solution)/shard_map/ppermute | solution.py:18
  101.4 15.3 %collective-permute-start.34 = (bf16[4,4,3,16,512]{4,3,2,1,0:T(8,128)(2,1)S(1)}, bf16[4,4,3,16,512]{4,3,2,1,0:T(8,128)(2,1)S(1)}, u32[]{:S(2)}, u32[]{:S(2)}) collective-permute-start(bf16[4,4,3,16,512]{4,3,2,1,0:T(8,128)(2,1)S(1)} %collective-permute-done.30.refs_7_), channel_id=1, source_target_pairs={{0,1},{1,0},{2,3},{3,2},{4,5},{5,4},{6,7},{7,6},{8,9},{9,8},{10,11... | collective-permute-start | bytes 2359304 | tf_op jit(solution)/shard_map/ppermute | solution.py:18
  101.5 18.1 %collective-permute-start.14 = (bf16[4,4,3,16,512]{4,3,2,1,0:T(8,128)(2,1)S(1)}, bf16[4,4,3,16,512]{4,3,2,1,0:T(8,128)(2,1)}, u32[]{:S(2)}, u32[]{:S(2)}) collective-permute-start(bf16[4,4,3,16,512]{4,3,2,1,0:T(8,128)(2,1)S(1)} %collective-permute-done.13.refs_7_), channel_id=1, source_target_pairs={{0,24},{8,0},{16,8},{24,16},{1,25},{9,1},{17,9},{25,17},{2,26},{10... | collective-permute-start | bytes 2359304 | tf_op jit(solution)/shard_map/ppermute | solution.py:18
  112.5 8.7 %collective-permute-start.35 = (bf16[4,4,3,16,512]{4,3,2,1,0:T(8,128)(2,1)S(1)}, bf16[4,4,3,16,512]{4,3,2,1,0:T(8,128)(2,1)S(1)}, u32[]{:S(2)}, u32[]{:S(2)}) collective-permute-start(bf16[4,4,3,16,512]{4,3,2,1,0:T(8,128)(2,1)S(1)} %collective-permute-done.31.refs_8_), channel_id=1, source_target_pairs={{0,1},{1,0},{2,3},{3,2},{4,5},{5,4},{6,7},{7,6},{8,9},{9,8},{10,11... | collective-permute-start | bytes 2359304 | tf_op jit(solution)/shard_map/ppermute | solution.py:18
  115.5 20.4 %collective-permute-start.1 = (bf16[3,256,512]{2,1,0:T(8,128)(2,1)S(1)}, bf16[3,256,512]{2,1,0:T(8,128)(2,1)}, u32[]{:S(2)}, u32[]{:S(2)}) collective-permute-start(bf16[3,256,512]{2,1,0:T(8,128)(2,1)S(1)} %collective-permute-done.refs_1_), channel_id=1, source_target_pairs={{0,32},{32,64},{64,96},{96,0},{1,33},{33,65},{65,97},{97,1},{2,34}... | collective-permute-start | bytes 2359304 | tf_op jit(solution)/shard_map/ppermute | solution.py:18
  116.4 19.6 %collective-permute-start.17 = (bf16[4,4,3,16,512]{4,3,2,1,0:T(8,128)(2,1)S(1)}, bf16[4,4,3,16,512]{4,3,2,1,0:T(8,128)(2,1)}, u32[]{:S(2)}, u32[]{:S(2)}) collective-permute-start(bf16[4,4,3,16,512]{4,3,2,1,0:T(8,128)(2,1)S(1)} %collective-permute-done.13.refs_7_), channel_id=1, source_target_pairs={{0,1},{1,0},{2,3},{3,2},{4,5},{5,4},{6,7},{7,6},{8,9},{9,8},{10,11... | collective-permute-start | bytes 2359304 | tf_op jit(solution)/shard_map/ppermute | solution.py:18
  116.7 19.2 %collective-permute-start.16 = (bf16[4,4,3,16,512]{4,3,2,1,0:T(8,128)(2,1)}, bf16[4,4,3,16,512]{4,3,2,1,0:T(8,128)(2,1)}, u32[]{:S(2)}, u32[]{:S(2)}) collective-permute-start(bf16[4,4,3,16,512]{4,3,2,1,0:T(8,128)(2,1)} %collective-permute-done.12.refs_6_), channel_id=1, source_target_pairs={{0,1},{1,0},{2,3},{3,2},{4,5},{5,4},{6,7},{7,6},{8,9},{9,8},{10,11... | collective-permute-start | bytes 2359304 | tf_op jit(solution)/shard_map/ppermute | solution.py:18
  119.6 17.6 %collective-permute-start.3 = (bf16[3,256,512]{2,1,0:T(8,128)(2,1)}, bf16[3,256,512]{2,1,0:T(8,128)(2,1)}, u32[]{:S(2)}, u32[]{:S(2)}) collective-permute-start(bf16[3,256,512]{2,1,0:T(8,128)(2,1)} %collective-permute-done.2.refs_3_), channel_id=1, source_target_pairs={{0,96},{32,0},{64,32},{96,64},{1,97},{33,1},{65,33},{97,65},{2,98}... | collective-permute-start | bytes 2359304 | tf_op jit(solution)/shard_map/ppermute | solution.py:18
  122.2 15.0 %collective-permute-start.18 = (bf16[4,4,3,16,512]{4,3,2,1,0:T(8,128)(2,1)}, bf16[4,4,3,16,512]{4,3,2,1,0:T(8,128)(2,1)}, u32[]{:S(2)}, u32[]{:S(2)}) collective-permute-start(bf16[4,4,3,16,512]{4,3,2,1,0:T(8,128)(2,1)} %collective-permute-done.14.refs_8_), channel_id=1, source_target_pairs={{0,1},{1,0},{2,3},{3,2},{4,5},{5,4},{6,7},{7,6},{8,9},{9,8},{10,11... | collective-permute-start | bytes 2359304 | tf_op jit(solution)/shard_map/ppermute | solution.py:18
  (18 other events, 483.2 us)

commit v2 on v0

v2 whole, which is shorter than its diff:
```python
import functools

import jax
import jax.numpy as jnp
from jax import lax
from jax.experimental import pallas as pl
from jax.experimental.pallas import tpu as pltpu
from jax.sharding import Mesh, PartitionSpec as P

AXES = ("zlo", "x", "y", "zhi", "core")
SIZES = (2, 4, 4, 4, 2)
SEQS_DP = 3
ROWS = 16
LANES = 256
SCALE = 14
SWAP = (0, 2, 1, 3)
VMEM = pl.BlockSpec(memory_space=pltpu.VMEM)


def swap(value, axis):
    return lax.ppermute(value, axis, [(0, 1), (1, 0)])


def send(value, axis, by):
    pairs = [
        (2 * i + c, 2 * ((i + (by if c == 0 else -by)) % 4) + c)
        for i in range(4)
        for c in range(2)
    ]
    return lax.ppermute(value, (axis, "core"), pairs)


def level(values):
    return lax.optimization_barrier(values)


def order(blocks, other):
    at = SWAP if other else range(4)
    return [blocks[dy][dz] for dy in at for dz in at]


def turn_body(place, acts, out):
    rows = [acts[0, pl.ds(pl.multiple_of(place[k], ROWS), ROWS), :] for k in range(16)]
    out[0] = jnp.concatenate(rows, axis=0).T


def turn(place, acts):
    seqs, tokens, feats = acts.shape
    return pl.pallas_call(
        turn_body,
        grid=(seqs,),
        in_specs=[
            pl.BlockSpec(memory_space=pltpu.SMEM),
            pl.BlockSpec((1, tokens, feats), lambda j: (j, 0, 0)),
        ],
        out_specs=pl.BlockSpec((1, feats, tokens), lambda j: (j, 0, 0)),
        out_shape=jax.ShapeDtypeStruct((seqs, feats, tokens), acts.dtype),
        compiler_params=pltpu.CompilerParams(vmem_limit_bytes=6 * 2**20),
        cost_estimate=pl.CostEstimate(
            flops=10**9, bytes_accessed=4 * acts.size, transcendentals=0
        ),
    )(place, acts)


def square_sum(seqs, table, swapped, last, core, *refs):
    acts, refs = refs[:4], refs[4:]
    if last:
        grads, (before, *_, out, total, turned, sem) = refs[:3], refs[3:]
    else:
        grads, sent, total = refs[:-2], *refs[-2:]
    half = total.shape[1]
    if last:
        back = jnp.exp2(before[-8:, :][:1] - SCALE)

    def add(source, seq, first=False):
        act = acts[source][seq]
        there = SWAP[source] if swapped else source
        rows = [grads[at][(*index, there, seq)] for at, index in table]
        grad = jnp.concatenate(rows, axis=0)
        for n in range(half // LANES):
            part = jnp.dot(
                act,
                grad[:, n * LANES : (n + 1) * LANES],
                preferred_element_type=jnp.float32,
            )
            at = (slice(None), slice(n * LANES, (n + 1) * LANES))
            if not first:
                total[at] += part * part
            elif last:
                total[at] = before[: total.shape[0], at[1]] * back[:, at[1]] + part * part
            else:
                total[at] = part * part

    add(0, 0, first=True)
    for source in range(1, 4):
        add(source, 0)

    @pl.loop(1, SEQS_DP)
    def _(seq):
        for source in range(4):
            add(source, seq)

    if last:
        where = 1 - core[0] if swapped else core[0]
        turned[...] = total[...].T * jnp.float32(1 / seqs)
        at = pl.ds(pl.multiple_of(where * half, half), half)
        copy = pltpu.make_async_copy(turned, out.at[at, :], sem)
        copy.start()
        copy.wait()
    else:
        peak = jnp.max(total[...], axis=(0, 1), keepdims=True)
        exponent = jnp.floor(jnp.log2(jnp.maximum(peak, jnp.float32(1e-30))))
        sent[: total.shape[0], :] = total[...] * jnp.exp2(SCALE - exponent)
        sent[total.shape[0] :, :] = jnp.broadcast_to(exponent, (ROWS, half))


def add_side(seqs, core, acts, grads, table, swapped, before=None, out=None):
    _, feats, tokens = acts[0].shape
    half = grads[0].shape[-1]
    last = before is not None
    total = jax.ShapeDtypeStruct((feats, half), jnp.float32)
    args = [core, *acts, *grads]
    specs = [pl.BlockSpec(memory_space=pltpu.SMEM)] + [VMEM] * (len(args) - 1)
    anywhere = pl.BlockSpec(memory_space=pl.ANY)
    if last:
        args.append(before)
        specs.append(VMEM)
        if swapped:
            args.append(out)
            specs.append(anywhere)
        result = dict(
            out_shape=jax.ShapeDtypeStruct((2 * half, feats), jnp.float32),
            out_specs=anywhere,
            scratch_shapes=[
                pltpu.VMEM(total.shape, jnp.float32),
                pltpu.VMEM((half, feats), jnp.float32),
                pltpu.SemaphoreType.DMA,
            ],
            input_output_aliases={len(args) - 1: 0} if swapped else {},
        )
    else:
        result = dict(
            out_shape=jax.ShapeDtypeStruct((feats + ROWS, half), jnp.float32),
            out_specs=VMEM,
            scratch_shapes=[pltpu.VMEM(total.shape, jnp.float32)],
        )
    return pl.pallas_call(
        functools.partial(square_sum, seqs, table, swapped, last),
        in_specs=specs,
        compiler_params=pltpu.CompilerParams(vmem_limit_bytes=6 * 2**20),
        cost_estimate=pl.CostEstimate(
            flops=2 * 12 * tokens * half * feats,
            bytes_accessed=8 * 2**20,
            transcendentals=0,
        ),
        **result,
    )(*args)


def to_owner(grads, core, zlo, sources):
    seq_dev, rows, width = grads.shape
    block = grads.reshape(seq_dev, rows, 2, 4, 2, width // 16).transpose(4, 3, 2, 0, 1, 5)
    mine = lax.dynamic_index_in_dim(block, core, 0, keepdims=False)
    other = lax.dynamic_index_in_dim(block, 1 - core, 0, keepdims=False)
    other = swap(other, "core")
    low = jnp.where(core == 0, mine, other)
    high = jnp.where(core == 0, other, mine)
    both = jnp.concatenate([low, high], axis=3)
    both = lax.all_to_all(both, "x", 0, 0, tiled=True)

    def part(s, z):
        start = (s, z, 0, 0, 0)
        return lax.dynamic_slice(both, start, (1, 1, *both.shape[2:])).reshape(both.shape[2:])

    return jnp.stack([jnp.stack([part(s, z) for s in sources]) for z in (1 - zlo, zlo)])


def cross_zlo(total):
    return swap(total.astype(jnp.float16), "zlo")


def per_device(activations, out_grads):
    zlo, y, zhi, core = (lax.axis_index(a) for a in ("zlo", "y", "zhi", "core"))
    seq_dev, rows, width = out_grads.shape
    seqs = seq_dev * 8
    way = 1 - 2 * core
    offsets = (0, -way, way, 2)
    place = [
        ROWS * (((y + dy) % 4) * 4 + (zhi + dz) % 4) for dy in offsets for dz in offsets
    ]
    place = jnp.stack(place).astype(jnp.int32)
    which = jnp.reshape(core, (1,)).astype(jnp.int32)

    x = lax.axis_index("x")
    g = to_owner(out_grads, core, zlo, [(x + by) % 4 for by in offsets])
    acts = turn(place, activations)
    g, acts = level((g, acts))

    z1p, z1q = send(g[0], "zhi", 1), send(g[0], "zhi", -1)
    own_p, own_q = send(g, "y", 1), send(g, "y", -1)
    ap = send(acts, "x", 1)
    z1p, z1q, own_p, own_q, ap, g, acts = level((z1p, z1q, own_p, own_q, ap, g, acts))

    z1f = send(z1p, "zhi", 1)
    own_f = send(own_p, "y", 1)
    aq = send(acts, "x", -1)
    z1p, z1q, z1f, own_p, own_q, own_f, g = level(
        (z1p, z1q, z1f, own_p, own_q, own_f, g)
    )

    r1 = jnp.stack([z1p, z1q, z1f])
    y1p, y1q = send(r1, "y", 1), send(r1, "y", -1)
    z2p, z2q = send(g[1], "zhi", 1), send(g[1], "zhi", -1)
    r1, y1p, y1q, z2p, z2q, ap, aq, acts, own_p, own_q = level(
        (r1, y1p, y1q, z2p, z2q, ap, aq, acts, own_p, own_q)
    )

    z2f = send(z2p, "zhi", 1)
    w1p = jnp.concatenate([own_p[:1], y1p])
    y1f = send(y1p, "y", 1)
    af = send(ap, "x", 1)
    some1 = jnp.stack(
        [jnp.concatenate([g[:1], r1]), w1p, jnp.concatenate([own_q[:1], y1q])]
    )
    some1_t = swap(some1, "core")
    z2p, z2q, z2f, own_p, own_q, own_f, some1_t, y1f, af = level(
        (z2p, z2q, z2f, own_p, own_q, own_f, some1_t, y1f, af)
    )
    w1f = jnp.concatenate([own_f[:1], y1f])

    r2 = jnp.stack([z2p, z2q, z2f])
    y2p, y2q = send(r2, "y", 1), send(r2, "y", -1)
    some2 = jnp.stack([w1f, jnp.concatenate([g[1:], r2])])
    some2_t = swap(some2, "core")

    def whole(at, *index):
        return [(at, (*index, dz)) for dz in range(4)]

    acts = [acts, ap, aq, af]
    table = order([whole(0, 0), whole(0, 1), whole(0, 2), whole(1)], False)
    first = add_side(seqs, which, acts, [some1, w1f], table, False)
    first = cross_zlo(first)
    table = order([whole(0, 0), whole(0, 1), whole(0, 2), whole(1, 0)], True)
    second = add_side(seqs, which, acts, [some1_t, some2_t], table, True)
    first, second, y2p, y2q, own_p, own_q = level(
        (first, second, y2p, y2q, own_p, own_q)
    )

    y2f = send(y2p, "y", 1)
    second = cross_zlo(second)
    some3 = jnp.concatenate([own_p[1:], y2p, own_q[1:], y2q, own_f[1:]])
    some3_t = swap(some3, "core")
    second, y2f_tied = level((second, y2f))
    y2f_t = swap(y2f_tied, "core")

    def last_blocks():
        below = [(1, (dz,)) for dz in range(4)]
        above = [(1, (4 + dz,)) for dz in range(4)]
        return [whole(0, 1), below, above, [(1, (8,))] + [(2, (dz,)) for dz in range(3)]]

    table = order(last_blocks(), False)
    grads = [some2, some3, y2f]
    out = add_side(seqs, which, acts, grads, table, False, first.astype(jnp.float32))
    table = order(last_blocks(), True)
    grads = [some2_t, some3_t, y2f_t]
    return add_side(seqs, which, acts, grads, table, True, second.astype(jnp.float32), out)


def solution(mesh):
    fine = Mesh(mesh.devices.reshape(SIZES), AXES)
    dp, tensor = AXES[:2], AXES[2:]
    placed = (P(dp, None, tensor), P(dp, tensor, None))
    return jax.shard_map(
        per_device, mesh=fine, in_specs=placed, out_specs=P(dp, tensor), check_vma=False
    )
```

time: 336 us -> 123 us (0.37)
  waiting for transfers between devices: 279 us -> 63.9 us
  matrix products: 40.8 us -> 0 us
  starting transfers between devices: 0.04 us -> 40.4 us
  Pallas kernels: 0 us -> 13.8 us
  between operations: 13.4 us -> 0.71 us
    reduce_scatter x1 -> x0, waiting for transfers between devices: 179 us -> none  [per_device(): lax.psum_scatter(lax.fori_loop(0, seq_dev, add_seq, jnp.zeros((lax.axis_s...]
    all_gather x1 -> x0, waiting for transfers between devices: 99.1 us -> none  [per_device(): full_grads = lax.all_gather(out_grads, 'tensor', axis=1, tiled=True)]
    ppermute x0 -> x25, waiting for transfers between devices: none -> 57.4 us  [the longest x18 31 us: send(): return lax.ppermute(value, (axis, 'core'), pairs)]
    dot_general x3 -> x0, matrix products: 40.8 us -> none  [squared_grad(): lax.dot_general(grads, acts, (((0,), (0,)), ((), ())), preferred_element_...]
    ppermute x0 -> x25, starting transfers between devices: none -> 37 us  [the longest x18 28.6 us: send(): return lax.ppermute(value, (axis, 'core'), pairs)]
    pallas_call x0 -> x5, Pallas kernels: none -> 13.8 us  [the longest x4 12.9 us: add_side(): pl.pallas_call(functools.partial(square_sum, seqs, table, swapped, last),...]
    all_to_all x0 -> x1, waiting for transfers between devices: none -> 6.51 us  [to_owner(): both = lax.all_to_all(both, 'x', 0, 0, tiled=True)]
    all_to_all x0 -> x1, starting transfers between devices: none -> 3.46 us  [to_owner(): both = lax.all_to_all(both, 'x', 0, 0, tiled=True)]
  transfers between devices with their start and end apart: 2 -> 26, of which waited for: 2 -> 12; matrix products, arithmetic and copies ran while one was open for 0% -> 1% of each run, Pallas kernels for 0% -> 8%
where the time goes in v2:
time: 123 us
  waiting for transfers between devices  63.9 us (52%)
  starting transfers between devices  40.4 us (33%)
  Pallas kernels  13.8 us (11%)
  other arithmetic  2.35 us (2%)
  local copies, waits for them, and re-layouts  1.43 us (1%)
    ppermute x18, waiting for transfers between devices, send(): return lax.ppermute(value, (axis, 'core'), pairs)  31 us
    ppermute x18, starting transfers between devices, send(): return lax.ppermute(value, (axis, 'core'), pairs)  28.6 us
    ppermute x7, waiting for transfers between devices, swap(): return lax.ppermute(value, axis, [(0, 1), (1, 0)])  26.4 us
    pallas_call x4, Pallas kernels, add_side(): pl.pallas_call(functools.partial(square_sum, seqs, table, swapped, last),...  12.9 us
    ppermute x7, starting transfers between devices, swap(): return lax.ppermute(value, axis, [(0, 1), (1, 0)])  8.42 us
    all_to_all x1, waiting for transfers between devices, to_owner(): both = lax.all_to_all(both, 'x', 0, 0, tiled=True)  6.51 us
    all_to_all x1, starting transfers between devices, to_owner(): both = lax.all_to_all(both, 'x', 0, 0, tiled=True)  3.46 us
  transfers between devices with their start and end apart: 26, of which 12 were waited for; matrix products, arithmetic and copies ran while one was open for 1% of the time, Pallas kernels for 8%

profile of v2, /device:TPU:1, one launch (start us, length us, event | category | flops | bytes accessed | tf_op | source)
XLA Modules:
  0.0 122.6 jit_solution(7276475723300252892)
XLA Ops:
  0.0 1.0 constant_dynamic-slice_fusion.1
  1.1 3.3 %collective-permute-start = (bf16[4,2,3,8,512]{4,3,2,1,0:T(8,128)(2,1)S(1)}, bf16[4,2,3,8,512]{4,3,2,1,0:T(8,128)(2,1)S(1)}, u32[]{:S(2)}, u32[]{:S(2)}) collective-permute-start(bf16[4,2,3,8,512]{4,3,2,1,0:T(8,128)(2,1)S(1)} %bitcast.81), channel_id=1, source_target_pairs={{0,1},{1,0},{2,3},{3,2},{4,5},{5,4},{6,7},{7,6},{8,9},{9,8},{10,11... | collective-permute-start | bytes 589832 | tf_op jit(solution)/shard_map/ppermute | solution.py:21
  4.4 1.1 collective-permute-done
  6.3 3.5 %all-to-all-start = ((bf16[4,2,3,16,512]{4,3,2,1,0:T(8,128)(2,1)}), bf16[4,2,3,16,512]{4,3,2,1,0:T(8,128)(2,1)S(1)}, u32[]{:S(2)}, u32[]{:S(2)}) async-start(bf16[4,2,3,16,512]{4,3,2,1,0:T(8,128)(2,1)} %pad_maximum_fusion.5), calls=%async_computation | async-start | bytes 786432 | tf_op jit(solution)/shard_map/all_to_all | solution.py:169
  10.1 1.0 shard_map.28.refs_0_
  11.1 6.5 %all-to-all-done = bf16[4,2,3,16,512]{4,3,2,1,0:T(8,128)(2,1)S(1)} async-done(((bf16[4,2,3,16,512]{4,3,2,1,0:T(8,128)(2,1)}), bf16[4,2,3,16,512]{4,3,2,1,0:T(8,128)(2,1)S(1)}, u32[]{:S(2)}, u32[]{:S(2)}) %all-to-all-start) | async-done | bytes 393248 | tf_op jit(solution)/shard_map/all_to_all | solution.py:169
  17.7 1.0 collective-permute-start.5
  18.7 2.7 %collective-permute-start.3 = (bf16[2,4,3,16,512]{4,3,2,1,0:T(8,128)(2,1)S(1)}, bf16[2,4,3,16,512]{4,3,2,1,0:T(8,128)(2,1)S(1)}, u32[]{:S(2)}, u32[]{:S(2)}) collective-permute-start(bf16[2,4,3,16,512]{4,3,2,1,0:T(8,128)(2,1)S(1)} %pad_maximum_fusion.6), channel_id=1, source_target_pairs={{0,8},{1,25},{8,16},{9,1},{16,24},{17,9},{24,0},{25,17},{2,10},{3,... | collective-permute-start | bytes 1179656 | tf_op jit(solution)/shard_map/ppermute | solution.py:30
  21.4 1.4 %collective-permute-start.2 = (bf16[4,3,16,512]{3,2,1,0:T(8,128)(2,1)S(1)}, bf16[4,3,16,512]{3,2,1,0:T(8,128)(2,1)S(1)}, u32[]{:S(2)}, u32[]{:S(2)}) collective-permute-start(bf16[4,3,16,512]{3,2,1,0:T(8,128)(2,1)S(1)} %slice_bitcast_fusion), channel_id=1, source_target_pairs={{0,6},{1,3},{2,0},{3,5},{4,2},{5,7},{6,4},{7,1},{8,14},{9,11},{10,... | collective-permute-start | bytes 589832 | tf_op jit(solution)/shard_map/ppermute | solution.py:30
  22.7 3.1 %collective-permute-start.1 = (bf16[4,3,16,512]{3,2,1,0:T(8,128)(2,1)S(1)}, bf16[4,3,16,512]{3,2,1,0:T(8,128)(2,1)S(1)}, u32[]{:S(2)}, u32[]{:S(2)}) collective-permute-start(bf16[4,3,16,512]{3,2,1,0:T(8,128)(2,1)S(1)} %slice_bitcast_fusion), channel_id=1, source_target_pairs={{0,2},{1,7},{2,4},{3,1},{4,6},{5,3},{6,0},{7,5},{8,10},{9,15},{10,... | collective-permute-start | bytes 589832 | tf_op jit(solution)/shard_map/ppermute | solution.py:30
  25.9 3.6 %collective-permute-done.2 = bf16[4,3,16,512]{3,2,1,0:T(8,128)(2,1)S(1)} collective-permute-done((bf16[4,3,16,512]{3,2,1,0:T(8,128)(2,1)S(1)}, bf16[4,3,16,512]{3,2,1,0:T(8,128)(2,1)S(1)}, u32[]{:S(2)}, u32[]{:S(2)}) %collective-permute-start.2) | collective-permute-done | bytes 196640 | tf_op jit(solution)/shard_map/ppermute | solution.py:30
  29.4 5.0 %collective-permute-done.1 = bf16[4,3,16,512]{3,2,1,0:T(8,128)(2,1)S(1)} collective-permute-done((bf16[4,3,16,512]{3,2,1,0:T(8,128)(2,1)S(1)}, bf16[4,3,16,512]{3,2,1,0:T(8,128)(2,1)S(1)}, u32[]{:S(2)}, u32[]{:S(2)}) %collective-permute-start.1) | collective-permute-done | bytes 196640 | tf_op jit(solution)/shard_map/ppermute | solution.py:30
  34.4 3.0 %collective-permute-start.7 = (bf16[2,4,3,16,512]{4,3,2,1,0:T(8,128)(2,1)S(1)}, bf16[2,4,3,16,512]{4,3,2,1,0:T(8,128)(2,1)S(1)}, u32[]{:S(2)}, u32[]{:S(2)}) collective-permute-start(bf16[2,4,3,16,512]{4,3,2,1,0:T(8,128)(2,1)S(1)} %collective-permute-done.3), channel_id=1, source_target_pairs={{0,8},{1,25},{8,16},{9,1},{16,24},{17,9},{24,0},{25,17},{2,10},{3,... | collective-permute-start | bytes 1179656 | tf_op jit(solution)/shard_map/ppermute | solution.py:30
  37.5 1.2 collective-permute-start.6
  38.7 1.3 %collective-permute-start.12 = (bf16[3,512,256]{2,1,0:T(8,128)(2,1)S(1)}, bf16[3,512,256]{2,1,0:T(8,128)(2,1)S(1)}, u32[]{:S(2)}, u32[]{:S(2)}) collective-permute-start(bf16[3,512,256]{2,1,0:T(8,128)(2,1)S(1)} %shard_map.28.refs_0_), channel_id=1, source_target_pairs={{0,96},{1,33},{32,0},{33,65},{64,32},{65,97},{96,64},{97,1},{2,98}... | collective-permute-start | bytes 2359304 | tf_op jit(solution)/shard_map/ppermute | solution.py:30
  40.0 6.0 %collective-permute-done.6 = bf16[4,3,16,512]{3,2,1,0:T(8,128)(2,1)S(1)} collective-permute-done((bf16[4,3,16,512]{3,2,1,0:T(8,128)(2,1)S(1)}, bf16[4,3,16,512]{3,2,1,0:T(8,128)(2,1)S(1)}, u32[]{:S(2)}, u32[]{:S(2)}) %collective-permute-start.6) | collective-permute-done | bytes 196640 | tf_op jit(solution)/shard_map/ppermute | solution.py:30
  46.2 2.7 %collective-permute-start.8 = (bf16[3,4,3,16,512]{4,3,2,1,0:T(8,128)(2,1)S(1)}, bf16[3,4,3,16,512]{4,3,2,1,0:T(8,128)(2,1)S(1)}, u32[]{:S(2)}, u32[]{:S(2)}) collective-permute-start(bf16[3,4,3,16,512]{4,3,2,1,0:T(8,128)(2,1)S(1)} %pad_maximum_fusion.3), channel_id=1, source_target_pairs={{0,8},{1,25},{8,16},{9,1},{16,24},{17,9},{24,0},{25,17},{2,10},{3,... | collective-permute-start | bytes 1769480 | tf_op jit(solution)/shard_map/ppermute | solution.py:30
  48.9 3.4 %collective-permute-start.11 = (bf16[4,3,16,512]{3,2,1,0:T(8,128)(2,1)S(1)}, bf16[4,3,16,512]{3,2,1,0:T(8,128)(2,1)S(1)}, u32[]{:S(2)}, u32[]{:S(2)}) collective-permute-start(bf16[4,3,16,512]{3,2,1,0:T(8,128)(2,1)S(1)} %get-tuple-element.94), channel_id=1, source_target_pairs={{0,6},{1,3},{2,0},{3,5},{4,2},{5,7},{6,4},{7,1},{8,14},{9,11},{10,... | collective-permute-start | bytes 589832 | tf_op jit(solution)/shard_map/ppermute | solution.py:30
  52.5 5.8 %collective-permute-done.11 = bf16[4,3,16,512]{3,2,1,0:T(8,128)(2,1)S(1)} collective-permute-done((bf16[4,3,16,512]{3,2,1,0:T(8,128)(2,1)S(1)}, bf16[4,3,16,512]{3,2,1,0:T(8,128)(2,1)S(1)}, u32[]{:S(2)}, u32[]{:S(2)}) %collective-permute-start.11) | collective-permute-done | bytes 196640 | tf_op jit(solution)/shard_map/ppermute | solution.py:30
  58.4 2.3 %collective-permute-done.10 = bf16[4,3,16,512]{3,2,1,0:T(8,128)(2,1)S(1)} collective-permute-done((bf16[4,3,16,512]{3,2,1,0:T(8,128)(2,1)S(1)}, bf16[4,3,16,512]{3,2,1,0:T(8,128)(2,1)S(1)}, u32[]{:S(2)}, u32[]{:S(2)}) %collective-permute-start.10) | collective-permute-done | bytes 196640 | tf_op jit(solution)/shard_map/ppermute | solution.py:30
  61.4 2.3 %collective-permute-start.14 = (bf16[3,4,4,3,16,512]{5,4,3,2,1,0:T(8,128)(2,1)S(1)}, bf16[3,4,4,3,16,512]{5,4,3,2,1,0:T(8,128)(2,1)S(1)}, u32[]{:S(2)}, u32[]{:S(2)}) collective-permute-start(bf16[3,4,4,3,16,512]{5,4,3,2,1,0:T(8,128)(2,1)S(1)} %pad_maximum_fusion.refs_4_), channel_id=1, source_target_pairs={{0,1},{1,0},{2,3},{3,2},{4,5},{5,4},{6,7},{7,6},{8,9},{9,8},{10,11... | collective-permute-start | bytes 7077896 | tf_op jit(solution)/shard_map/ppermute | solution.py:21
  63.7 4.4 %collective-permute-start.16 = (bf16[3,512,256]{2,1,0:T(8,128)(2,1)S(1)}, bf16[3,512,256]{2,1,0:T(8,128)(2,1)S(1)}, u32[]{:S(2)}, u32[]{:S(2)}) collective-permute-start(bf16[3,512,256]{2,1,0:T(8,128)(2,1)S(1)} %collective-permute-done.5.refs_1_), channel_id=1, source_target_pairs={{0,32},{1,97},{32,64},{33,1},{64,96},{65,33},{96,0},{97,65},{2,34}... | collective-permute-start | bytes 2359304 | tf_op jit(solution)/shard_map/ppermute | solution.py:30
  69.0 6.0 %collective-permute-done.13 = bf16[4,3,16,512]{3,2,1,0:T(8,128)(2,1)S(1)} collective-permute-done((bf16[4,3,16,512]{3,2,1,0:T(8,128)(2,1)S(1)}, bf16[4,3,16,512]{3,2,1,0:T(8,128)(2,1)S(1)}, u32[]{:S(2)}, u32[]{:S(2)}) %collective-permute-start.13) | collective-permute-done | bytes 196640 | tf_op jit(solution)/shard_map/ppermute | solution.py:30
  75.0 2.1 %collective-permute-done.15 = bf16[3,4,3,16,512]{4,3,2,1,0:T(8,128)(2,1)S(1)} collective-permute-done((bf16[3,4,3,16,512]{4,3,2,1,0:T(8,128)(2,1)S(1)}, bf16[3,4,3,16,512]{4,3,2,1,0:T(8,128)(2,1)S(1)}, u32[]{:S(2)}, u32[]{:S(2)}) %collective-permute-start.15) | collective-permute-done | bytes 589856 | tf_op jit(solution)/shard_map/ppermute | solution.py:30
  77.5 1.6 %collective-permute-start.17 = (bf16[2,4,4,3,16,512]{5,4,3,2,1,0:T(8,128)(2,1)S(1)}, bf16[2,4,4,3,16,512]{5,4,3,2,1,0:T(8,128)(2,1)S(1)}, u32[]{:S(2)}, u32[]{:S(2)}) collective-permute-start(bf16[2,4,4,3,16,512]{5,4,3,2,1,0:T(8,128)(2,1)S(1)} %pad_maximum_fusion.1.refs_4_), channel_id=1, source_target_pairs={{0,1},{1,0},{2,3},{3,2},{4,5},{5,4},{6,7},{7,6},{8,9},{9,8},{10,11... | collective-permute-start | bytes 4718600 | tf_op jit(solution)/shard_map/ppermute | solution.py:21
  79.3 2.7 %collective-permute-start.19 = (bf16[3,4,3,16,512]{4,3,2,1,0:T(8,128)(2,1)S(1)}, bf16[3,4,3,16,512]{4,3,2,1,0:T(8,128)(2,1)S(1)}, u32[]{:S(2)}, u32[]{:S(2)}) collective-permute-start(bf16[3,4,3,16,512]{4,3,2,1,0:T(8,128)(2,1)S(1)} %pad_maximum_fusion.4), channel_id=1, source_target_pairs={{0,8},{1,25},{8,16},{9,1},{16,24},{17,9},{24,0},{25,17},{2,10},{3,... | collective-permute-start | bytes 1769480 | tf_op jit(solution)/shard_map/ppermute | solution.py:30
  81.9 2.8 %shard_map.29 = f32[528,512]{1,0:T(8,128)S(1)} custom-call(s32[1]{0:T(128)} %bitcast.core, bf16[3,512,256]{2,1,0:T(8,128)(2,1)S(1)} %shard_map.28.refs_0_, bf16[3,512,256]{2,1,0:T(8,128)(2,1)S(1)} %collective-permute-done.5.refs_1_, bf16[3,512,256]{2,1,0:T(8,128)(2,1)S(1)} %collective-permute-done.12.refs_2_, ...), custom_call_target="tpu_custom_call" | custom-call | flops 1610612736 | bytes 8388608 | tf_op jit(solution)/shard_map/pallas_call | solution.py:147
  84.9 2.8 %shard_map.30 = f32[528,512]{1,0:T(8,128)S(1)} custom-call(s32[1]{0:T(128)} %bitcast.core, bf16[3,512,256]{2,1,0:T(8,128)(2,1)S(1)} %shard_map.28.refs_0_, bf16[3,512,256]{2,1,0:T(8,128)(2,1)S(1)} %collective-permute-done.5.refs_1_, bf16[3,512,256]{2,1,0:T(8,128)(2,1)S(1)} %collective-permute-done.12.refs_2_, ...), custom_call_target="tpu_custom_call" | custom-call | flops 1610612736 | bytes 8388608 | tf_op jit(solution)/shard_map/pallas_call | solution.py:147
  87.7 11.1 %collective-permute-done.18 = f16[528,512]{1,0:T(8,128)(2,1)S(1)} collective-permute-done((f16[528,512]{1,0:T(8,128)(2,1)S(1)}, f16[528,512]{1,0:T(8,128)(2,1)S(1)}, u32[]{:S(2)}, u32[]{:S(2)}) %collective-permute-start.18) | collective-permute-done | bytes 540704 | tf_op jit(solution)/shard_map/ppermute | solution.py:21
  100.2 14.2 %collective-permute-done.22 = f16[528,512]{1,0:T(8,128)(2,1)S(1)} collective-permute-done((f16[528,512]{1,0:T(8,128)(2,1)S(1)}, f16[528,512]{1,0:T(8,128)(2,1)S(1)}, u32[]{:S(2)}, u32[]{:S(2)}) %collective-permute-start.22) | collective-permute-done | bytes 540704 | tf_op jit(solution)/shard_map/ppermute | solution.py:21
  115.1 3.6 %shard_map.31.refs_8_ = f32[1024,512]{1,0:T(8,128)} custom-call(s32[1]{0:T(128)} %bitcast.core, bf16[3,512,256]{2,1,0:T(8,128)(2,1)S(1)} %shard_map.28.refs_0_, bf16[3,512,256]{2,1,0:T(8,128)(2,1)S(1)} %collective-permute-done.5.refs_1_, bf16[3,512,256]{2,1,0:T(8,128)(2,1)S(1)} %collective-permute-done.12.refs_2_, ...), custom_call_target="tpu_custom_call" | custom-call | flops 1610612736 | bytes 8388608 | tf_op jit(solution)/shard_map/pallas_call | solution.py:147
  118.8 3.6 %shard_map.32 = f32[1024,512]{1,0:T(8,128)} custom-call(s32[1]{0:T(128)} %bitcast.core, bf16[3,512,256]{2,1,0:T(8,128)(2,1)S(1)} %shard_map.28.refs_0_, bf16[3,512,256]{2,1,0:T(8,128)(2,1)S(1)} %collective-permute-done.5.refs_1_, bf16[3,512,256]{2,1,0:T(8,128)(2,1)S(1)} %collective-permute-done.12.refs_2_, ...), custom_call_target="tpu_custom_call", output_to_operand_aliasing={{}: (9, {})} | custom-call | flops 1610612736 | bytes 8388608 | tf_op jit(solution)/shard_map/pallas_call | solution.py:147
  (58 shorter events, 6.0 us)
Async XLA Ops:
  1.1 9.0 %copy-start = (bf16[3,256,512]{2,1,0:T(8,128)(2,1)S(1)}, bf16[3,256,512]{2,1,0:T(8,128)(2,1)}, u32[]{:S(2)}) copy-start(bf16[3,256,512]{2,1,0:T(8,128)(2,1)} %acts.1) | copy-start | bytes 2359300
  1.1 4.4 %collective-permute-start = (bf16[4,2,3,8,512]{4,3,2,1,0:T(8,128)(2,1)S(1)}, bf16[4,2,3,8,512]{4,3,2,1,0:T(8,128)(2,1)S(1)}, u32[]{:S(2)}, u32[]{:S(2)}) collective-permute-start(bf16[4,2,3,8,512]{4,3,2,1,0:T(8,128)(2,1)S(1)} %bitcast.81), channel_id=1, source_target_pairs={{0,1},{1,0},{2,3},{3,2},{4,5},{5,4},{6,7},{7,6},{8,9},{9,8},{10,11... | collective-permute-start | bytes 589832 | tf_op jit(solution)/shard_map/ppermute | solution.py:21
  6.3 11.3 %all-to-all-start = ((bf16[4,2,3,16,512]{4,3,2,1,0:T(8,128)(2,1)}), bf16[4,2,3,16,512]{4,3,2,1,0:T(8,128)(2,1)S(1)}, u32[]{:S(2)}, u32[]{:S(2)}) async-start(bf16[4,2,3,16,512]{4,3,2,1,0:T(8,128)(2,1)} %pad_maximum_fusion.5), calls=%async_computation | async-start | bytes 786432 | tf_op jit(solution)/shard_map/all_to_all | solution.py:169
  17.7 16.7 %collective-permute-start.5 = (bf16[3,512,256]{2,1,0:T(8,128)(2,1)S(1)}, bf16[3,512,256]{2,1,0:T(8,128)(2,1)S(1)}, u32[]{:S(2)}, u32[]{:S(2)}) collective-permute-start(bf16[3,512,256]{2,1,0:T(8,128)(2,1)S(1)} %shard_map.28.refs_0_), channel_id=1, source_target_pairs={{0,32},{1,97},{32,64},{33,1},{64,96},{65,33},{96,0},{97,65},{2,34}... | collective-permute-start | bytes 2359304 | tf_op jit(solution)/shard_map/ppermute | solution.py:30
  18.7 15.7 %collective-permute-start.4 = (bf16[2,4,3,16,512]{4,3,2,1,0:T(8,128)(2,1)S(1)}, bf16[2,4,3,16,512]{4,3,2,1,0:T(8,128)(2,1)S(1)}, u32[]{:S(2)}, u32[]{:S(2)}) collective-permute-start(bf16[2,4,3,16,512]{4,3,2,1,0:T(8,128)(2,1)S(1)} %pad_maximum_fusion.6), channel_id=1, source_target_pairs={{0,24},{1,9},{8,0},{9,17},{16,8},{17,25},{24,16},{25,1},{2,26},{3,... | collective-permute-start | bytes 1179656 | tf_op jit(solution)/shard_map/ppermute | solution.py:30
  18.7 15.7 %collective-permute-start.3 = (bf16[2,4,3,16,512]{4,3,2,1,0:T(8,128)(2,1)S(1)}, bf16[2,4,3,16,512]{4,3,2,1,0:T(8,128)(2,1)S(1)}, u32[]{:S(2)}, u32[]{:S(2)}) collective-permute-start(bf16[2,4,3,16,512]{4,3,2,1,0:T(8,128)(2,1)S(1)} %pad_maximum_fusion.6), channel_id=1, source_target_pairs={{0,8},{1,25},{8,16},{9,1},{16,24},{17,9},{24,0},{25,17},{2,10},{3,... | collective-permute-start | bytes 1179656 | tf_op jit(solution)/shard_map/ppermute | solution.py:30
  21.4 8.1 %collective-permute-start.2 = (bf16[4,3,16,512]{3,2,1,0:T(8,128)(2,1)S(1)}, bf16[4,3,16,512]{3,2,1,0:T(8,128)(2,1)S(1)}, u32[]{:S(2)}, u32[]{:S(2)}) collective-permute-start(bf16[4,3,16,512]{3,2,1,0:T(8,128)(2,1)S(1)} %slice_bitcast_fusion), channel_id=1, source_target_pairs={{0,6},{1,3},{2,0},{3,5},{4,2},{5,7},{6,4},{7,1},{8,14},{9,11},{10,... | collective-permute-start | bytes 589832 | tf_op jit(solution)/shard_map/ppermute | solution.py:30
  22.7 11.7 %collective-permute-start.1 = (bf16[4,3,16,512]{3,2,1,0:T(8,128)(2,1)S(1)}, bf16[4,3,16,512]{3,2,1,0:T(8,128)(2,1)S(1)}, u32[]{:S(2)}, u32[]{:S(2)}) collective-permute-start(bf16[4,3,16,512]{3,2,1,0:T(8,128)(2,1)S(1)} %slice_bitcast_fusion), channel_id=1, source_target_pairs={{0,2},{1,7},{2,4},{3,1},{4,6},{5,3},{6,0},{7,5},{8,10},{9,15},{10,... | collective-permute-start | bytes 589832 | tf_op jit(solution)/shard_map/ppermute | solution.py:30
  34.4 11.6 %collective-permute-start.7 = (bf16[2,4,3,16,512]{4,3,2,1,0:T(8,128)(2,1)S(1)}, bf16[2,4,3,16,512]{4,3,2,1,0:T(8,128)(2,1)S(1)}, u32[]{:S(2)}, u32[]{:S(2)}) collective-permute-start(bf16[2,4,3,16,512]{4,3,2,1,0:T(8,128)(2,1)S(1)} %collective-permute-done.3), channel_id=1, source_target_pairs={{0,8},{1,25},{8,16},{9,1},{16,24},{17,9},{24,0},{25,17},{2,10},{3,... | collective-permute-start | bytes 1179656 | tf_op jit(solution)/shard_map/ppermute | solution.py:30
  37.5 8.5 %collective-permute-start.6 = (bf16[4,3,16,512]{3,2,1,0:T(8,128)(2,1)S(1)}, bf16[4,3,16,512]{3,2,1,0:T(8,128)(2,1)S(1)}, u32[]{:S(2)}, u32[]{:S(2)}) collective-permute-start(bf16[4,3,16,512]{3,2,1,0:T(8,128)(2,1)S(1)} %collective-permute-done.1), channel_id=1, source_target_pairs={{0,2},{1,7},{2,4},{3,1},{4,6},{5,3},{6,0},{7,5},{8,10},{9,15},{10,... | collective-permute-start | bytes 589832 | tf_op jit(solution)/shard_map/ppermute | solution.py:30
  38.7 22.0 %collective-permute-start.12 = (bf16[3,512,256]{2,1,0:T(8,128)(2,1)S(1)}, bf16[3,512,256]{2,1,0:T(8,128)(2,1)S(1)}, u32[]{:S(2)}, u32[]{:S(2)}) collective-permute-start(bf16[3,512,256]{2,1,0:T(8,128)(2,1)S(1)} %shard_map.28.refs_0_), channel_id=1, source_target_pairs={{0,96},{1,33},{32,0},{33,65},{64,32},{65,97},{96,64},{97,1},{2,98}... | collective-permute-start | bytes 2359304 | tf_op jit(solution)/shard_map/ppermute | solution.py:30
  46.1 14.6 %collective-permute-start.9 = (bf16[3,4,3,16,512]{4,3,2,1,0:T(8,128)(2,1)S(1)}, bf16[3,4,3,16,512]{4,3,2,1,0:T(8,128)(2,1)S(1)}, u32[]{:S(2)}, u32[]{:S(2)}) collective-permute-start(bf16[3,4,3,16,512]{4,3,2,1,0:T(8,128)(2,1)S(1)} %pad_maximum_fusion.3), channel_id=1, source_target_pairs={{0,24},{1,9},{8,0},{9,17},{16,8},{17,25},{24,16},{25,1},{2,26},{3,... | collective-permute-start | bytes 1769480 | tf_op jit(solution)/shard_map/ppermute | solution.py:30
  46.2 14.7 %collective-permute-start.8 = (bf16[3,4,3,16,512]{4,3,2,1,0:T(8,128)(2,1)S(1)}, bf16[3,4,3,16,512]{4,3,2,1,0:T(8,128)(2,1)S(1)}, u32[]{:S(2)}, u32[]{:S(2)}) collective-permute-start(bf16[3,4,3,16,512]{4,3,2,1,0:T(8,128)(2,1)S(1)} %pad_maximum_fusion.3), channel_id=1, source_target_pairs={{0,8},{1,25},{8,16},{9,1},{16,24},{17,9},{24,0},{25,17},{2,10},{3,... | collective-permute-start | bytes 1769480 | tf_op jit(solution)/shard_map/ppermute | solution.py:30
  48.9 9.5 %collective-permute-start.11 = (bf16[4,3,16,512]{3,2,1,0:T(8,128)(2,1)S(1)}, bf16[4,3,16,512]{3,2,1,0:T(8,128)(2,1)S(1)}, u32[]{:S(2)}, u32[]{:S(2)}) collective-permute-start(bf16[4,3,16,512]{3,2,1,0:T(8,128)(2,1)S(1)} %get-tuple-element.94), channel_id=1, source_target_pairs={{0,6},{1,3},{2,0},{3,5},{4,2},{5,7},{6,4},{7,1},{8,14},{9,11},{10,... | collective-permute-start | bytes 589832 | tf_op jit(solution)/shard_map/ppermute | solution.py:30
  52.2 8.4 %collective-permute-start.10 = (bf16[4,3,16,512]{3,2,1,0:T(8,128)(2,1)S(1)}, bf16[4,3,16,512]{3,2,1,0:T(8,128)(2,1)S(1)}, u32[]{:S(2)}, u32[]{:S(2)}) collective-permute-start(bf16[4,3,16,512]{3,2,1,0:T(8,128)(2,1)S(1)} %get-tuple-element.94), channel_id=1, source_target_pairs={{0,2},{1,7},{2,4},{3,1},{4,6},{5,3},{6,0},{7,5},{8,10},{9,15},{10,... | collective-permute-start | bytes 589832 | tf_op jit(solution)/shard_map/ppermute | solution.py:30
  61.4 15.7 %collective-permute-start.14 = (bf16[3,4,4,3,16,512]{5,4,3,2,1,0:T(8,128)(2,1)S(1)}, bf16[3,4,4,3,16,512]{5,4,3,2,1,0:T(8,128)(2,1)S(1)}, u32[]{:S(2)}, u32[]{:S(2)}) collective-permute-start(bf16[3,4,4,3,16,512]{5,4,3,2,1,0:T(8,128)(2,1)S(1)} %pad_maximum_fusion.refs_4_), channel_id=1, source_target_pairs={{0,1},{1,0},{2,3},{3,2},{4,5},{5,4},{6,7},{7,6},{8,9},{9,8},{10,11... | collective-permute-start | bytes 7077896 | tf_op jit(solution)/shard_map/ppermute | solution.py:21
  63.7 13.4 %collective-permute-start.16 = (bf16[3,512,256]{2,1,0:T(8,128)(2,1)S(1)}, bf16[3,512,256]{2,1,0:T(8,128)(2,1)S(1)}, u32[]{:S(2)}, u32[]{:S(2)}) collective-permute-start(bf16[3,512,256]{2,1,0:T(8,128)(2,1)S(1)} %collective-permute-done.5.refs_1_), channel_id=1, source_target_pairs={{0,32},{1,97},{32,64},{33,1},{64,96},{65,33},{96,0},{97,65},{2,34}... | collective-permute-start | bytes 2359304 | tf_op jit(solution)/shard_map/ppermute | solution.py:30
  68.1 9.0 %collective-permute-start.15 = (bf16[3,4,3,16,512]{4,3,2,1,0:T(8,128)(2,1)S(1)}, bf16[3,4,3,16,512]{4,3,2,1,0:T(8,128)(2,1)S(1)}, u32[]{:S(2)}, u32[]{:S(2)}) collective-permute-start(bf16[3,4,3,16,512]{4,3,2,1,0:T(8,128)(2,1)S(1)} %collective-permute-done.8), channel_id=1, source_target_pairs={{0,8},{1,25},{8,16},{9,1},{16,24},{17,9},{24,0},{25,17},{2,10},{3,... | collective-permute-start | bytes 1769480 | tf_op jit(solution)/shard_map/ppermute | solution.py:30
  69.0 6.0 %collective-permute-start.13 = (bf16[4,3,16,512]{3,2,1,0:T(8,128)(2,1)S(1)}, bf16[4,3,16,512]{3,2,1,0:T(8,128)(2,1)S(1)}, u32[]{:S(2)}, u32[]{:S(2)}) collective-permute-start(bf16[4,3,16,512]{3,2,1,0:T(8,128)(2,1)S(1)} %collective-permute-done.10), channel_id=1, source_target_pairs={{0,2},{1,7},{2,4},{3,1},{4,6},{5,3},{6,0},{7,5},{8,10},{9,15},{10,... | collective-permute-start | bytes 589832 | tf_op jit(solution)/shard_map/ppermute | solution.py:30
  77.5 7.4 %collective-permute-start.17 = (bf16[2,4,4,3,16,512]{5,4,3,2,1,0:T(8,128)(2,1)S(1)}, bf16[2,4,4,3,16,512]{5,4,3,2,1,0:T(8,128)(2,1)S(1)}, u32[]{:S(2)}, u32[]{:S(2)}) collective-permute-start(bf16[2,4,4,3,16,512]{5,4,3,2,1,0:T(8,128)(2,1)S(1)} %pad_maximum_fusion.1.refs_4_), channel_id=1, source_target_pairs={{0,1},{1,0},{2,3},{3,2},{4,5},{5,4},{6,7},{7,6},{8,9},{9,8},{10,11... | collective-permute-start | bytes 4718600 | tf_op jit(solution)/shard_map/ppermute | solution.py:21
  79.2 19.7 %collective-permute-start.20 = (bf16[3,4,3,16,512]{4,3,2,1,0:T(8,128)(2,1)S(1)}, bf16[3,4,3,16,512]{4,3,2,1,0:T(8,128)(2,1)S(1)}, u32[]{:S(2)}, u32[]{:S(2)}) collective-permute-start(bf16[3,4,3,16,512]{4,3,2,1,0:T(8,128)(2,1)S(1)} %pad_maximum_fusion.4), channel_id=1, source_target_pairs={{0,24},{1,9},{8,0},{9,17},{16,8},{17,25},{24,16},{25,1},{2,26},{3,... | collective-permute-start | bytes 1769480 | tf_op jit(solution)/shard_map/ppermute | solution.py:30
  79.3 19.6 %collective-permute-start.19 = (bf16[3,4,3,16,512]{4,3,2,1,0:T(8,128)(2,1)S(1)}, bf16[3,4,3,16,512]{4,3,2,1,0:T(8,128)(2,1)S(1)}, u32[]{:S(2)}, u32[]{:S(2)}) collective-permute-start(bf16[3,4,3,16,512]{4,3,2,1,0:T(8,128)(2,1)S(1)} %pad_maximum_fusion.4), channel_id=1, source_target_pairs={{0,8},{1,25},{8,16},{9,1},{16,24},{17,9},{24,0},{25,17},{2,10},{3,... | collective-permute-start | bytes 1769480 | tf_op jit(solution)/shard_map/ppermute | solution.py:30
  84.8 14.0 %collective-permute-start.18 = (f16[528,512]{1,0:T(8,128)(2,1)S(1)}, f16[528,512]{1,0:T(8,128)(2,1)S(1)}, u32[]{:S(2)}, u32[]{:S(2)}) collective-permute-start(f16[528,512]{1,0:T(8,128)(2,1)S(1)} %convert_element_type.12), channel_id=1, source_target_pairs={{0,128},{128,0},{1,129},{129,1},{2,130},{130,2},{3,131},{131,3},{4... | collective-permute-start | bytes 1622024 | tf_op jit(solution)/shard_map/ppermute | solution.py:21
  99.0 19.8 %collective-permute-start.21 = (bf16[9,4,3,16,512]{4,3,2,1,0:T(8,128)(2,1)S(1)}, bf16[9,4,3,16,512]{4,3,2,1,0:T(8,128)(2,1)S(1)}, u32[]{:S(2)}, u32[]{:S(2)}) collective-permute-start(bf16[9,4,3,16,512]{4,3,2,1,0:T(8,128)(2,1)S(1)} %slice_dynamic-update-slice_fusion.refs_5_), channel_id=1, source_target_pairs={{0,1},{1,0},{2,3},{3,2},{4,5},{5,4},{6,7},{7,6},{8,9},{9,8},{10,11... | collective-permute-start | bytes 5308424 | tf_op jit(solution)/shard_map/ppermute | solution.py:21
  99.5 14.8 %collective-permute-start.23 = (bf16[3,4,3,16,512]{4,3,2,1,0:T(8,128)(2,1)S(1)}, bf16[3,4,3,16,512]{4,3,2,1,0:T(8,128)(2,1)S(1)}, u32[]{:S(2)}, u32[]{:S(2)}) collective-permute-start(bf16[3,4,3,16,512]{4,3,2,1,0:T(8,128)(2,1)S(1)} %collective-permute-done.19), channel_id=1, source_target_pairs={{0,8},{1,25},{8,16},{9,1},{16,24},{17,9},{24,0},{25,17},{2,10},{3,... | collective-permute-start | bytes 1769480 | tf_op jit(solution)/shard_map/ppermute | solution.py:30
  100.1 14.3 %collective-permute-start.22 = (f16[528,512]{1,0:T(8,128)(2,1)S(1)}, f16[528,512]{1,0:T(8,128)(2,1)S(1)}, u32[]{:S(2)}, u32[]{:S(2)}) collective-permute-start(f16[528,512]{1,0:T(8,128)(2,1)S(1)} %convert_element_type.13), channel_id=1, source_target_pairs={{0,128},{128,0},{1,129},{129,1},{2,130},{130,2},{3,131},{131,3},{4... | collective-permute-start | bytes 1622024 | tf_op jit(solution)/shard_map/ppermute | solution.py:21
  114.3 4.5 %collective-permute-start.24 = (bf16[3,4,3,16,512]{4,3,2,1,0:T(8,128)(2,1)S(1)}, bf16[3,4,3,16,512]{4,3,2,1,0:T(8,128)(2,1)S(1)}, u32[]{:S(2)}, u32[]{:S(2)}) collective-permute-start(bf16[3,4,3,16,512]{4,3,2,1,0:T(8,128)(2,1)S(1)} %collective-permute-done.23.refs_6_), channel_id=1, source_target_pairs={{0,1},{1,0},{2,3},{3,2},{4,5},{5,4},{6,7},{7,6},{8,9},{9,8},{10,11... | collective-permute-start | bytes 1769480 | tf_op jit(solution)/shard_map/ppermute | solution.py:21

commit v3 on v2

--- a/solution.py
+++ b/solution.py
@@ -62,18 +62,18 @@
     )(place, acts)
 
 
-def square_sum(seqs, table, swapped, last, core, *refs):
-    acts, refs = refs[:4], refs[4:]
+def square_sum(seqs, table, swapped, last, sources, more, core, *refs):
+    acts, refs = refs[: len(sources)], refs[len(sources) :]
     if last:
         grads, (before, *_, out, total, turned, sem) = refs[:3], refs[3:]
     else:
-        grads, sent, total = refs[:-2], *refs[-2:]
+        grads, sent, total = refs[:2], *refs[-2:]
     half = total.shape[1]
     if last:
         back = jnp.exp2(before[-8:, :][:1] - SCALE)
 
     def add(source, seq, first=False):
-        act = acts[source][seq]
+        act = acts[sources.index(source)][seq]
         there = SWAP[source] if swapped else source
         rows = [grads[at][(*index, there, seq)] for at, index in table]
         grad = jnp.concatenate(rows, axis=0)
@@ -88,16 +88,17 @@
                 total[at] += part * part
             elif last:
                 total[at] = before[: total.shape[0], at[1]] * back[:, at[1]] + part * part
+            elif more == "after":
+                total[at] = refs[2][at] + part * part
             else:
                 total[at] = part * part
 
-    add(0, 0, first=True)
-    for source in range(1, 4):
-        add(source, 0)
+    for source in sources:
+        add(source, 0, first=source == sources[0])
 
     @pl.loop(1, SEQS_DP)
     def _(seq):
-        for source in range(4):
+        for source in sources:
             add(source, seq)
 
     if last:
@@ -107,6 +108,8 @@
         copy = pltpu.make_async_copy(turned, out.at[at, :], sem)
         copy.start()
         copy.wait()
+    elif more == "before":
+        sent[...] = total[...]
     else:
         peak = jnp.max(total[...], axis=(0, 1), keepdims=True)
         exponent = jnp.floor(jnp.log2(jnp.maximum(peak, jnp.float32(1e-30))))
@@ -114,10 +117,13 @@
         sent[total.shape[0] :, :] = jnp.broadcast_to(exponent, (ROWS, half))
 
 
-def add_side(seqs, core, acts, grads, table, swapped, before=None, out=None):
+def add_side(
+    seqs, core, acts, grads, table, swapped, before=None, out=None, sources=(0, 1, 2, 3), more=""
+):
+    acts = [acts[k] for k in sources]
     _, feats, tokens = acts[0].shape
     half = grads[0].shape[-1]
-    last = before is not None
+    last = before is not None and more != "after"
     total = jax.ShapeDtypeStruct((feats, half), jnp.float32)
     args = [core, *acts, *grads]
     specs = [pl.BlockSpec(memory_space=pltpu.SMEM)] + [VMEM] * (len(args) - 1)
@@ -139,17 +145,21 @@
             input_output_aliases={len(args) - 1: 0} if swapped else {},
         )
     else:
+        if more == "after":
+            args.append(before)
+            specs.append(VMEM)
+        rows = feats + (0 if more == "before" else ROWS)
         result = dict(
-            out_shape=jax.ShapeDtypeStruct((feats + ROWS, half), jnp.float32),
+            out_shape=jax.ShapeDtypeStruct((rows, half), jnp.float32),
             out_specs=VMEM,
             scratch_shapes=[pltpu.VMEM(total.shape, jnp.float32)],
         )
     return pl.pallas_call(
-        functools.partial(square_sum, seqs, table, swapped, last),
+        functools.partial(square_sum, seqs, table, swapped, last, sources, more),
         in_specs=specs,
         compiler_params=pltpu.CompilerParams(vmem_limit_bytes=6 * 2**20),
         cost_estimate=pl.CostEstimate(
-            flops=2 * 12 * tokens * half * feats,
+            flops=2 * 3 * len(sources) * tokens * half * feats,
             bytes_accessed=8 * 2**20,
             transcendentals=0,
         ),
@@ -157,7 +167,7 @@
     )(*args)
 
 
-def to_owner(grads, core, zlo, sources):
+def to_owner(grads, core, zlo):
     seq_dev, rows, width = grads.shape
     block = grads.reshape(seq_dev, rows, 2, 4, 2, width // 16).transpose(4, 3, 2, 0, 1, 5)
     mine = lax.dynamic_index_in_dim(block, core, 0, keepdims=False)
@@ -166,13 +176,15 @@
     low = jnp.where(core == 0, mine, other)
     high = jnp.where(core == 0, other, mine)
     both = jnp.concatenate([low, high], axis=3)
-    both = lax.all_to_all(both, "x", 0, 0, tiled=True)
-
-    def part(s, z):
-        start = (s, z, 0, 0, 0)
-        return lax.dynamic_slice(both, start, (1, 1, *both.shape[2:])).reshape(both.shape[2:])
-
-    return jnp.stack([jnp.stack([part(s, z) for s in sources]) for z in (1 - zlo, zlo)])
+    x = lax.axis_index("x")
+    way = 1 - 2 * core
+
+    def piece(by):
+        return lax.dynamic_index_in_dim(both, (x + by) % 4, 0, keepdims=False)
+
+    parts = [piece(0), send(piece(way), "x", 1), send(piece(-way), "x", -1)]
+    parts = jnp.stack([*parts, send(piece(2), "x", 2)])
+    return jnp.stack([lax.dynamic_index_in_dim(parts, z, 1, keepdims=False) for z in (1 - zlo, zlo)])
 
 
 def cross_zlo(total):
@@ -191,8 +203,7 @@
     place = jnp.stack(place).astype(jnp.int32)
     which = jnp.reshape(core, (1,)).astype(jnp.int32)
 
-    x = lax.axis_index("x")
-    g = to_owner(out_grads, core, zlo, [(x + by) % 4 for by in offsets])
+    g = to_owner(out_grads, core, zlo)
     acts = turn(place, activations)
     g, acts = level((g, acts))
 
@@ -223,22 +234,28 @@
         [jnp.concatenate([g[:1], r1]), w1p, jnp.concatenate([own_q[:1], y1q])]
     )
     some1_t = swap(some1, "core")
-    z2p, z2q, z2f, own_p, own_q, own_f, some1_t, y1f, af = level(
-        (z2p, z2q, z2f, own_p, own_q, own_f, some1_t, y1f, af)
-    )
     w1f = jnp.concatenate([own_f[:1], y1f])
+
+    def whole(at, *index):
+        return [(at, (*index, dz)) for dz in range(4)]
+
+    acts = [acts, ap, aq, af]
+    table = order([whole(0, 0), whole(0, 1), whole(0, 2), whole(1)], False)
+    first = add_side(
+        seqs, which, acts, [some1, w1f], table, False, None, None, (0, 1, 2), "before"
+    )
+    z2p, z2q, z2f, own_p, own_q, some1_t, first, acts = level(
+        (z2p, z2q, z2f, own_p, own_q, some1_t, first, acts)
+    )
 
     r2 = jnp.stack([z2p, z2q, z2f])
     y2p, y2q = send(r2, "y", 1), send(r2, "y", -1)
     some2 = jnp.stack([w1f, jnp.concatenate([g[1:], r2])])
     some2_t = swap(some2, "core")
 
-    def whole(at, *index):
-        return [(at, (*index, dz)) for dz in range(4)]
-
-    acts = [acts, ap, aq, af]
-    table = order([whole(0, 0), whole(0, 1), whole(0, 2), whole(1)], False)
-    first = add_side(seqs, which, acts, [some1, w1f], table, False)
+    first = add_side(
+        seqs, which, acts, [some1, w1f], table, False, first, None, (3,), "after"
+    )
     first = cross_zlo(first)
     table = order([whole(0, 0), whole(0, 1), whole(0, 2), whole(1, 0)], True)
     second = add_side(seqs, which, acts, [some1_t, some2_t], table, True)
@@ -250,9 +267,6 @@
     second = cross_zlo(second)
     some3 = jnp.concatenate([own_p[1:], y2p, own_q[1:], y2q, own_f[1:]])
     some3_t = swap(some3, "core")
-    second, y2f_tied = level((second, y2f))
-    y2f_t = swap(y2f_tied, "core")
-
     def last_blocks():
         below = [(1, (dz,)) for dz in range(4)]
         above = [(1, (4 + dz,)) for dz in range(4)]
@@ -261,6 +275,8 @@
     table = order(last_blocks(), False)
     grads = [some2, some3, y2f]
     out = add_side(seqs, which, acts, grads, table, False, first.astype(jnp.float32))
+    second, y2f, out = level((second, y2f, out))
+    y2f_t = swap(y2f, "core")
     table = order(last_blocks(), True)
     grads = [some2_t, some3_t, y2f_t]
     return add_side(seqs, which, acts, grads, table, True, second.astype(jnp.float32), out)

time: 123 us -> 116 us (0.943)
  waiting for transfers between devices: 63.9 us -> 56 us
  starting transfers between devices: 40.4 us -> 41.7 us
    ppermute x7, waiting for transfers between devices: 26.4 us -> 16.2 us  [swap(): return lax.ppermute(value, axis, [(0, 1), (1, 0)])]
    ppermute x18 -> x21, waiting for transfers between devices: 31 us -> 39.9 us  [send(): return lax.ppermute(value, (axis, 'core'), pairs)]
    all_to_all x1 -> x0, waiting for transfers between devices: 6.51 us -> none  [to_owner(): both = lax.all_to_all(both, 'x', 0, 0, tiled=True)]
    ppermute x18 -> x21, starting transfers between devices: 28.6 us -> 34.7 us  [send(): return lax.ppermute(value, (axis, 'core'), pairs)]
    all_to_all x1 -> x0, starting transfers between devices: 3.46 us -> none  [to_owner(): both = lax.all_to_all(both, 'x', 0, 0, tiled=True)]
    ppermute x7, starting transfers between devices: 8.42 us -> 7.05 us  [swap(): return lax.ppermute(value, axis, [(0, 1), (1, 0)])]
    pallas_call x4 -> x5, Pallas kernels: 12.9 us -> 13.2 us  [add_side(): pl.pallas_call(functools.partial(square_sum, seqs, table, swapped, last,...]
  transfers between devices with their start and end apart: 26 -> 28, of which waited for: 12 -> 15; matrix products, arithmetic and copies ran while one was open for 1% -> 1% of each run, Pallas kernels for 8% -> 9%
where the time goes in v3:
time: 116 us; the launch traced here: 115 us
  waiting for transfers between devices  56 us (48%)
  starting transfers between devices  41.7 us (36%)
  Pallas kernels  14.2 us (12%)
  other arithmetic  1.59 us (1%)
  local copies, waits for them, and re-layouts  1.5 us (1%)
    ppermute x21, waiting for transfers between devices, send(): return lax.ppermute(value, (axis, 'core'), pairs)  39.9 us
    ppermute x21, starting transfers between devices, send(): return lax.ppermute(value, (axis, 'core'), pairs)  34.7 us
    ppermute x7, waiting for transfers between devices, swap(): return lax.ppermute(value, axis, [(0, 1), (1, 0)])  16.2 us
    pallas_call x5, Pallas kernels, add_side(): pl.pallas_call(functools.partial(square_sum, seqs, table, swapped, last,...  13.2 us
    ppermute x7, starting transfers between devices, swap(): return lax.ppermute(value, axis, [(0, 1), (1, 0)])  7.05 us
  transfers between devices with their start and end apart: 28, of which 15 were waited for; matrix products, arithmetic and copies ran while one was open for 1% of the time, Pallas kernels for 9%

profile of v3, /device:TPU:1, one launch (start us, length us, event | category | flops | bytes accessed | tf_op | source)
XLA Modules:
  0.0 115.5 jit_solution(14812589479844597296)
XLA Ops:
  1.1 3.3 %collective-permute-start = (bf16[4,2,3,8,512]{4,3,2,0,1:T(8,128)(2,1)S(1)}, bf16[4,2,3,8,512]{4,3,2,0,1:T(8,128)(2,1)S(1)}, u32[]{:S(2)}, u32[]{:S(2)}) collective-permute-start(bf16[4,2,3,8,512]{4,3,2,0,1:T(8,128)(2,1)S(1)} %bitcast.74), channel_id=1, source_target_pairs={{0,1},{1,0},{2,3},{3,2},{4,5},{5,4},{6,7},{7,6},{8,9},{9,8},{10,11... | collective-permute-start | bytes 589832 | tf_op jit(solution)/shard_map/ppermute | solution.py:21
  9.6 3.8 %collective-permute-done.2 = bf16[2,3,16,512]{3,2,1,0:T(8,128)(2,1)S(1)} collective-permute-done((bf16[2,3,16,512]{3,2,1,0:T(8,128)(2,1)S(1)}, bf16[2,3,16,512]{3,2,1,0:T(8,128)(2,1)S(1)}, u32[]{:S(2)}, u32[]{:S(2)}) %collective-permute-start.2) | collective-permute-done | bytes 98336 | tf_op jit(solution)/shard_map/ppermute | solution.py:30
  13.6 1.8 %collective-permute-start.8 = (bf16[3,512,256]{2,1,0:T(8,128)(2,1)S(1)}, bf16[3,512,256]{2,1,0:T(8,128)(2,1)S(1)}, u32[]{:S(2)}, u32[]{:S(2)}) collective-permute-start(bf16[3,512,256]{2,1,0:T(8,128)(2,1)S(1)} %shard_map.28.refs_0_), channel_id=1, source_target_pairs={{0,32},{1,97},{32,64},{33,1},{64,96},{65,33},{96,0},{97,65},{2,34}... | collective-permute-start | bytes 2359304 | tf_op jit(solution)/shard_map/ppermute | solution.py:30
  15.4 1.4 %collective-permute-start.7 = (bf16[2,4,3,16,512]{4,3,2,1,0:T(8,128)(2,1)S(1)}, bf16[2,4,3,16,512]{4,3,2,1,0:T(8,128)(2,1)S(1)}, u32[]{:S(2)}, u32[]{:S(2)}) collective-permute-start(bf16[2,4,3,16,512]{4,3,2,1,0:T(8,128)(2,1)S(1)} %pad_maximum_fusion.6), channel_id=1, source_target_pairs={{0,24},{1,9},{8,0},{9,17},{16,8},{17,25},{24,16},{25,1},{2,26},{3,... | collective-permute-start | bytes 1179656 | tf_op jit(solution)/shard_map/ppermute | solution.py:30
  16.8 1.4 %collective-permute-start.6 = (bf16[2,4,3,16,512]{4,3,2,1,0:T(8,128)(2,1)S(1)}, bf16[2,4,3,16,512]{4,3,2,1,0:T(8,128)(2,1)S(1)}, u32[]{:S(2)}, u32[]{:S(2)}) collective-permute-start(bf16[2,4,3,16,512]{4,3,2,1,0:T(8,128)(2,1)S(1)} %pad_maximum_fusion.6), channel_id=1, source_target_pairs={{0,8},{1,25},{8,16},{9,1},{16,24},{17,9},{24,0},{25,17},{2,10},{3,... | collective-permute-start | bytes 1179656 | tf_op jit(solution)/shard_map/ppermute | solution.py:30
  18.2 3.1 %collective-permute-start.5 = (bf16[4,3,16,512]{3,2,1,0:T(8,128)(2,1)S(1)}, bf16[4,3,16,512]{3,2,1,0:T(8,128)(2,1)S(1)}, u32[]{:S(2)}, u32[]{:S(2)}) collective-permute-start(bf16[4,3,16,512]{3,2,1,0:T(8,128)(2,1)S(1)} %slice_bitcast_fusion), channel_id=1, source_target_pairs={{0,6},{1,3},{2,0},{3,5},{4,2},{5,7},{6,4},{7,1},{8,14},{9,11},{10,... | collective-permute-start | bytes 589832 | tf_op jit(solution)/shard_map/ppermute | solution.py:30
  21.3 3.1 %collective-permute-start.4 = (bf16[4,3,16,512]{3,2,1,0:T(8,128)(2,1)S(1)}, bf16[4,3,16,512]{3,2,1,0:T(8,128)(2,1)S(1)}, u32[]{:S(2)}, u32[]{:S(2)}) collective-permute-start(bf16[4,3,16,512]{3,2,1,0:T(8,128)(2,1)S(1)} %slice_bitcast_fusion), channel_id=1, source_target_pairs={{0,2},{1,7},{2,4},{3,1},{4,6},{5,3},{6,0},{7,5},{8,10},{9,15},{10,... | collective-permute-start | bytes 589832 | tf_op jit(solution)/shard_map/ppermute | solution.py:30
  24.4 3.6 %collective-permute-done.5 = bf16[4,3,16,512]{3,2,1,0:T(8,128)(2,1)S(1)} collective-permute-done((bf16[4,3,16,512]{3,2,1,0:T(8,128)(2,1)S(1)}, bf16[4,3,16,512]{3,2,1,0:T(8,128)(2,1)S(1)}, u32[]{:S(2)}, u32[]{:S(2)}) %collective-permute-start.5) | collective-permute-done | bytes 196640 | tf_op jit(solution)/shard_map/ppermute | solution.py:30
  28.0 5.1 %collective-permute-done.4 = bf16[4,3,16,512]{3,2,1,0:T(8,128)(2,1)S(1)} collective-permute-done((bf16[4,3,16,512]{3,2,1,0:T(8,128)(2,1)S(1)}, bf16[4,3,16,512]{3,2,1,0:T(8,128)(2,1)S(1)}, u32[]{:S(2)}, u32[]{:S(2)}) %collective-permute-start.4) | collective-permute-done | bytes 196640 | tf_op jit(solution)/shard_map/ppermute | solution.py:30
  34.0 4.7 %collective-permute-start.9 = (bf16[4,3,16,512]{3,2,1,0:T(8,128)(2,1)S(1)}, bf16[4,3,16,512]{3,2,1,0:T(8,128)(2,1)S(1)}, u32[]{:S(2)}, u32[]{:S(2)}) collective-permute-start(bf16[4,3,16,512]{3,2,1,0:T(8,128)(2,1)S(1)} %collective-permute-done.4), channel_id=1, source_target_pairs={{0,2},{1,7},{2,4},{3,1},{4,6},{5,3},{6,0},{7,5},{8,10},{9,15},{10,... | collective-permute-start | bytes 589832 | tf_op jit(solution)/shard_map/ppermute | solution.py:30
  38.6 3.8 %collective-permute-done.9 = bf16[4,3,16,512]{3,2,1,0:T(8,128)(2,1)S(1)} collective-permute-done((bf16[4,3,16,512]{3,2,1,0:T(8,128)(2,1)S(1)}, bf16[4,3,16,512]{3,2,1,0:T(8,128)(2,1)S(1)}, u32[]{:S(2)}, u32[]{:S(2)}) %collective-permute-start.9) | collective-permute-done | bytes 196640 | tf_op jit(solution)/shard_map/ppermute | solution.py:30
  42.5 1.3 %collective-permute-start.12 = (bf16[3,4,3,16,512]{4,3,2,1,0:T(8,128)(2,1)S(1)}, bf16[3,4,3,16,512]{4,3,2,1,0:T(8,128)(2,1)S(1)}, u32[]{:S(2)}, u32[]{:S(2)}) collective-permute-start(bf16[3,4,3,16,512]{4,3,2,1,0:T(8,128)(2,1)S(1)} %pad_maximum_fusion.3), channel_id=1, source_target_pairs={{0,24},{1,9},{8,0},{9,17},{16,8},{17,25},{24,16},{25,1},{2,26},{3,... | collective-permute-start | bytes 1769480 | tf_op jit(solution)/shard_map/ppermute | solution.py:30
  43.8 1.5 %collective-permute-start.11 = (bf16[3,4,3,16,512]{4,3,2,1,0:T(8,128)(2,1)S(1)}, bf16[3,4,3,16,512]{4,3,2,1,0:T(8,128)(2,1)S(1)}, u32[]{:S(2)}, u32[]{:S(2)}) collective-permute-start(bf16[3,4,3,16,512]{4,3,2,1,0:T(8,128)(2,1)S(1)} %pad_maximum_fusion.3), channel_id=1, source_target_pairs={{0,8},{1,25},{8,16},{9,1},{16,24},{17,9},{24,0},{25,17},{2,10},{3,... | collective-permute-start | bytes 1769480 | tf_op jit(solution)/shard_map/ppermute | solution.py:30
  45.3 3.3 %collective-permute-start.14 = (bf16[4,3,16,512]{3,2,1,0:T(8,128)(2,1)S(1)}, bf16[4,3,16,512]{3,2,1,0:T(8,128)(2,1)S(1)}, u32[]{:S(2)}, u32[]{:S(2)}) collective-permute-start(bf16[4,3,16,512]{3,2,1,0:T(8,128)(2,1)S(1)} %get-tuple-element.100), channel_id=1, source_target_pairs={{0,6},{1,3},{2,0},{3,5},{4,2},{5,7},{6,4},{7,1},{8,14},{9,11},{10,... | collective-permute-start | bytes 589832 | tf_op jit(solution)/shard_map/ppermute | solution.py:30
  48.9 8.2 %collective-permute-done.14 = bf16[4,3,16,512]{3,2,1,0:T(8,128)(2,1)S(1)} collective-permute-done((bf16[4,3,16,512]{3,2,1,0:T(8,128)(2,1)S(1)}, bf16[4,3,16,512]{3,2,1,0:T(8,128)(2,1)S(1)}, u32[]{:S(2)}, u32[]{:S(2)}) %collective-permute-start.14) | collective-permute-done | bytes 196640 | tf_op jit(solution)/shard_map/ppermute | solution.py:30
  57.2 1.3 %collective-permute-done.13 = bf16[4,3,16,512]{3,2,1,0:T(8,128)(2,1)S(1)} collective-permute-done((bf16[4,3,16,512]{3,2,1,0:T(8,128)(2,1)S(1)}, bf16[4,3,16,512]{3,2,1,0:T(8,128)(2,1)S(1)}, u32[]{:S(2)}, u32[]{:S(2)}) %collective-permute-start.13) | collective-permute-done | bytes 196640 | tf_op jit(solution)/shard_map/ppermute | solution.py:30
  59.0 1.1 collective-permute-start.17
  60.1 2.7 %collective-permute-start.18 = (bf16[3,4,3,16,512]{4,3,2,1,0:T(8,128)(2,1)S(1)}, bf16[3,4,3,16,512]{4,3,2,1,0:T(8,128)(2,1)S(1)}, u32[]{:S(2)}, u32[]{:S(2)}) collective-permute-start(bf16[3,4,3,16,512]{4,3,2,1,0:T(8,128)(2,1)S(1)} %collective-permute-done.11), channel_id=1, source_target_pairs={{0,8},{1,25},{8,16},{9,1},{16,24},{17,9},{24,0},{25,17},{2,10},{3,... | collective-permute-start | bytes 1769480 | tf_op jit(solution)/shard_map/ppermute | solution.py:30
  62.8 3.0 %collective-permute-start.19 = (bf16[3,512,256]{2,1,0:T(8,128)(2,1)S(1)}, bf16[3,512,256]{2,1,0:T(8,128)(2,1)S(1)}, u32[]{:S(2)}, u32[]{:S(2)}) collective-permute-start(bf16[3,512,256]{2,1,0:T(8,128)(2,1)S(1)} %collective-permute-done.8.refs_1_), channel_id=1, source_target_pairs={{0,32},{1,97},{32,64},{33,1},{64,96},{65,33},{96,0},{97,65},{2,34}... | collective-permute-start | bytes 2359304 | tf_op jit(solution)/shard_map/ppermute | solution.py:30
  66.3 3.3 %collective-permute-done.18 = bf16[3,4,3,16,512]{4,3,2,1,0:T(8,128)(2,1)S(1)} collective-permute-done((bf16[3,4,3,16,512]{4,3,2,1,0:T(8,128)(2,1)S(1)}, bf16[3,4,3,16,512]{4,3,2,1,0:T(8,128)(2,1)S(1)}, u32[]{:S(2)}, u32[]{:S(2)}) %collective-permute-start.18) | collective-permute-done | bytes 589856 | tf_op jit(solution)/shard_map/ppermute | solution.py:30
  69.7 1.8 %shard_map.29.refs_3_ = f32[512,512]{1,0:T(8,128)S(1)} custom-call(s32[1]{0:T(128)} %bitcast.core, bf16[3,512,256]{2,1,0:T(8,128)(2,1)S(1)} %shard_map.28.refs_0_, bf16[3,512,256]{2,1,0:T(8,128)(2,1)S(1)} %collective-permute-done.8.refs_1_, bf16[3,512,256]{2,1,0:T(8,128)(2,1)S(1)} %collective-permute-done.15.refs_2_, ...), custom_call_target="tpu_custom_call" | custom-call | flops 1207959552 | bytes 8388608 | tf_op jit(solution)/shard_map/pallas_call | solution.py:157
  71.5 1.1 collective-permute-done.16
  72.7 2.0 %collective-permute-done.19.refs_0_.refs_3_ = bf16[3,512,256]{2,1,0:T(8,128)(2,1)S(1)} collective-permute-done((bf16[3,512,256]{2,1,0:T(8,128)(2,1)S(1)}, bf16[3,512,256]{2,1,0:T(8,128)(2,1)S(1)}, u32[]{:S(2)}, u32[]{:S(2)}) %collective-permute-start.19) | collective-permute-done | bytes 786464 | tf_op jit(solution)/shard_map/ppermute | solution.py:30
  75.9 2.0 %collective-permute-start.22 = (bf16[3,4,3,16,512]{4,3,2,1,0:T(8,128)(2,1)S(1)}, bf16[3,4,3,16,512]{4,3,2,1,0:T(8,128)(2,1)S(1)}, u32[]{:S(2)}, u32[]{:S(2)}) collective-permute-start(bf16[3,4,3,16,512]{4,3,2,1,0:T(8,128)(2,1)S(1)} %pad_maximum_fusion.4), channel_id=1, source_target_pairs={{0,8},{1,25},{8,16},{9,1},{16,24},{17,9},{24,0},{25,17},{2,10},{3,... | collective-permute-start | bytes 1769480 | tf_op jit(solution)/shard_map/ppermute | solution.py:30
  77.9 1.4 %shard_map.30 = f32[528,512]{1,0:T(8,128)S(1)} custom-call(s32[1]{0:T(128)} %bitcast.core, bf16[3,512,256]{2,1,0:T(8,128)(2,1)S(1)} %collective-permute-done.19.refs_0_.refs_3_, bf16[3,4,4,3,16,512]{5,4,3,2,1,0:T(8,128)(2,1)S(1)} %pad_maximum_fusion.refs_3_.refs_1_, bf16[4,4,3,16,512]{4,3,2,1,0:T(8,128)(2,1)S(1)} %get-tuple-element.98.refs_4_.refs_2_, ...), custom_call_target="tpu_custom_call" | custom-call | flops 402653184 | bytes 8388608 | tf_op jit(solution)/shard_map/pallas_call | solution.py:157
  79.5 2.8 %shard_map.31 = f32[528,512]{1,0:T(8,128)S(1)} custom-call(s32[1]{0:T(128)} %bitcast.core, bf16[3,512,256]{2,1,0:T(8,128)(2,1)S(1)} %shard_map.28.refs_0_, bf16[3,512,256]{2,1,0:T(8,128)(2,1)S(1)} %collective-permute-done.8.refs_1_, bf16[3,512,256]{2,1,0:T(8,128)(2,1)S(1)} %collective-permute-done.15.refs_2_, ...), custom_call_target="tpu_custom_call" | custom-call | flops 1610612736 | bytes 8388608 | tf_op jit(solution)/shard_map/pallas_call | solution.py:157
  82.3 11.2 %collective-permute-done.21 = f16[528,512]{1,0:T(8,128)(2,1)S(1)} collective-permute-done((f16[528,512]{1,0:T(8,128)(2,1)S(1)}, f16[528,512]{1,0:T(8,128)(2,1)S(1)}, u32[]{:S(2)}, u32[]{:S(2)}) %collective-permute-start.21) | collective-permute-done | bytes 540704 | tf_op jit(solution)/shard_map/ppermute | solution.py:21
  96.3 7.2 %collective-permute-done.26.refs_6_ = bf16[3,4,3,16,512]{4,3,2,1,0:T(8,128)(2,1)S(1)} collective-permute-done((bf16[3,4,3,16,512]{4,3,2,1,0:T(8,128)(2,1)S(1)}, bf16[3,4,3,16,512]{4,3,2,1,0:T(8,128)(2,1)S(1)}, u32[]{:S(2)}, u32[]{:S(2)}) %collective-permute-start.26) | collective-permute-done | bytes 589856 | tf_op jit(solution)/shard_map/ppermute | solution.py:30
  103.4 3.6 %shard_map.32.refs_8_ = f32[1024,512]{1,0:T(8,128)} custom-call(s32[1]{0:T(128)} %bitcast.core, bf16[3,512,256]{2,1,0:T(8,128)(2,1)S(1)} %shard_map.28.refs_0_, bf16[3,512,256]{2,1,0:T(8,128)(2,1)S(1)} %collective-permute-done.8.refs_1_, bf16[3,512,256]{2,1,0:T(8,128)(2,1)S(1)} %collective-permute-done.15.refs_2_, ...), custom_call_target="tpu_custom_call" | custom-call | flops 1610612736 | bytes 8388608 | tf_op jit(solution)/shard_map/pallas_call | solution.py:157
  107.1 2.4 %collective-permute-done.25 = f16[528,512]{1,0:T(8,128)(2,1)S(1)} collective-permute-done((f16[528,512]{1,0:T(8,128)(2,1)S(1)}, f16[528,512]{1,0:T(8,128)(2,1)S(1)}, u32[]{:S(2)}, u32[]{:S(2)}) %collective-permute-start.25) | collective-permute-done | bytes 540704 | tf_op jit(solution)/shard_map/ppermute | solution.py:21
  110.2 1.5 %collective-permute-done.27.refs_6_ = bf16[3,4,3,16,512]{4,3,2,1,0:T(8,128)(2,1)S(1)} collective-permute-done((bf16[3,4,3,16,512]{4,3,2,1,0:T(8,128)(2,1)S(1)}, bf16[3,4,3,16,512]{4,3,2,1,0:T(8,128)(2,1)S(1)}, u32[]{:S(2)}, u32[]{:S(2)}) %collective-permute-start.27) | collective-permute-done | bytes 589856 | tf_op jit(solution)/shard_map/ppermute | solution.py:21
  111.7 3.6 %shard_map.33 = f32[1024,512]{1,0:T(8,128)} custom-call(s32[1]{0:T(128)} %bitcast.core, bf16[3,512,256]{2,1,0:T(8,128)(2,1)S(1)} %shard_map.28.refs_0_, bf16[3,512,256]{2,1,0:T(8,128)(2,1)S(1)} %collective-permute-done.8.refs_1_, bf16[3,512,256]{2,1,0:T(8,128)(2,1)S(1)} %collective-permute-done.15.refs_2_, ...), custom_call_target="tpu_custom_call", output_to_operand_aliasing={{}: (9, {})} | custom-call | flops 1610612736 | bytes 8388608 | tf_op jit(solution)/shard_map/pallas_call | solution.py:157
  (62 shorter events, 13.6 us)
Async XLA Ops:
  0.0 8.3 %copy-start = (bf16[3,256,512]{2,1,0:T(8,128)(2,1)S(1)}, bf16[3,256,512]{2,1,0:T(8,128)(2,1)}, u32[]{:S(2)}) copy-start(bf16[3,256,512]{2,1,0:T(8,128)(2,1)} %acts.1) | copy-start | bytes 2359300
  1.1 4.4 %collective-permute-start = (bf16[4,2,3,8,512]{4,3,2,0,1:T(8,128)(2,1)S(1)}, bf16[4,2,3,8,512]{4,3,2,0,1:T(8,128)(2,1)S(1)}, u32[]{:S(2)}, u32[]{:S(2)}) collective-permute-start(bf16[4,2,3,8,512]{4,3,2,0,1:T(8,128)(2,1)S(1)} %bitcast.74), channel_id=1, source_target_pairs={{0,1},{1,0},{2,3},{3,2},{4,5},{5,4},{6,7},{7,6},{8,9},{9,8},{10,11... | collective-permute-start | bytes 589832 | tf_op jit(solution)/shard_map/ppermute | solution.py:21
  5.6 4.0 %collective-permute-start.1 = (bf16[2,3,16,512]{3,2,1,0:T(8,128)(2,1)S(1)}, bf16[2,3,16,512]{3,2,1,0:T(8,128)(2,1)S(1)}, u32[]{:S(2)}, u32[]{:S(2)}) collective-permute-start(bf16[2,3,16,512]{3,2,1,0:T(8,128)(2,1)S(1)} %get-tuple-element.105), channel_id=1, source_target_pairs={{0,32},{1,97},{32,64},{33,1},{64,96},{65,33},{96,0},{97,65},{2,34}... | collective-permute-start | bytes 294920 | tf_op jit(solution)/shard_map/ppermute | solution.py:30
  6.5 7.0 %collective-permute-start.2 = (bf16[2,3,16,512]{3,2,1,0:T(8,128)(2,1)S(1)}, bf16[2,3,16,512]{3,2,1,0:T(8,128)(2,1)S(1)}, u32[]{:S(2)}, u32[]{:S(2)}) collective-permute-start(bf16[2,3,16,512]{3,2,1,0:T(8,128)(2,1)S(1)} %get-tuple-element.106), channel_id=1, source_target_pairs={{0,96},{1,33},{32,0},{33,65},{64,32},{65,97},{96,64},{97,1},{2,98}... | collective-permute-start | bytes 294920 | tf_op jit(solution)/shard_map/ppermute | solution.py:30
  7.2 6.3 %collective-permute-start.3 = (bf16[2,3,16,512]{3,2,1,0:T(8,128)(2,1)S(1)}, bf16[2,3,16,512]{3,2,1,0:T(8,128)(2,1)S(1)}, u32[]{:S(2)}, u32[]{:S(2)}) collective-permute-start(bf16[2,3,16,512]{3,2,1,0:T(8,128)(2,1)S(1)} %get-tuple-element.107), channel_id=1, source_target_pairs={{0,64},{1,65},{32,96},{33,97},{64,0},{65,1},{96,32},{97,33},{2,66}... | collective-permute-start | bytes 294920 | tf_op jit(solution)/shard_map/ppermute | solution.py:30
  13.6 19.6 %collective-permute-start.8 = (bf16[3,512,256]{2,1,0:T(8,128)(2,1)S(1)}, bf16[3,512,256]{2,1,0:T(8,128)(2,1)S(1)}, u32[]{:S(2)}, u32[]{:S(2)}) collective-permute-start(bf16[3,512,256]{2,1,0:T(8,128)(2,1)S(1)} %shard_map.28.refs_0_), channel_id=1, source_target_pairs={{0,32},{1,97},{32,64},{33,1},{64,96},{65,33},{96,0},{97,65},{2,34}... | collective-permute-start | bytes 2359304 | tf_op jit(solution)/shard_map/ppermute | solution.py:30
  15.4 17.7 %collective-permute-start.7 = (bf16[2,4,3,16,512]{4,3,2,1,0:T(8,128)(2,1)S(1)}, bf16[2,4,3,16,512]{4,3,2,1,0:T(8,128)(2,1)S(1)}, u32[]{:S(2)}, u32[]{:S(2)}) collective-permute-start(bf16[2,4,3,16,512]{4,3,2,1,0:T(8,128)(2,1)S(1)} %pad_maximum_fusion.6), channel_id=1, source_target_pairs={{0,24},{1,9},{8,0},{9,17},{16,8},{17,25},{24,16},{25,1},{2,26},{3,... | collective-permute-start | bytes 1179656 | tf_op jit(solution)/shard_map/ppermute | solution.py:30
  16.8 16.4 %collective-permute-start.6 = (bf16[2,4,3,16,512]{4,3,2,1,0:T(8,128)(2,1)S(1)}, bf16[2,4,3,16,512]{4,3,2,1,0:T(8,128)(2,1)S(1)}, u32[]{:S(2)}, u32[]{:S(2)}) collective-permute-start(bf16[2,4,3,16,512]{4,3,2,1,0:T(8,128)(2,1)S(1)} %pad_maximum_fusion.6), channel_id=1, source_target_pairs={{0,8},{1,25},{8,16},{9,1},{16,24},{17,9},{24,0},{25,17},{2,10},{3,... | collective-permute-start | bytes 1179656 | tf_op jit(solution)/shard_map/ppermute | solution.py:30
  18.2 9.8 %collective-permute-start.5 = (bf16[4,3,16,512]{3,2,1,0:T(8,128)(2,1)S(1)}, bf16[4,3,16,512]{3,2,1,0:T(8,128)(2,1)S(1)}, u32[]{:S(2)}, u32[]{:S(2)}) collective-permute-start(bf16[4,3,16,512]{3,2,1,0:T(8,128)(2,1)S(1)} %slice_bitcast_fusion), channel_id=1, source_target_pairs={{0,6},{1,3},{2,0},{3,5},{4,2},{5,7},{6,4},{7,1},{8,14},{9,11},{10,... | collective-permute-start | bytes 589832 | tf_op jit(solution)/shard_map/ppermute | solution.py:30
  21.3 11.8 %collective-permute-start.4 = (bf16[4,3,16,512]{3,2,1,0:T(8,128)(2,1)S(1)}, bf16[4,3,16,512]{3,2,1,0:T(8,128)(2,1)S(1)}, u32[]{:S(2)}, u32[]{:S(2)}) collective-permute-start(bf16[4,3,16,512]{3,2,1,0:T(8,128)(2,1)S(1)} %slice_bitcast_fusion), channel_id=1, source_target_pairs={{0,2},{1,7},{2,4},{3,1},{4,6},{5,3},{6,0},{7,5},{8,10},{9,15},{10,... | collective-permute-start | bytes 589832 | tf_op jit(solution)/shard_map/ppermute | solution.py:30
  33.2 9.2 %collective-permute-start.10 = (bf16[2,4,3,16,512]{4,3,2,1,0:T(8,128)(2,1)S(1)}, bf16[2,4,3,16,512]{4,3,2,1,0:T(8,128)(2,1)S(1)}, u32[]{:S(2)}, u32[]{:S(2)}) collective-permute-start(bf16[2,4,3,16,512]{4,3,2,1,0:T(8,128)(2,1)S(1)} %collective-permute-done.6), channel_id=1, source_target_pairs={{0,8},{1,25},{8,16},{9,1},{16,24},{17,9},{24,0},{25,17},{2,10},{3,... | collective-permute-start | bytes 1179656 | tf_op jit(solution)/shard_map/ppermute | solution.py:30
  34.0 8.4 %collective-permute-start.9 = (bf16[4,3,16,512]{3,2,1,0:T(8,128)(2,1)S(1)}, bf16[4,3,16,512]{3,2,1,0:T(8,128)(2,1)S(1)}, u32[]{:S(2)}, u32[]{:S(2)}) collective-permute-start(bf16[4,3,16,512]{3,2,1,0:T(8,128)(2,1)S(1)} %collective-permute-done.4), channel_id=1, source_target_pairs={{0,2},{1,7},{2,4},{3,1},{4,6},{5,3},{6,0},{7,5},{8,10},{9,15},{10,... | collective-permute-start | bytes 589832 | tf_op jit(solution)/shard_map/ppermute | solution.py:30
  38.6 19.8 %collective-permute-start.15 = (bf16[3,512,256]{2,1,0:T(8,128)(2,1)S(1)}, bf16[3,512,256]{2,1,0:T(8,128)(2,1)S(1)}, u32[]{:S(2)}, u32[]{:S(2)}) collective-permute-start(bf16[3,512,256]{2,1,0:T(8,128)(2,1)S(1)} %shard_map.28.refs_0_), channel_id=1, source_target_pairs={{0,96},{1,33},{32,0},{33,65},{64,32},{65,97},{96,64},{97,1},{2,98}... | collective-permute-start | bytes 2359304 | tf_op jit(solution)/shard_map/ppermute | solution.py:30
  42.5 16.0 %collective-permute-start.12 = (bf16[3,4,3,16,512]{4,3,2,1,0:T(8,128)(2,1)S(1)}, bf16[3,4,3,16,512]{4,3,2,1,0:T(8,128)(2,1)S(1)}, u32[]{:S(2)}, u32[]{:S(2)}) collective-permute-start(bf16[3,4,3,16,512]{4,3,2,1,0:T(8,128)(2,1)S(1)} %pad_maximum_fusion.3), channel_id=1, source_target_pairs={{0,24},{1,9},{8,0},{9,17},{16,8},{17,25},{24,16},{25,1},{2,26},{3,... | collective-permute-start | bytes 1769480 | tf_op jit(solution)/shard_map/ppermute | solution.py:30
  43.8 14.7 %collective-permute-start.11 = (bf16[3,4,3,16,512]{4,3,2,1,0:T(8,128)(2,1)S(1)}, bf16[3,4,3,16,512]{4,3,2,1,0:T(8,128)(2,1)S(1)}, u32[]{:S(2)}, u32[]{:S(2)}) collective-permute-start(bf16[3,4,3,16,512]{4,3,2,1,0:T(8,128)(2,1)S(1)} %pad_maximum_fusion.3), channel_id=1, source_target_pairs={{0,8},{1,25},{8,16},{9,1},{16,24},{17,9},{24,0},{25,17},{2,10},{3,... | collective-permute-start | bytes 1769480 | tf_op jit(solution)/shard_map/ppermute | solution.py:30
  45.3 11.9 %collective-permute-start.14 = (bf16[4,3,16,512]{3,2,1,0:T(8,128)(2,1)S(1)}, bf16[4,3,16,512]{3,2,1,0:T(8,128)(2,1)S(1)}, u32[]{:S(2)}, u32[]{:S(2)}) collective-permute-start(bf16[4,3,16,512]{3,2,1,0:T(8,128)(2,1)S(1)} %get-tuple-element.100), channel_id=1, source_target_pairs={{0,6},{1,3},{2,0},{3,5},{4,2},{5,7},{6,4},{7,1},{8,14},{9,11},{10,... | collective-permute-start | bytes 589832 | tf_op jit(solution)/shard_map/ppermute | solution.py:30
  48.6 9.9 %collective-permute-start.13 = (bf16[4,3,16,512]{3,2,1,0:T(8,128)(2,1)S(1)}, bf16[4,3,16,512]{3,2,1,0:T(8,128)(2,1)S(1)}, u32[]{:S(2)}, u32[]{:S(2)}) collective-permute-start(bf16[4,3,16,512]{3,2,1,0:T(8,128)(2,1)S(1)} %get-tuple-element.100), channel_id=1, source_target_pairs={{0,2},{1,7},{2,4},{3,1},{4,6},{5,3},{6,0},{7,5},{8,10},{9,15},{10,... | collective-permute-start | bytes 589832 | tf_op jit(solution)/shard_map/ppermute | solution.py:30
  59.0 15.7 %collective-permute-start.17 = (bf16[3,4,4,3,16,512]{5,4,3,2,1,0:T(8,128)(2,1)S(1)}, bf16[3,4,4,3,16,512]{5,4,3,2,1,0:T(8,128)(2,1)S(1)}, u32[]{:S(2)}, u32[]{:S(2)}) collective-permute-start(bf16[3,4,4,3,16,512]{5,4,3,2,1,0:T(8,128)(2,1)S(1)} %pad_maximum_fusion.refs_3_.refs_1_), channel_id=1, source_target_pairs={{0,1},{1,0},{2,3},{3,2},{4,5},{5,4},{6,7},{7,6},{8,9},{9,8},{10,11... | collective-permute-start | bytes 7077896 | tf_op jit(solution)/shard_map/ppermute | solution.py:21
  60.1 9.5 %collective-permute-start.18 = (bf16[3,4,3,16,512]{4,3,2,1,0:T(8,128)(2,1)S(1)}, bf16[3,4,3,16,512]{4,3,2,1,0:T(8,128)(2,1)S(1)}, u32[]{:S(2)}, u32[]{:S(2)}) collective-permute-start(bf16[3,4,3,16,512]{4,3,2,1,0:T(8,128)(2,1)S(1)} %collective-permute-done.11), channel_id=1, source_target_pairs={{0,8},{1,25},{8,16},{9,1},{16,24},{17,9},{24,0},{25,17},{2,10},{3,... | collective-permute-start | bytes 1769480 | tf_op jit(solution)/shard_map/ppermute | solution.py:30
  62.8 11.9 %collective-permute-start.19 = (bf16[3,512,256]{2,1,0:T(8,128)(2,1)S(1)}, bf16[3,512,256]{2,1,0:T(8,128)(2,1)S(1)}, u32[]{:S(2)}, u32[]{:S(2)}) collective-permute-start(bf16[3,512,256]{2,1,0:T(8,128)(2,1)S(1)} %collective-permute-done.8.refs_1_), channel_id=1, source_target_pairs={{0,32},{1,97},{32,64},{33,1},{64,96},{65,33},{96,0},{97,65},{2,34}... | collective-permute-start | bytes 2359304 | tf_op jit(solution)/shard_map/ppermute | solution.py:30
  65.8 6.9 %collective-permute-start.16 = (bf16[4,3,16,512]{3,2,1,0:T(8,128)(2,1)S(1)}, bf16[4,3,16,512]{3,2,1,0:T(8,128)(2,1)S(1)}, u32[]{:S(2)}, u32[]{:S(2)}) collective-permute-start(bf16[4,3,16,512]{3,2,1,0:T(8,128)(2,1)S(1)} %collective-permute-done.13), channel_id=1, source_target_pairs={{0,2},{1,7},{2,4},{3,1},{4,6},{5,3},{6,0},{7,5},{8,10},{9,15},{10,... | collective-permute-start | bytes 589832 | tf_op jit(solution)/shard_map/ppermute | solution.py:30
  75.0 4.5 %collective-permute-start.20 = (bf16[2,4,4,3,16,512]{5,4,3,2,1,0:T(8,128)(2,1)S(1)}, bf16[2,4,4,3,16,512]{5,4,3,2,1,0:T(8,128)(2,1)S(1)}, u32[]{:S(2)}, u32[]{:S(2)}) collective-permute-start(bf16[2,4,4,3,16,512]{5,4,3,2,1,0:T(8,128)(2,1)S(1)} %pad_maximum_fusion.1.refs_4_), channel_id=1, source_target_pairs={{0,1},{1,0},{2,3},{3,2},{4,5},{5,4},{6,7},{7,6},{8,9},{9,8},{10,11... | collective-permute-start | bytes 4718600 | tf_op jit(solution)/shard_map/ppermute | solution.py:21
  75.1 18.3 %collective-permute-start.23 = (bf16[3,4,3,16,512]{4,3,2,1,0:T(8,128)(2,1)S(1)}, bf16[3,4,3,16,512]{4,3,2,1,0:T(8,128)(2,1)S(1)}, u32[]{:S(2)}, u32[]{:S(2)}) collective-permute-start(bf16[3,4,3,16,512]{4,3,2,1,0:T(8,128)(2,1)S(1)} %pad_maximum_fusion.4), channel_id=1, source_target_pairs={{0,24},{1,9},{8,0},{9,17},{16,8},{17,25},{24,16},{25,1},{2,26},{3,... | collective-permute-start | bytes 1769480 | tf_op jit(solution)/shard_map/ppermute | solution.py:30
  75.9 17.5 %collective-permute-start.22 = (bf16[3,4,3,16,512]{4,3,2,1,0:T(8,128)(2,1)S(1)}, bf16[3,4,3,16,512]{4,3,2,1,0:T(8,128)(2,1)S(1)}, u32[]{:S(2)}, u32[]{:S(2)}) collective-permute-start(bf16[3,4,3,16,512]{4,3,2,1,0:T(8,128)(2,1)S(1)} %pad_maximum_fusion.4), channel_id=1, source_target_pairs={{0,8},{1,25},{8,16},{9,1},{16,24},{17,9},{24,0},{25,17},{2,10},{3,... | collective-permute-start | bytes 1769480 | tf_op jit(solution)/shard_map/ppermute | solution.py:30
  79.4 14.1 %collective-permute-start.21 = (f16[528,512]{1,0:T(8,128)(2,1)S(1)}, f16[528,512]{1,0:T(8,128)(2,1)S(1)}, u32[]{:S(2)}, u32[]{:S(2)}) collective-permute-start(f16[528,512]{1,0:T(8,128)(2,1)S(1)} %convert_element_type.12), channel_id=1, source_target_pairs={{0,128},{128,0},{1,129},{129,1},{2,130},{130,2},{3,131},{131,3},{4... | collective-permute-start | bytes 1622024 | tf_op jit(solution)/shard_map/ppermute | solution.py:21
  93.6 18.1 %collective-permute-start.24 = (bf16[9,4,3,16,512]{4,3,2,1,0:T(8,128)(2,1)S(1)}, bf16[9,4,3,16,512]{4,3,2,1,0:T(8,128)(2,1)S(1)}, u32[]{:S(2)}, u32[]{:S(2)}) collective-permute-start(bf16[9,4,3,16,512]{4,3,2,1,0:T(8,128)(2,1)S(1)} %slice_dynamic-update-slice_fusion.refs_5_), channel_id=1, source_target_pairs={{0,1},{1,0},{2,3},{3,2},{4,5},{5,4},{6,7},{7,6},{8,9},{9,8},{10,11... | collective-permute-start | bytes 5308424 | tf_op jit(solution)/shard_map/ppermute | solution.py:21
  94.4 9.0 %collective-permute-start.26 = (bf16[3,4,3,16,512]{4,3,2,1,0:T(8,128)(2,1)S(1)}, bf16[3,4,3,16,512]{4,3,2,1,0:T(8,128)(2,1)S(1)}, u32[]{:S(2)}, u32[]{:S(2)}) collective-permute-start(bf16[3,4,3,16,512]{4,3,2,1,0:T(8,128)(2,1)S(1)} %collective-permute-done.22), channel_id=1, source_target_pairs={{0,8},{1,25},{8,16},{9,1},{16,24},{17,9},{24,0},{25,17},{2,10},{3,... | collective-permute-start | bytes 1769480 | tf_op jit(solution)/shard_map/ppermute | solution.py:30
  95.1 14.4 %collective-permute-start.25 = (f16[528,512]{1,0:T(8,128)(2,1)S(1)}, f16[528,512]{1,0:T(8,128)(2,1)S(1)}, u32[]{:S(2)}, u32[]{:S(2)}) collective-permute-start(f16[528,512]{1,0:T(8,128)(2,1)S(1)} %convert_element_type.13), channel_id=1, source_target_pairs={{0,128},{128,0},{1,129},{129,1},{2,130},{130,2},{3,131},{131,3},{4... | collective-permute-start | bytes 1622024 | tf_op jit(solution)/shard_map/ppermute | solution.py:21
  109.5 2.2 %collective-permute-start.27 = (bf16[3,4,3,16,512]{4,3,2,1,0:T(8,128)(2,1)S(1)}, bf16[3,4,3,16,512]{4,3,2,1,0:T(8,128)(2,1)S(1)}, u32[]{:S(2)}, u32[]{:S(2)}) collective-permute-start(bf16[3,4,3,16,512]{4,3,2,1,0:T(8,128)(2,1)S(1)} %collective-permute-done.26.refs_6_), channel_id=1, source_target_pairs={{0,1},{1,0},{2,3},{3,2},{4,5},{5,4},{6,7},{7,6},{8,9},{9,8},{10,11... | collective-permute-start | bytes 1769480 | tf_op jit(solution)/shard_map/ppermute | solution.py:21

commit v4 on v3

--- a/solution.py
+++ b/solution.py
@@ -62,12 +62,12 @@
     )(place, acts)
 
 
-def square_sum(seqs, table, swapped, last, sources, more, core, *refs):
+def square_sum(seqs, table, swapped, last, sources, more, count, core, *refs):
     acts, refs = refs[: len(sources)], refs[len(sources) :]
     if last:
         grads, (before, *_, out, total, turned, sem) = refs[:3], refs[3:]
     else:
-        grads, sent, total = refs[:2], *refs[-2:]
+        grads, sent, total = refs[:count], *refs[-2:]
     half = total.shape[1]
     if last:
         back = jnp.exp2(before[-8:, :][:1] - SCALE)
@@ -89,7 +89,7 @@
             elif last:
                 total[at] = before[: total.shape[0], at[1]] * back[:, at[1]] + part * part
             elif more == "after":
-                total[at] = refs[2][at] + part * part
+                total[at] = refs[count][at] + part * part
             else:
                 total[at] = part * part
 
@@ -155,7 +155,7 @@
             scratch_shapes=[pltpu.VMEM(total.shape, jnp.float32)],
         )
     return pl.pallas_call(
-        functools.partial(square_sum, seqs, table, swapped, last, sources, more),
+        functools.partial(square_sum, seqs, table, swapped, last, sources, more, len(grads)),
         in_specs=specs,
         compiler_params=pltpu.CompilerParams(vmem_limit_bytes=6 * 2**20),
         cost_estimate=pl.CostEstimate(
@@ -165,6 +165,31 @@
         ),
         **result,
     )(*args)
+
+
+def finish_body(seqs, core, total, before, token, given, out, turned, sem):
+    half = total.shape[1]
+    back = jnp.exp2(before[-8:, :][:1] - SCALE)
+    whole = total[...] + before[: total.shape[0], :] * back
+    turned[...] = whole.T * jnp.float32(1 / seqs)
+    at = pl.ds(pl.multiple_of((1 - core[0]) * half, half), half)
+    copy = pltpu.make_async_copy(turned, out.at[at, :], sem)
+    copy.start()
+    copy.wait()
+
+
+def finish(seqs, core, total, before, token, out):
+    feats, half = total.shape
+    anywhere = pl.BlockSpec(memory_space=pl.ANY)
+    return pl.pallas_call(
+        functools.partial(finish_body, seqs),
+        in_specs=[pl.BlockSpec(memory_space=pltpu.SMEM), VMEM, VMEM, anywhere, anywhere],
+        out_specs=anywhere,
+        out_shape=jax.ShapeDtypeStruct(out.shape, jnp.float32),
+        scratch_shapes=[pltpu.VMEM((half, feats), jnp.float32), pltpu.SemaphoreType.DMA],
+        input_output_aliases={4: 0},
+        compiler_params=pltpu.CompilerParams(vmem_limit_bytes=6 * 2**20),
+    )(core, total, before, token, out)
 
 
 def to_owner(grads, core, zlo):
@@ -275,11 +300,14 @@
     table = order(last_blocks(), False)
     grads = [some2, some3, y2f]
     out = add_side(seqs, which, acts, grads, table, False, first.astype(jnp.float32))
-    second, y2f, out = level((second, y2f, out))
     y2f_t = swap(y2f, "core")
+    second, out = level((second, out))
+    token = swap(second[-ROWS:, :128].astype(jnp.float32), "core")
     table = order(last_blocks(), True)
     grads = [some2_t, some3_t, y2f_t]
-    return add_side(seqs, which, acts, grads, table, True, second.astype(jnp.float32), out)
+    rest = add_side(seqs, which, acts, grads, table, True, more="before")
+    second, token, rest = level((second, token, rest))
+    return finish(seqs, which, rest, second.astype(jnp.float32), token, out)
 
 
 def solution(mesh):

time: 116 us -> 114 us (0.983)
  waiting for transfers between devices: 56 us -> 50.8 us
  starting transfers between devices: 41.7 us -> 45.7 us
    ppermute x7 -> x8, waiting for transfers between devices: 16.2 us -> 11.8 us  [swap(): return lax.ppermute(value, axis, [(0, 1), (1, 0)])]
    ppermute x7 -> x8, starting transfers between devices: 7.05 us -> 9.19 us  [swap(): return lax.ppermute(value, axis, [(0, 1), (1, 0)])]
    ppermute x21, starting transfers between devices: 34.7 us -> 36.5 us  [send(): return lax.ppermute(value, (axis, 'core'), pairs)]
    pallas_call x0 -> x1, Pallas kernels: none -> 1.33 us  [finish(): pl.pallas_call(functools.partial(finish_body, seqs), in_specs=[pl.BlockSp...]
    pallas_call x5, Pallas kernels: 13.2 us -> 11.9 us  [add_side(): pl.pallas_call(functools.partial(square_sum, seqs, table, swapped, last,...]
  transfers between devices with their start and end apart: 28 -> 29, of which waited for: 15 -> 12; matrix products, arithmetic and copies ran while one was open for 1% -> 1% of each run, Pallas kernels for 9% -> 11%
where the time goes in v4:
time: 114 us
  waiting for transfers between devices  50.8 us (45%)
  starting transfers between devices  45.7 us (40%)
  Pallas kernels  14.2 us (12%)
  other arithmetic  1.59 us (1%)
  local copies, waits for them, and re-layouts  1.5 us (1%)
    ppermute x21, waiting for transfers between devices, send(): return lax.ppermute(value, (axis, 'core'), pairs)  39 us
    ppermute x21, starting transfers between devices, send(): return lax.ppermute(value, (axis, 'core'), pairs)  36.5 us
    pallas_call x5, Pallas kernels, add_side(): pl.pallas_call(functools.partial(square_sum, seqs, table, swapped, last,...  11.9 us
    ppermute x8, waiting for transfers between devices, swap(): return lax.ppermute(value, axis, [(0, 1), (1, 0)])  11.8 us
    ppermute x8, starting transfers between devices, swap(): return lax.ppermute(value, axis, [(0, 1), (1, 0)])  9.19 us
  transfers between devices with their start and end apart: 29, of which 12 were waited for; matrix products, arithmetic and copies ran while one was open for 1% of the time, Pallas kernels for 11%

profile of v4, /device:TPU:1, one launch (start us, length us, event | category | flops | bytes accessed | tf_op | source)
XLA Modules:
  0.0 114.3 jit_solution(9152019989360566610)
XLA Ops:
  0.0 1.1 constant_dynamic-slice_fusion.1
  1.1 3.3 %collective-permute-start = (bf16[4,2,3,8,512]{4,3,2,0,1:T(8,128)(2,1)S(1)}, bf16[4,2,3,8,512]{4,3,2,0,1:T(8,128)(2,1)S(1)}, u32[]{:S(2)}, u32[]{:S(2)}) collective-permute-start(bf16[4,2,3,8,512]{4,3,2,0,1:T(8,128)(2,1)S(1)} %bitcast.74), channel_id=1, source_target_pairs={{0,1},{1,0},{2,3},{3,2},{4,5},{5,4},{6,7},{7,6},{8,9},{9,8},{10,11... | collective-permute-start | bytes 589832 | tf_op jit(solution)/shard_map/ppermute | solution.py:21
  7.0 2.4 %collective-permute-start.1 = (bf16[2,3,16,512]{3,2,1,0:T(8,128)(2,1)S(1)}, bf16[2,3,16,512]{3,2,1,0:T(8,128)(2,1)S(1)}, u32[]{:S(2)}, u32[]{:S(2)}) collective-permute-start(bf16[2,3,16,512]{3,2,1,0:T(8,128)(2,1)S(1)} %get-tuple-element.109), channel_id=1, source_target_pairs={{0,32},{1,97},{32,64},{33,1},{64,96},{65,33},{96,0},{97,65},{2,34}... | collective-permute-start | bytes 294920 | tf_op jit(solution)/shard_map/ppermute | solution.py:30
  11.2 2.0 %collective-permute-done.2 = bf16[2,3,16,512]{3,2,1,0:T(8,128)(2,1)S(1)} collective-permute-done((bf16[2,3,16,512]{3,2,1,0:T(8,128)(2,1)S(1)}, bf16[2,3,16,512]{3,2,1,0:T(8,128)(2,1)S(1)}, u32[]{:S(2)}, u32[]{:S(2)}) %collective-permute-start.2) | collective-permute-done | bytes 98336 | tf_op jit(solution)/shard_map/ppermute | solution.py:30
  13.4 1.7 %collective-permute-start.8 = (bf16[3,512,256]{2,1,0:T(8,128)(2,1)S(1)}, bf16[3,512,256]{2,1,0:T(8,128)(2,1)S(1)}, u32[]{:S(2)}, u32[]{:S(2)}) collective-permute-start(bf16[3,512,256]{2,1,0:T(8,128)(2,1)S(1)} %shard_map.28.refs_0_), channel_id=1, source_target_pairs={{0,32},{1,97},{32,64},{33,1},{64,96},{65,33},{96,0},{97,65},{2,34}... | collective-permute-start | bytes 2359304 | tf_op jit(solution)/shard_map/ppermute | solution.py:30
  15.1 2.7 %collective-permute-start.6 = (bf16[2,4,3,16,512]{4,3,2,1,0:T(8,128)(2,1)S(1)}, bf16[2,4,3,16,512]{4,3,2,1,0:T(8,128)(2,1)S(1)}, u32[]{:S(2)}, u32[]{:S(2)}) collective-permute-start(bf16[2,4,3,16,512]{4,3,2,1,0:T(8,128)(2,1)S(1)} %pad_maximum_fusion.6), channel_id=1, source_target_pairs={{0,8},{1,25},{8,16},{9,1},{16,24},{17,9},{24,0},{25,17},{2,10},{3,... | collective-permute-start | bytes 1179656 | tf_op jit(solution)/shard_map/ppermute | solution.py:30
  17.8 6.1 %collective-permute-start.4 = (bf16[4,3,16,512]{3,2,1,0:T(8,128)(2,1)S(1)}, bf16[4,3,16,512]{3,2,1,0:T(8,128)(2,1)S(1)}, u32[]{:S(2)}, u32[]{:S(2)}) collective-permute-start(bf16[4,3,16,512]{3,2,1,0:T(8,128)(2,1)S(1)} %slice_bitcast_fusion), channel_id=1, source_target_pairs={{0,2},{1,7},{2,4},{3,1},{4,6},{5,3},{6,0},{7,5},{8,10},{9,15},{10,... | collective-permute-start | bytes 589832 | tf_op jit(solution)/shard_map/ppermute | solution.py:30
  23.9 8.2 %collective-permute-done.4 = bf16[4,3,16,512]{3,2,1,0:T(8,128)(2,1)S(1)} collective-permute-done((bf16[4,3,16,512]{3,2,1,0:T(8,128)(2,1)S(1)}, bf16[4,3,16,512]{3,2,1,0:T(8,128)(2,1)S(1)}, u32[]{:S(2)}, u32[]{:S(2)}) %collective-permute-start.4) | collective-permute-done | bytes 196640 | tf_op jit(solution)/shard_map/ppermute | solution.py:30
  32.2 4.5 %collective-permute-start.10 = (bf16[2,4,3,16,512]{4,3,2,1,0:T(8,128)(2,1)S(1)}, bf16[2,4,3,16,512]{4,3,2,1,0:T(8,128)(2,1)S(1)}, u32[]{:S(2)}, u32[]{:S(2)}) collective-permute-start(bf16[2,4,3,16,512]{4,3,2,1,0:T(8,128)(2,1)S(1)} %collective-permute-done.6), channel_id=1, source_target_pairs={{0,8},{1,25},{8,16},{9,1},{16,24},{17,9},{24,0},{25,17},{2,10},{3,... | collective-permute-start | bytes 1179656 | tf_op jit(solution)/shard_map/ppermute | solution.py:30
  36.7 2.4 %collective-permute-start.9 = (bf16[4,3,16,512]{3,2,1,0:T(8,128)(2,1)S(1)}, bf16[4,3,16,512]{3,2,1,0:T(8,128)(2,1)S(1)}, u32[]{:S(2)}, u32[]{:S(2)}) collective-permute-start(bf16[4,3,16,512]{3,2,1,0:T(8,128)(2,1)S(1)} %collective-permute-done.4), channel_id=1, source_target_pairs={{0,2},{1,7},{2,4},{3,1},{4,6},{5,3},{6,0},{7,5},{8,10},{9,15},{10,... | collective-permute-start | bytes 589832 | tf_op jit(solution)/shard_map/ppermute | solution.py:30
  39.1 3.3 %collective-permute-done.9 = bf16[4,3,16,512]{3,2,1,0:T(8,128)(2,1)S(1)} collective-permute-done((bf16[4,3,16,512]{3,2,1,0:T(8,128)(2,1)S(1)}, bf16[4,3,16,512]{3,2,1,0:T(8,128)(2,1)S(1)}, u32[]{:S(2)}, u32[]{:S(2)}) %collective-permute-start.9) | collective-permute-done | bytes 196640 | tf_op jit(solution)/shard_map/ppermute | solution.py:30
  42.5 2.4 %collective-permute-start.11 = (bf16[3,4,3,16,512]{4,3,2,1,0:T(8,128)(2,1)S(1)}, bf16[3,4,3,16,512]{4,3,2,1,0:T(8,128)(2,1)S(1)}, u32[]{:S(2)}, u32[]{:S(2)}) collective-permute-start(bf16[3,4,3,16,512]{4,3,2,1,0:T(8,128)(2,1)S(1)} %pad_maximum_fusion.3), channel_id=1, source_target_pairs={{0,8},{1,25},{8,16},{9,1},{16,24},{17,9},{24,0},{25,17},{2,10},{3,... | collective-permute-start | bytes 1769480 | tf_op jit(solution)/shard_map/ppermute | solution.py:30
  45.1 3.9 %collective-permute-start.13 = (bf16[4,3,16,512]{3,2,1,0:T(8,128)(2,1)S(1)}, bf16[4,3,16,512]{3,2,1,0:T(8,128)(2,1)S(1)}, u32[]{:S(2)}, u32[]{:S(2)}) collective-permute-start(bf16[4,3,16,512]{3,2,1,0:T(8,128)(2,1)S(1)} %get-tuple-element.104), channel_id=1, source_target_pairs={{0,2},{1,7},{2,4},{3,1},{4,6},{5,3},{6,0},{7,5},{8,10},{9,15},{10,... | collective-permute-start | bytes 589832 | tf_op jit(solution)/shard_map/ppermute | solution.py:30
  48.9 3.6 %collective-permute-done.13 = bf16[4,3,16,512]{3,2,1,0:T(8,128)(2,1)S(1)} collective-permute-done((bf16[4,3,16,512]{3,2,1,0:T(8,128)(2,1)S(1)}, bf16[4,3,16,512]{3,2,1,0:T(8,128)(2,1)S(1)}, u32[]{:S(2)}, u32[]{:S(2)}) %collective-permute-start.13) | collective-permute-done | bytes 196640 | tf_op jit(solution)/shard_map/ppermute | solution.py:30
  52.6 6.4 %collective-permute-done.14 = bf16[4,3,16,512]{3,2,1,0:T(8,128)(2,1)S(1)} collective-permute-done((bf16[4,3,16,512]{3,2,1,0:T(8,128)(2,1)S(1)}, bf16[4,3,16,512]{3,2,1,0:T(8,128)(2,1)S(1)}, u32[]{:S(2)}, u32[]{:S(2)}) %collective-permute-start.14) | collective-permute-done | bytes 196640 | tf_op jit(solution)/shard_map/ppermute | solution.py:30
  59.0 1.9 %collective-permute-done.12 = bf16[3,4,3,16,512]{4,3,2,1,0:T(8,128)(2,1)S(1)} collective-permute-done((bf16[3,4,3,16,512]{4,3,2,1,0:T(8,128)(2,1)S(1)}, bf16[3,4,3,16,512]{4,3,2,1,0:T(8,128)(2,1)S(1)}, u32[]{:S(2)}, u32[]{:S(2)}) %collective-permute-start.12) | collective-permute-done | bytes 589856 | tf_op jit(solution)/shard_map/ppermute | solution.py:30
  62.6 1.3 %collective-permute-start.19 = (bf16[3,512,256]{2,1,0:T(8,128)(2,1)S(1)}, bf16[3,512,256]{2,1,0:T(8,128)(2,1)S(1)}, u32[]{:S(2)}, u32[]{:S(2)}) collective-permute-start(bf16[3,512,256]{2,1,0:T(8,128)(2,1)S(1)} %collective-permute-done.8.refs_1_), channel_id=1, source_target_pairs={{0,32},{1,97},{32,64},{33,1},{64,96},{65,33},{96,0},{97,65},{2,34}... | collective-permute-start | bytes 2359304 | tf_op jit(solution)/shard_map/ppermute | solution.py:30
  63.8 1.8 %collective-permute-start.16 = (bf16[4,3,16,512]{3,2,1,0:T(8,128)(2,1)S(1)}, bf16[4,3,16,512]{3,2,1,0:T(8,128)(2,1)S(1)}, u32[]{:S(2)}, u32[]{:S(2)}) collective-permute-start(bf16[4,3,16,512]{3,2,1,0:T(8,128)(2,1)S(1)} %collective-permute-done.13), channel_id=1, source_target_pairs={{0,2},{1,7},{2,4},{3,1},{4,6},{5,3},{6,0},{7,5},{8,10},{9,15},{10,... | collective-permute-start | bytes 589832 | tf_op jit(solution)/shard_map/ppermute | solution.py:30
  65.6 5.3 %collective-permute-done.18 = bf16[3,4,3,16,512]{4,3,2,1,0:T(8,128)(2,1)S(1)} collective-permute-done((bf16[3,4,3,16,512]{4,3,2,1,0:T(8,128)(2,1)S(1)}, bf16[3,4,3,16,512]{4,3,2,1,0:T(8,128)(2,1)S(1)}, u32[]{:S(2)}, u32[]{:S(2)}) %collective-permute-start.18) | collective-permute-done | bytes 589856 | tf_op jit(solution)/shard_map/ppermute | solution.py:30
  71.1 1.8 %shard_map.29.refs_3_ = f32[512,512]{1,0:T(8,128)S(1)} custom-call(s32[1]{0:T(128)} %bitcast.core, bf16[3,512,256]{2,1,0:T(8,128)(2,1)S(1)} %shard_map.28.refs_0_, bf16[3,512,256]{2,1,0:T(8,128)(2,1)S(1)} %collective-permute-done.8.refs_1_, bf16[3,512,256]{2,1,0:T(8,128)(2,1)S(1)} %collective-permute-done.15.refs_2_, ...), custom_call_target="tpu_custom_call" | custom-call | flops 1207959552 | bytes 8388608 | tf_op jit(solution)/shard_map/pallas_call | solution.py:157
  74.0 1.7 %collective-permute-start.21 = (bf16[2,4,4,3,16,512]{5,4,3,2,1,0:T(8,128)(2,1)S(1)}, bf16[2,4,4,3,16,512]{5,4,3,2,1,0:T(8,128)(2,1)S(1)}, u32[]{:S(2)}, u32[]{:S(2)}) collective-permute-start(bf16[2,4,4,3,16,512]{5,4,3,2,1,0:T(8,128)(2,1)S(1)} %pad_maximum_fusion.1.refs_4_), channel_id=1, source_target_pairs={{0,1},{1,0},{2,3},{3,2},{4,5},{5,4},{6,7},{7,6},{8,9},{9,8},{10,11... | collective-permute-start | bytes 4718600 | tf_op jit(solution)/shard_map/ppermute | solution.py:21
  75.7 3.0 %collective-permute-start.22 = (bf16[3,4,3,16,512]{4,3,2,1,0:T(8,128)(2,1)S(1)}, bf16[3,4,3,16,512]{4,3,2,1,0:T(8,128)(2,1)S(1)}, u32[]{:S(2)}, u32[]{:S(2)}) collective-permute-start(bf16[3,4,3,16,512]{4,3,2,1,0:T(8,128)(2,1)S(1)} %pad_maximum_fusion.4), channel_id=1, source_target_pairs={{0,8},{1,25},{8,16},{9,1},{16,24},{17,9},{24,0},{25,17},{2,10},{3,... | collective-permute-start | bytes 1769480 | tf_op jit(solution)/shard_map/ppermute | solution.py:30
  78.7 1.3 %shard_map.30 = f32[528,512]{1,0:T(8,128)S(1)} custom-call(s32[1]{0:T(128)} %bitcast.core, bf16[3,512,256]{2,1,0:T(8,128)(2,1)S(1)} %collective-permute-done.19.refs_0_.refs_3_, bf16[3,4,4,3,16,512]{5,4,3,2,1,0:T(8,128)(2,1)S(1)} %pad_maximum_fusion.refs_3_.refs_1_, bf16[4,4,3,16,512]{4,3,2,1,0:T(8,128)(2,1)S(1)} %get-tuple-element.102.refs_4_.refs_2_, ...), custom_call_target="tpu_custom_call" | custom-call | flops 402653184 | bytes 8388608 | tf_op jit(solution)/shard_map/pallas_call | solution.py:157
  80.3 2.8 %shard_map.31 = f32[528,512]{1,0:T(8,128)S(1)} custom-call(s32[1]{0:T(128)} %bitcast.core, bf16[3,512,256]{2,1,0:T(8,128)(2,1)S(1)} %shard_map.28.refs_0_, bf16[3,512,256]{2,1,0:T(8,128)(2,1)S(1)} %collective-permute-done.8.refs_1_, bf16[3,512,256]{2,1,0:T(8,128)(2,1)S(1)} %collective-permute-done.15.refs_2_, ...), custom_call_target="tpu_custom_call" | custom-call | flops 1610612736 | bytes 8388608 | tf_op jit(solution)/shard_map/pallas_call | solution.py:157
  83.1 10.7 %collective-permute-done.20 = f16[528,512]{1,0:T(8,128)(2,1)S(1)} collective-permute-done((f16[528,512]{1,0:T(8,128)(2,1)S(1)}, f16[528,512]{1,0:T(8,128)(2,1)S(1)}, u32[]{:S(2)}, u32[]{:S(2)}) %collective-permute-start.20) | collective-permute-done | bytes 540704 | tf_op jit(solution)/shard_map/ppermute | solution.py:21
  93.9 1.3 %collective-permute-start.27 = (bf16[9,4,3,16,512]{4,3,2,1,0:T(8,128)(2,1)S(1)}, bf16[9,4,3,16,512]{4,3,2,1,0:T(8,128)(2,1)S(1)}, u32[]{:S(2)}, u32[]{:S(2)}) collective-permute-start(bf16[9,4,3,16,512]{4,3,2,1,0:T(8,128)(2,1)S(1)} %slice_dynamic-update-slice_fusion.refs_5_), channel_id=1, source_target_pairs={{0,1},{1,0},{2,3},{3,2},{4,5},{5,4},{6,7},{7,6},{8,9},{9,8},{10,11... | collective-permute-start | bytes 5308424 | tf_op jit(solution)/shard_map/ppermute | solution.py:21
  95.2 2.2 %collective-permute-start.25 = (bf16[3,4,3,16,512]{4,3,2,1,0:T(8,128)(2,1)S(1)}, bf16[3,4,3,16,512]{4,3,2,1,0:T(8,128)(2,1)S(1)}, u32[]{:S(2)}, u32[]{:S(2)}) collective-permute-start(bf16[3,4,3,16,512]{4,3,2,1,0:T(8,128)(2,1)S(1)} %collective-permute-done.22), channel_id=1, source_target_pairs={{0,8},{1,25},{8,16},{9,1},{16,24},{17,9},{24,0},{25,17},{2,10},{3,... | collective-permute-start | bytes 1769480 | tf_op jit(solution)/shard_map/ppermute | solution.py:30
  97.7 6.6 %collective-permute-done.25.refs_6_ = bf16[3,4,3,16,512]{4,3,2,1,0:T(8,128)(2,1)S(1)} collective-permute-done((bf16[3,4,3,16,512]{4,3,2,1,0:T(8,128)(2,1)S(1)}, bf16[3,4,3,16,512]{4,3,2,1,0:T(8,128)(2,1)S(1)}, u32[]{:S(2)}, u32[]{:S(2)}) %collective-permute-start.25) | collective-permute-done | bytes 589856 | tf_op jit(solution)/shard_map/ppermute | solution.py:30
  104.3 2.1 %collective-permute-start.28 = (bf16[3,4,3,16,512]{4,3,2,1,0:T(8,128)(2,1)S(1)}, bf16[3,4,3,16,512]{4,3,2,1,0:T(8,128)(2,1)S(1)}, u32[]{:S(2)}, u32[]{:S(2)}) collective-permute-start(bf16[3,4,3,16,512]{4,3,2,1,0:T(8,128)(2,1)S(1)} %collective-permute-done.25.refs_6_), channel_id=1, source_target_pairs={{0,1},{1,0},{2,3},{3,2},{4,5},{5,4},{6,7},{7,6},{8,9},{9,8},{10,11... | collective-permute-start | bytes 1769480 | tf_op jit(solution)/shard_map/ppermute | solution.py:21
  106.5 3.6 %shard_map.32.given = f32[1024,512]{1,0:T(8,128)} custom-call(s32[1]{0:T(128)} %bitcast.core, bf16[3,512,256]{2,1,0:T(8,128)(2,1)S(1)} %shard_map.28.refs_0_, bf16[3,512,256]{2,1,0:T(8,128)(2,1)S(1)} %collective-permute-done.8.refs_1_, bf16[3,512,256]{2,1,0:T(8,128)(2,1)S(1)} %collective-permute-done.15.refs_2_, ...), custom_call_target="tpu_custom_call" | custom-call | flops 1610612736 | bytes 8388608 | tf_op jit(solution)/shard_map/pallas_call | solution.py:157
  110.3 2.4 %shard_map.33.total = f32[512,512]{1,0:T(8,128)S(1)} custom-call(s32[1]{0:T(128)} %bitcast.core, bf16[3,512,256]{2,1,0:T(8,128)(2,1)S(1)} %shard_map.28.refs_0_, bf16[3,512,256]{2,1,0:T(8,128)(2,1)S(1)} %collective-permute-done.8.refs_1_, bf16[3,512,256]{2,1,0:T(8,128)(2,1)S(1)} %collective-permute-done.15.refs_2_, ...), custom_call_target="tpu_custom_call" | custom-call | flops 1610612736 | bytes 8388608 | tf_op jit(solution)/shard_map/pallas_call | solution.py:157
  112.8 1.3 %shard_map.34 = f32[1024,512]{1,0:T(8,128)} custom-call(s32[1]{0:T(128)} %bitcast.core, f32[512,512]{1,0:T(8,128)S(1)} %shard_map.33.total, f32[528,512]{1,0:T(8,128)S(1)} %convert_element_type.19.before, f32[16,128]{1,0:T(8,128)S(1)} %collective-permute-done.26.token, f32[1024,512]{1,0:T(8,128)} %shard_map.32.given), custom_call_target="tpu_custom_call", output_to_operand_aliasing={{}: (4, {})} | custom-call | tf_op jit(solution)/shard_map/pallas_call | solution.py:184
  (66 shorter events, 8.4 us)
Async XLA Ops:
  0.0 9.5 %copy-start = (bf16[3,256,512]{2,1,0:T(8,128)(2,1)S(1)}, bf16[3,256,512]{2,1,0:T(8,128)(2,1)}, u32[]{:S(2)}) copy-start(bf16[3,256,512]{2,1,0:T(8,128)(2,1)} %acts.1) | copy-start | bytes 2359300
  1.1 4.4 %collective-permute-start = (bf16[4,2,3,8,512]{4,3,2,0,1:T(8,128)(2,1)S(1)}, bf16[4,2,3,8,512]{4,3,2,0,1:T(8,128)(2,1)S(1)}, u32[]{:S(2)}, u32[]{:S(2)}) collective-permute-start(bf16[4,2,3,8,512]{4,3,2,0,1:T(8,128)(2,1)S(1)} %bitcast.74), channel_id=1, source_target_pairs={{0,1},{1,0},{2,3},{3,2},{4,5},{5,4},{6,7},{7,6},{8,9},{9,8},{10,11... | collective-permute-start | bytes 589832 | tf_op jit(solution)/shard_map/ppermute | solution.py:21
  5.6 5.6 %collective-permute-start.3 = (bf16[2,3,16,512]{3,2,1,0:T(8,128)(2,1)S(1)}, bf16[2,3,16,512]{3,2,1,0:T(8,128)(2,1)S(1)}, u32[]{:S(2)}, u32[]{:S(2)}) collective-permute-start(bf16[2,3,16,512]{3,2,1,0:T(8,128)(2,1)S(1)} %get-tuple-element.111), channel_id=1, source_target_pairs={{0,64},{1,65},{32,96},{33,97},{64,0},{65,1},{96,32},{97,33},{2,66}... | collective-permute-start | bytes 294920 | tf_op jit(solution)/shard_map/ppermute | solution.py:30
  6.7 6.5 %collective-permute-start.2 = (bf16[2,3,16,512]{3,2,1,0:T(8,128)(2,1)S(1)}, bf16[2,3,16,512]{3,2,1,0:T(8,128)(2,1)S(1)}, u32[]{:S(2)}, u32[]{:S(2)}) collective-permute-start(bf16[2,3,16,512]{3,2,1,0:T(8,128)(2,1)S(1)} %get-tuple-element.110), channel_id=1, source_target_pairs={{0,96},{1,33},{32,0},{33,65},{64,32},{65,97},{96,64},{97,1},{2,98}... | collective-permute-start | bytes 294920 | tf_op jit(solution)/shard_map/ppermute | solution.py:30
  7.0 6.2 %collective-permute-start.1 = (bf16[2,3,16,512]{3,2,1,0:T(8,128)(2,1)S(1)}, bf16[2,3,16,512]{3,2,1,0:T(8,128)(2,1)S(1)}, u32[]{:S(2)}, u32[]{:S(2)}) collective-permute-start(bf16[2,3,16,512]{3,2,1,0:T(8,128)(2,1)S(1)} %get-tuple-element.109), channel_id=1, source_target_pairs={{0,32},{1,97},{32,64},{33,1},{64,96},{65,33},{96,0},{97,65},{2,34}... | collective-permute-start | bytes 294920 | tf_op jit(solution)/shard_map/ppermute | solution.py:30
  13.4 18.8 %collective-permute-start.8 = (bf16[3,512,256]{2,1,0:T(8,128)(2,1)S(1)}, bf16[3,512,256]{2,1,0:T(8,128)(2,1)S(1)}, u32[]{:S(2)}, u32[]{:S(2)}) collective-permute-start(bf16[3,512,256]{2,1,0:T(8,128)(2,1)S(1)} %shard_map.28.refs_0_), channel_id=1, source_target_pairs={{0,32},{1,97},{32,64},{33,1},{64,96},{65,33},{96,0},{97,65},{2,34}... | collective-permute-start | bytes 2359304 | tf_op jit(solution)/shard_map/ppermute | solution.py:30
  15.1 17.1 %collective-permute-start.6 = (bf16[2,4,3,16,512]{4,3,2,1,0:T(8,128)(2,1)S(1)}, bf16[2,4,3,16,512]{4,3,2,1,0:T(8,128)(2,1)S(1)}, u32[]{:S(2)}, u32[]{:S(2)}) collective-permute-start(bf16[2,4,3,16,512]{4,3,2,1,0:T(8,128)(2,1)S(1)} %pad_maximum_fusion.6), channel_id=1, source_target_pairs={{0,8},{1,25},{8,16},{9,1},{16,24},{17,9},{24,0},{25,17},{2,10},{3,... | collective-permute-start | bytes 1179656 | tf_op jit(solution)/shard_map/ppermute | solution.py:30
  17.8 14.4 %collective-permute-start.7 = (bf16[2,4,3,16,512]{4,3,2,1,0:T(8,128)(2,1)S(1)}, bf16[2,4,3,16,512]{4,3,2,1,0:T(8,128)(2,1)S(1)}, u32[]{:S(2)}, u32[]{:S(2)}) collective-permute-start(bf16[2,4,3,16,512]{4,3,2,1,0:T(8,128)(2,1)S(1)} %pad_maximum_fusion.6), channel_id=1, source_target_pairs={{0,24},{1,9},{8,0},{9,17},{16,8},{17,25},{24,16},{25,1},{2,26},{3,... | collective-permute-start | bytes 1179656 | tf_op jit(solution)/shard_map/ppermute | solution.py:30
  17.8 14.3 %collective-permute-start.4 = (bf16[4,3,16,512]{3,2,1,0:T(8,128)(2,1)S(1)}, bf16[4,3,16,512]{3,2,1,0:T(8,128)(2,1)S(1)}, u32[]{:S(2)}, u32[]{:S(2)}) collective-permute-start(bf16[4,3,16,512]{3,2,1,0:T(8,128)(2,1)S(1)} %slice_bitcast_fusion), channel_id=1, source_target_pairs={{0,2},{1,7},{2,4},{3,1},{4,6},{5,3},{6,0},{7,5},{8,10},{9,15},{10,... | collective-permute-start | bytes 589832 | tf_op jit(solution)/shard_map/ppermute | solution.py:30
  23.9 8.2 %collective-permute-start.5 = (bf16[4,3,16,512]{3,2,1,0:T(8,128)(2,1)S(1)}, bf16[4,3,16,512]{3,2,1,0:T(8,128)(2,1)S(1)}, u32[]{:S(2)}, u32[]{:S(2)}) collective-permute-start(bf16[4,3,16,512]{3,2,1,0:T(8,128)(2,1)S(1)} %slice_bitcast_fusion), channel_id=1, source_target_pairs={{0,6},{1,3},{2,0},{3,5},{4,2},{5,7},{6,4},{7,1},{8,14},{9,11},{10,... | collective-permute-start | bytes 589832 | tf_op jit(solution)/shard_map/ppermute | solution.py:30
  32.2 10.3 %collective-permute-start.10 = (bf16[2,4,3,16,512]{4,3,2,1,0:T(8,128)(2,1)S(1)}, bf16[2,4,3,16,512]{4,3,2,1,0:T(8,128)(2,1)S(1)}, u32[]{:S(2)}, u32[]{:S(2)}) collective-permute-start(bf16[2,4,3,16,512]{4,3,2,1,0:T(8,128)(2,1)S(1)} %collective-permute-done.6), channel_id=1, source_target_pairs={{0,8},{1,25},{8,16},{9,1},{16,24},{17,9},{24,0},{25,17},{2,10},{3,... | collective-permute-start | bytes 1179656 | tf_op jit(solution)/shard_map/ppermute | solution.py:30
  36.7 5.8 %collective-permute-start.9 = (bf16[4,3,16,512]{3,2,1,0:T(8,128)(2,1)S(1)}, bf16[4,3,16,512]{3,2,1,0:T(8,128)(2,1)S(1)}, u32[]{:S(2)}, u32[]{:S(2)}) collective-permute-start(bf16[4,3,16,512]{3,2,1,0:T(8,128)(2,1)S(1)} %collective-permute-done.4), channel_id=1, source_target_pairs={{0,2},{1,7},{2,4},{3,1},{4,6},{5,3},{6,0},{7,5},{8,10},{9,15},{10,... | collective-permute-start | bytes 589832 | tf_op jit(solution)/shard_map/ppermute | solution.py:30
  39.1 19.8 %collective-permute-start.15 = (bf16[3,512,256]{2,1,0:T(8,128)(2,1)S(1)}, bf16[3,512,256]{2,1,0:T(8,128)(2,1)S(1)}, u32[]{:S(2)}, u32[]{:S(2)}) collective-permute-start(bf16[3,512,256]{2,1,0:T(8,128)(2,1)S(1)} %shard_map.28.refs_0_), channel_id=1, source_target_pairs={{0,96},{1,33},{32,0},{33,65},{64,32},{65,97},{96,64},{97,1},{2,98}... | collective-permute-start | bytes 2359304 | tf_op jit(solution)/shard_map/ppermute | solution.py:30
  42.5 16.5 %collective-permute-start.11 = (bf16[3,4,3,16,512]{4,3,2,1,0:T(8,128)(2,1)S(1)}, bf16[3,4,3,16,512]{4,3,2,1,0:T(8,128)(2,1)S(1)}, u32[]{:S(2)}, u32[]{:S(2)}) collective-permute-start(bf16[3,4,3,16,512]{4,3,2,1,0:T(8,128)(2,1)S(1)} %pad_maximum_fusion.3), channel_id=1, source_target_pairs={{0,8},{1,25},{8,16},{9,1},{16,24},{17,9},{24,0},{25,17},{2,10},{3,... | collective-permute-start | bytes 1769480 | tf_op jit(solution)/shard_map/ppermute | solution.py:30
  45.0 15.9 %collective-permute-start.12 = (bf16[3,4,3,16,512]{4,3,2,1,0:T(8,128)(2,1)S(1)}, bf16[3,4,3,16,512]{4,3,2,1,0:T(8,128)(2,1)S(1)}, u32[]{:S(2)}, u32[]{:S(2)}) collective-permute-start(bf16[3,4,3,16,512]{4,3,2,1,0:T(8,128)(2,1)S(1)} %pad_maximum_fusion.3), channel_id=1, source_target_pairs={{0,24},{1,9},{8,0},{9,17},{16,8},{17,25},{24,16},{25,1},{2,26},{3,... | collective-permute-start | bytes 1769480 | tf_op jit(solution)/shard_map/ppermute | solution.py:30
  45.1 7.5 %collective-permute-start.13 = (bf16[4,3,16,512]{3,2,1,0:T(8,128)(2,1)S(1)}, bf16[4,3,16,512]{3,2,1,0:T(8,128)(2,1)S(1)}, u32[]{:S(2)}, u32[]{:S(2)}) collective-permute-start(bf16[4,3,16,512]{3,2,1,0:T(8,128)(2,1)S(1)} %get-tuple-element.104), channel_id=1, source_target_pairs={{0,2},{1,7},{2,4},{3,1},{4,6},{5,3},{6,0},{7,5},{8,10},{9,15},{10,... | collective-permute-start | bytes 589832 | tf_op jit(solution)/shard_map/ppermute | solution.py:30
  48.9 10.0 %collective-permute-start.14 = (bf16[4,3,16,512]{3,2,1,0:T(8,128)(2,1)S(1)}, bf16[4,3,16,512]{3,2,1,0:T(8,128)(2,1)S(1)}, u32[]{:S(2)}, u32[]{:S(2)}) collective-permute-start(bf16[4,3,16,512]{3,2,1,0:T(8,128)(2,1)S(1)} %get-tuple-element.104), channel_id=1, source_target_pairs={{0,6},{1,3},{2,0},{3,5},{4,2},{5,7},{6,4},{7,1},{8,14},{9,11},{10,... | collective-permute-start | bytes 589832 | tf_op jit(solution)/shard_map/ppermute | solution.py:30
  61.4 12.3 %collective-permute-start.17 = (bf16[3,4,4,3,16,512]{5,4,3,2,1,0:T(8,128)(2,1)S(1)}, bf16[3,4,4,3,16,512]{5,4,3,2,1,0:T(8,128)(2,1)S(1)}, u32[]{:S(2)}, u32[]{:S(2)}) collective-permute-start(bf16[3,4,4,3,16,512]{5,4,3,2,1,0:T(8,128)(2,1)S(1)} %pad_maximum_fusion.refs_3_.refs_1_), channel_id=1, source_target_pairs={{0,1},{1,0},{2,3},{3,2},{4,5},{5,4},{6,7},{7,6},{8,9},{9,8},{10,11... | collective-permute-start | bytes 7077896 | tf_op jit(solution)/shard_map/ppermute | solution.py:21
  61.9 9.0 %collective-permute-start.18 = (bf16[3,4,3,16,512]{4,3,2,1,0:T(8,128)(2,1)S(1)}, bf16[3,4,3,16,512]{4,3,2,1,0:T(8,128)(2,1)S(1)}, u32[]{:S(2)}, u32[]{:S(2)}) collective-permute-start(bf16[3,4,3,16,512]{4,3,2,1,0:T(8,128)(2,1)S(1)} %collective-permute-done.11), channel_id=1, source_target_pairs={{0,8},{1,25},{8,16},{9,1},{16,24},{17,9},{24,0},{25,17},{2,10},{3,... | collective-permute-start | bytes 1769480 | tf_op jit(solution)/shard_map/ppermute | solution.py:30
  62.6 11.1 %collective-permute-start.19 = (bf16[3,512,256]{2,1,0:T(8,128)(2,1)S(1)}, bf16[3,512,256]{2,1,0:T(8,128)(2,1)S(1)}, u32[]{:S(2)}, u32[]{:S(2)}) collective-permute-start(bf16[3,512,256]{2,1,0:T(8,128)(2,1)S(1)} %collective-permute-done.8.refs_1_), channel_id=1, source_target_pairs={{0,32},{1,97},{32,64},{33,1},{64,96},{65,33},{96,0},{97,65},{2,34}... | collective-permute-start | bytes 2359304 | tf_op jit(solution)/shard_map/ppermute | solution.py:30
  63.8 9.1 %collective-permute-start.16 = (bf16[4,3,16,512]{3,2,1,0:T(8,128)(2,1)S(1)}, bf16[4,3,16,512]{3,2,1,0:T(8,128)(2,1)S(1)}, u32[]{:S(2)}, u32[]{:S(2)}) collective-permute-start(bf16[4,3,16,512]{3,2,1,0:T(8,128)(2,1)S(1)} %collective-permute-done.13), channel_id=1, source_target_pairs={{0,2},{1,7},{2,4},{3,1},{4,6},{5,3},{6,0},{7,5},{8,10},{9,15},{10,... | collective-permute-start | bytes 589832 | tf_op jit(solution)/shard_map/ppermute | solution.py:30
  74.0 6.3 %collective-permute-start.21 = (bf16[2,4,4,3,16,512]{5,4,3,2,1,0:T(8,128)(2,1)S(1)}, bf16[2,4,4,3,16,512]{5,4,3,2,1,0:T(8,128)(2,1)S(1)}, u32[]{:S(2)}, u32[]{:S(2)}) collective-permute-start(bf16[2,4,4,3,16,512]{5,4,3,2,1,0:T(8,128)(2,1)S(1)} %pad_maximum_fusion.1.refs_4_), channel_id=1, source_target_pairs={{0,1},{1,0},{2,3},{3,2},{4,5},{5,4},{6,7},{7,6},{8,9},{9,8},{10,11... | collective-permute-start | bytes 4718600 | tf_op jit(solution)/shard_map/ppermute | solution.py:21
  75.7 18.0 %collective-permute-start.22 = (bf16[3,4,3,16,512]{4,3,2,1,0:T(8,128)(2,1)S(1)}, bf16[3,4,3,16,512]{4,3,2,1,0:T(8,128)(2,1)S(1)}, u32[]{:S(2)}, u32[]{:S(2)}) collective-permute-start(bf16[3,4,3,16,512]{4,3,2,1,0:T(8,128)(2,1)S(1)} %pad_maximum_fusion.4), channel_id=1, source_target_pairs={{0,8},{1,25},{8,16},{9,1},{16,24},{17,9},{24,0},{25,17},{2,10},{3,... | collective-permute-start | bytes 1769480 | tf_op jit(solution)/shard_map/ppermute | solution.py:30
  78.7 15.0 %collective-permute-start.23 = (bf16[3,4,3,16,512]{4,3,2,1,0:T(8,128)(2,1)S(1)}, bf16[3,4,3,16,512]{4,3,2,1,0:T(8,128)(2,1)S(1)}, u32[]{:S(2)}, u32[]{:S(2)}) collective-permute-start(bf16[3,4,3,16,512]{4,3,2,1,0:T(8,128)(2,1)S(1)} %pad_maximum_fusion.4), channel_id=1, source_target_pairs={{0,24},{1,9},{8,0},{9,17},{16,8},{17,25},{24,16},{25,1},{2,26},{3,... | collective-permute-start | bytes 1769480 | tf_op jit(solution)/shard_map/ppermute | solution.py:30
  80.2 13.6 %collective-permute-start.20 = (f16[528,512]{1,0:T(8,128)(2,1)S(1)}, f16[528,512]{1,0:T(8,128)(2,1)S(1)}, u32[]{:S(2)}, u32[]{:S(2)}) collective-permute-start(f16[528,512]{1,0:T(8,128)(2,1)S(1)} %convert_element_type.15), channel_id=1, source_target_pairs={{0,128},{128,0},{1,129},{129,1},{2,130},{130,2},{3,131},{131,3},{4... | collective-permute-start | bytes 1622024 | tf_op jit(solution)/shard_map/ppermute | solution.py:21
  93.9 16.4 %collective-permute-start.27 = (bf16[9,4,3,16,512]{4,3,2,1,0:T(8,128)(2,1)S(1)}, bf16[9,4,3,16,512]{4,3,2,1,0:T(8,128)(2,1)S(1)}, u32[]{:S(2)}, u32[]{:S(2)}) collective-permute-start(bf16[9,4,3,16,512]{4,3,2,1,0:T(8,128)(2,1)S(1)} %slice_dynamic-update-slice_fusion.refs_5_), channel_id=1, source_target_pairs={{0,1},{1,0},{2,3},{3,2},{4,5},{5,4},{6,7},{7,6},{8,9},{9,8},{10,11... | collective-permute-start | bytes 5308424 | tf_op jit(solution)/shard_map/ppermute | solution.py:21
  95.2 9.1 %collective-permute-start.25 = (bf16[3,4,3,16,512]{4,3,2,1,0:T(8,128)(2,1)S(1)}, bf16[3,4,3,16,512]{4,3,2,1,0:T(8,128)(2,1)S(1)}, u32[]{:S(2)}, u32[]{:S(2)}) collective-permute-start(bf16[3,4,3,16,512]{4,3,2,1,0:T(8,128)(2,1)S(1)} %collective-permute-done.22), channel_id=1, source_target_pairs={{0,8},{1,25},{8,16},{9,1},{16,24},{17,9},{24,0},{25,17},{2,10},{3,... | collective-permute-start | bytes 1769480 | tf_op jit(solution)/shard_map/ppermute | solution.py:30
  97.6 12.6 %collective-permute-start.24 = (f16[528,512]{1,0:T(8,128)(2,1)S(1)}, f16[528,512]{1,0:T(8,128)(2,1)S(1)}, u32[]{:S(2)}, u32[]{:S(2)}) collective-permute-start(f16[528,512]{1,0:T(8,128)(2,1)S(1)} %convert_element_type.16), channel_id=1, source_target_pairs={{0,128},{128,0},{1,129},{129,1},{2,130},{130,2},{3,131},{131,3},{4... | collective-permute-start | bytes 1622024 | tf_op jit(solution)/shard_map/ppermute | solution.py:21
  104.3 6.0 %collective-permute-start.28 = (bf16[3,4,3,16,512]{4,3,2,1,0:T(8,128)(2,1)S(1)}, bf16[3,4,3,16,512]{4,3,2,1,0:T(8,128)(2,1)S(1)}, u32[]{:S(2)}, u32[]{:S(2)}) collective-permute-start(bf16[3,4,3,16,512]{4,3,2,1,0:T(8,128)(2,1)S(1)} %collective-permute-done.25.refs_6_), channel_id=1, source_target_pairs={{0,1},{1,0},{2,3},{3,2},{4,5},{5,4},{6,7},{7,6},{8,9},{9,8},{10,11... | collective-permute-start | bytes 1769480 | tf_op jit(solution)/shard_map/ppermute | solution.py:21
  110.2 2.5 %collective-permute-start.26 = (f32[16,128]{1,0:T(8,128)S(1)}, f32[16,128]{1,0:T(8,128)S(1)}, u32[]{:S(2)}, u32[]{:S(2)}) collective-permute-start(f32[16,128]{1,0:T(8,128)S(1)} %slice_convert_fusion), channel_id=1, source_target_pairs={{0,1},{1,0},{2,3},{3,2},{4,5},{5,4},{6,7},{7,6},{8,9},{9,8},{10,11... | collective-permute-start | bytes 24584 | tf_op jit(solution)/shard_map/ppermute | solution.py:21

commit v5 on v4

--- a/solution.py
+++ b/solution.py
@@ -12,6 +12,7 @@
 SEQS_DP = 3
 ROWS = 16
 LANES = 256
+PARTS = 4
 SCALE = 14
 SWAP = (0, 2, 1, 3)
 VMEM = pl.BlockSpec(memory_space=pltpu.VMEM)
@@ -60,6 +61,20 @@
             flops=10**9, bytes_accessed=4 * acts.size, transcendentals=0
         ),
     )(place, acts)
+
+
+def write_out(total, turned, out, sems, where, seqs):
+    half = total.shape[1]
+    size = half // PARTS
+    copies = []
+    for part in range(PARTS):
+        rows = slice(part * size, (part + 1) * size)
+        turned[rows, :] = total[:, rows].T * jnp.float32(1 / seqs)
+        at = pl.ds(pl.multiple_of(where * half + part * size, size), size)
+        copies.append(pltpu.make_async_copy(turned.at[rows, :], out.at[at, :], sems.at[part]))
+        copies[-1].start()
+    for copy in copies:
+        copy.wait()
 
 
 def square_sum(seqs, table, swapped, last, sources, more, count, core, *refs):
@@ -103,11 +118,7 @@
 
     if last:
         where = 1 - core[0] if swapped else core[0]
-        turned[...] = total[...].T * jnp.float32(1 / seqs)
-        at = pl.ds(pl.multiple_of(where * half, half), half)
-        copy = pltpu.make_async_copy(turned, out.at[at, :], sem)
-        copy.start()
-        copy.wait()
+        write_out(total, turned, out, sem, where, seqs)
     elif more == "before":
         sent[...] = total[...]
     else:
@@ -140,7 +151,7 @@
             scratch_shapes=[
                 pltpu.VMEM(total.shape, jnp.float32),
                 pltpu.VMEM((half, feats), jnp.float32),
-                pltpu.SemaphoreType.DMA,
+                pltpu.SemaphoreType.DMA((PARTS,)),
             ],
             input_output_aliases={len(args) - 1: 0} if swapped else {},
         )
@@ -167,15 +178,10 @@
     )(*args)
 
 
-def finish_body(seqs, core, total, before, token, given, out, turned, sem):
-    half = total.shape[1]
+def finish_body(seqs, core, given_total, before, token, given, out, turned, sem, total):
     back = jnp.exp2(before[-8:, :][:1] - SCALE)
-    whole = total[...] + before[: total.shape[0], :] * back
-    turned[...] = whole.T * jnp.float32(1 / seqs)
-    at = pl.ds(pl.multiple_of((1 - core[0]) * half, half), half)
-    copy = pltpu.make_async_copy(turned, out.at[at, :], sem)
-    copy.start()
-    copy.wait()
+    total[...] = given_total[...] + before[: total.shape[0], :] * back
+    write_out(total, turned, out, sem, 1 - core[0], seqs)
 
 
 def finish(seqs, core, total, before, token, out):
@@ -186,7 +192,11 @@
         in_specs=[pl.BlockSpec(memory_space=pltpu.SMEM), VMEM, VMEM, anywhere, anywhere],
         out_specs=anywhere,
         out_shape=jax.ShapeDtypeStruct(out.shape, jnp.float32),
-        scratch_shapes=[pltpu.VMEM((half, feats), jnp.float32), pltpu.SemaphoreType.DMA],
+        scratch_shapes=[
+            pltpu.VMEM((half, feats), jnp.float32),
+            pltpu.SemaphoreType.DMA((PARTS,)),
+            pltpu.VMEM((feats, half), jnp.float32),
+        ],
         input_output_aliases={4: 0},
         compiler_params=pltpu.CompilerParams(vmem_limit_bytes=6 * 2**20),
     )(core, total, before, token, out)

time: 114 us -> 114 us (level)
  no operation moved by 1% of the time
where the time goes in v5:
time: 114 us
  waiting for transfers between devices  50.8 us (45%)
  starting transfers between devices  45.7 us (40%)
  Pallas kernels  13.9 us (12%)
  other arithmetic  1.59 us (1%)
  local copies, waits for them, and re-layouts  1.5 us (1%)
    ppermute x21, waiting for transfers between devices, send(): return lax.ppermute(value, (axis, 'core'), pairs)  39 us
    ppermute x21, starting transfers between devices, send(): return lax.ppermute(value, (axis, 'core'), pairs)  36.5 us
    ppermute x8, waiting for transfers between devices, swap(): return lax.ppermute(value, axis, [(0, 1), (1, 0)])  11.8 us
    pallas_call x5, Pallas kernels, add_side(): pl.pallas_call(functools.partial(square_sum, seqs, table, swapped, last,...  11.7 us
    ppermute x8, starting transfers between devices, swap(): return lax.ppermute(value, axis, [(0, 1), (1, 0)])  9.19 us
  transfers between devices with their start and end apart: 29, of which 12 were waited for; matrix products, arithmetic and copies ran while one was open for 1% of the time, Pallas kernels for 11%

profile of v5, /device:TPU:1, one launch (start us, length us, event | category | flops | bytes accessed | tf_op | source)
XLA Modules:
  0.0 114.0 jit_solution(12789009647448173429)
XLA Ops:
  0.0 1.1 constant_dynamic-slice_fusion.1
  1.1 3.3 %collective-permute-start = (bf16[4,2,3,8,512]{4,3,2,0,1:T(8,128)(2,1)S(1)}, bf16[4,2,3,8,512]{4,3,2,0,1:T(8,128)(2,1)S(1)}, u32[]{:S(2)}, u32[]{:S(2)}) collective-permute-start(bf16[4,2,3,8,512]{4,3,2,0,1:T(8,128)(2,1)S(1)} %bitcast.74), channel_id=1, source_target_pairs={{0,1},{1,0},{2,3},{3,2},{4,5},{5,4},{6,7},{7,6},{8,9},{9,8},{10,11... | collective-permute-start | bytes 589832 | tf_op jit(solution)/shard_map/ppermute | solution.py:22
  7.0 2.4 %collective-permute-start.1 = (bf16[2,3,16,512]{3,2,1,0:T(8,128)(2,1)S(1)}, bf16[2,3,16,512]{3,2,1,0:T(8,128)(2,1)S(1)}, u32[]{:S(2)}, u32[]{:S(2)}) collective-permute-start(bf16[2,3,16,512]{3,2,1,0:T(8,128)(2,1)S(1)} %get-tuple-element.109), channel_id=1, source_target_pairs={{0,32},{1,97},{32,64},{33,1},{64,96},{65,33},{96,0},{97,65},{2,34}... | collective-permute-start | bytes 294920 | tf_op jit(solution)/shard_map/ppermute | solution.py:31
  11.2 2.0 %collective-permute-done.2 = bf16[2,3,16,512]{3,2,1,0:T(8,128)(2,1)S(1)} collective-permute-done((bf16[2,3,16,512]{3,2,1,0:T(8,128)(2,1)S(1)}, bf16[2,3,16,512]{3,2,1,0:T(8,128)(2,1)S(1)}, u32[]{:S(2)}, u32[]{:S(2)}) %collective-permute-start.2) | collective-permute-done | bytes 98336 | tf_op jit(solution)/shard_map/ppermute | solution.py:31
  13.4 1.7 %collective-permute-start.8 = (bf16[3,512,256]{2,1,0:T(8,128)(2,1)S(1)}, bf16[3,512,256]{2,1,0:T(8,128)(2,1)S(1)}, u32[]{:S(2)}, u32[]{:S(2)}) collective-permute-start(bf16[3,512,256]{2,1,0:T(8,128)(2,1)S(1)} %shard_map.28.refs_0_), channel_id=1, source_target_pairs={{0,32},{1,97},{32,64},{33,1},{64,96},{65,33},{96,0},{97,65},{2,34}... | collective-permute-start | bytes 2359304 | tf_op jit(solution)/shard_map/ppermute | solution.py:31
  15.1 2.7 %collective-permute-start.6 = (bf16[2,4,3,16,512]{4,3,2,1,0:T(8,128)(2,1)S(1)}, bf16[2,4,3,16,512]{4,3,2,1,0:T(8,128)(2,1)S(1)}, u32[]{:S(2)}, u32[]{:S(2)}) collective-permute-start(bf16[2,4,3,16,512]{4,3,2,1,0:T(8,128)(2,1)S(1)} %pad_maximum_fusion.6), channel_id=1, source_target_pairs={{0,8},{1,25},{8,16},{9,1},{16,24},{17,9},{24,0},{25,17},{2,10},{3,... | collective-permute-start | bytes 1179656 | tf_op jit(solution)/shard_map/ppermute | solution.py:31
  17.8 6.1 %collective-permute-start.4 = (bf16[4,3,16,512]{3,2,1,0:T(8,128)(2,1)S(1)}, bf16[4,3,16,512]{3,2,1,0:T(8,128)(2,1)S(1)}, u32[]{:S(2)}, u32[]{:S(2)}) collective-permute-start(bf16[4,3,16,512]{3,2,1,0:T(8,128)(2,1)S(1)} %slice_bitcast_fusion), channel_id=1, source_target_pairs={{0,2},{1,7},{2,4},{3,1},{4,6},{5,3},{6,0},{7,5},{8,10},{9,15},{10,... | collective-permute-start | bytes 589832 | tf_op jit(solution)/shard_map/ppermute | solution.py:31
  23.9 8.2 %collective-permute-done.4 = bf16[4,3,16,512]{3,2,1,0:T(8,128)(2,1)S(1)} collective-permute-done((bf16[4,3,16,512]{3,2,1,0:T(8,128)(2,1)S(1)}, bf16[4,3,16,512]{3,2,1,0:T(8,128)(2,1)S(1)}, u32[]{:S(2)}, u32[]{:S(2)}) %collective-permute-start.4) | collective-permute-done | bytes 196640 | tf_op jit(solution)/shard_map/ppermute | solution.py:31
  32.2 4.5 %collective-permute-start.10 = (bf16[2,4,3,16,512]{4,3,2,1,0:T(8,128)(2,1)S(1)}, bf16[2,4,3,16,512]{4,3,2,1,0:T(8,128)(2,1)S(1)}, u32[]{:S(2)}, u32[]{:S(2)}) collective-permute-start(bf16[2,4,3,16,512]{4,3,2,1,0:T(8,128)(2,1)S(1)} %collective-permute-done.6), channel_id=1, source_target_pairs={{0,8},{1,25},{8,16},{9,1},{16,24},{17,9},{24,0},{25,17},{2,10},{3,... | collective-permute-start | bytes 1179656 | tf_op jit(solution)/shard_map/ppermute | solution.py:31
  36.7 2.4 %collective-permute-start.9 = (bf16[4,3,16,512]{3,2,1,0:T(8,128)(2,1)S(1)}, bf16[4,3,16,512]{3,2,1,0:T(8,128)(2,1)S(1)}, u32[]{:S(2)}, u32[]{:S(2)}) collective-permute-start(bf16[4,3,16,512]{3,2,1,0:T(8,128)(2,1)S(1)} %collective-permute-done.4), channel_id=1, source_target_pairs={{0,2},{1,7},{2,4},{3,1},{4,6},{5,3},{6,0},{7,5},{8,10},{9,15},{10,... | collective-permute-start | bytes 589832 | tf_op jit(solution)/shard_map/ppermute | solution.py:31
  39.1 3.3 %collective-permute-done.9 = bf16[4,3,16,512]{3,2,1,0:T(8,128)(2,1)S(1)} collective-permute-done((bf16[4,3,16,512]{3,2,1,0:T(8,128)(2,1)S(1)}, bf16[4,3,16,512]{3,2,1,0:T(8,128)(2,1)S(1)}, u32[]{:S(2)}, u32[]{:S(2)}) %collective-permute-start.9) | collective-permute-done | bytes 196640 | tf_op jit(solution)/shard_map/ppermute | solution.py:31
  42.5 2.4 %collective-permute-start.11 = (bf16[3,4,3,16,512]{4,3,2,1,0:T(8,128)(2,1)S(1)}, bf16[3,4,3,16,512]{4,3,2,1,0:T(8,128)(2,1)S(1)}, u32[]{:S(2)}, u32[]{:S(2)}) collective-permute-start(bf16[3,4,3,16,512]{4,3,2,1,0:T(8,128)(2,1)S(1)} %pad_maximum_fusion.3), channel_id=1, source_target_pairs={{0,8},{1,25},{8,16},{9,1},{16,24},{17,9},{24,0},{25,17},{2,10},{3,... | collective-permute-start | bytes 1769480 | tf_op jit(solution)/shard_map/ppermute | solution.py:31
  45.1 3.9 %collective-permute-start.13 = (bf16[4,3,16,512]{3,2,1,0:T(8,128)(2,1)S(1)}, bf16[4,3,16,512]{3,2,1,0:T(8,128)(2,1)S(1)}, u32[]{:S(2)}, u32[]{:S(2)}) collective-permute-start(bf16[4,3,16,512]{3,2,1,0:T(8,128)(2,1)S(1)} %get-tuple-element.104), channel_id=1, source_target_pairs={{0,2},{1,7},{2,4},{3,1},{4,6},{5,3},{6,0},{7,5},{8,10},{9,15},{10,... | collective-permute-start | bytes 589832 | tf_op jit(solution)/shard_map/ppermute | solution.py:31
  48.9 3.6 %collective-permute-done.13 = bf16[4,3,16,512]{3,2,1,0:T(8,128)(2,1)S(1)} collective-permute-done((bf16[4,3,16,512]{3,2,1,0:T(8,128)(2,1)S(1)}, bf16[4,3,16,512]{3,2,1,0:T(8,128)(2,1)S(1)}, u32[]{:S(2)}, u32[]{:S(2)}) %collective-permute-start.13) | collective-permute-done | bytes 196640 | tf_op jit(solution)/shard_map/ppermute | solution.py:31
  52.6 6.4 %collective-permute-done.14 = bf16[4,3,16,512]{3,2,1,0:T(8,128)(2,1)S(1)} collective-permute-done((bf16[4,3,16,512]{3,2,1,0:T(8,128)(2,1)S(1)}, bf16[4,3,16,512]{3,2,1,0:T(8,128)(2,1)S(1)}, u32[]{:S(2)}, u32[]{:S(2)}) %collective-permute-start.14) | collective-permute-done | bytes 196640 | tf_op jit(solution)/shard_map/ppermute | solution.py:31
  59.0 1.9 %collective-permute-done.12 = bf16[3,4,3,16,512]{4,3,2,1,0:T(8,128)(2,1)S(1)} collective-permute-done((bf16[3,4,3,16,512]{4,3,2,1,0:T(8,128)(2,1)S(1)}, bf16[3,4,3,16,512]{4,3,2,1,0:T(8,128)(2,1)S(1)}, u32[]{:S(2)}, u32[]{:S(2)}) %collective-permute-start.12) | collective-permute-done | bytes 589856 | tf_op jit(solution)/shard_map/ppermute | solution.py:31
  62.6 1.3 %collective-permute-start.19 = (bf16[3,512,256]{2,1,0:T(8,128)(2,1)S(1)}, bf16[3,512,256]{2,1,0:T(8,128)(2,1)S(1)}, u32[]{:S(2)}, u32[]{:S(2)}) collective-permute-start(bf16[3,512,256]{2,1,0:T(8,128)(2,1)S(1)} %collective-permute-done.8.refs_1_), channel_id=1, source_target_pairs={{0,32},{1,97},{32,64},{33,1},{64,96},{65,33},{96,0},{97,65},{2,34}... | collective-permute-start | bytes 2359304 | tf_op jit(solution)/shard_map/ppermute | solution.py:31
  63.8 1.8 %collective-permute-start.16 = (bf16[4,3,16,512]{3,2,1,0:T(8,128)(2,1)S(1)}, bf16[4,3,16,512]{3,2,1,0:T(8,128)(2,1)S(1)}, u32[]{:S(2)}, u32[]{:S(2)}) collective-permute-start(bf16[4,3,16,512]{3,2,1,0:T(8,128)(2,1)S(1)} %collective-permute-done.13), channel_id=1, source_target_pairs={{0,2},{1,7},{2,4},{3,1},{4,6},{5,3},{6,0},{7,5},{8,10},{9,15},{10,... | collective-permute-start | bytes 589832 | tf_op jit(solution)/shard_map/ppermute | solution.py:31
  65.6 5.3 %collective-permute-done.18 = bf16[3,4,3,16,512]{4,3,2,1,0:T(8,128)(2,1)S(1)} collective-permute-done((bf16[3,4,3,16,512]{4,3,2,1,0:T(8,128)(2,1)S(1)}, bf16[3,4,3,16,512]{4,3,2,1,0:T(8,128)(2,1)S(1)}, u32[]{:S(2)}, u32[]{:S(2)}) %collective-permute-start.18) | collective-permute-done | bytes 589856 | tf_op jit(solution)/shard_map/ppermute | solution.py:31
  71.1 1.8 %shard_map.29.refs_3_ = f32[512,512]{1,0:T(8,128)S(1)} custom-call(s32[1]{0:T(128)} %bitcast.core, bf16[3,512,256]{2,1,0:T(8,128)(2,1)S(1)} %shard_map.28.refs_0_, bf16[3,512,256]{2,1,0:T(8,128)(2,1)S(1)} %collective-permute-done.8.refs_1_, bf16[3,512,256]{2,1,0:T(8,128)(2,1)S(1)} %collective-permute-done.15.refs_2_, ...), custom_call_target="tpu_custom_call" | custom-call | flops 1207959552 | bytes 8388608 | tf_op jit(solution)/shard_map/pallas_call | solution.py:168
  74.0 1.7 %collective-permute-start.21 = (bf16[2,4,4,3,16,512]{5,4,3,2,1,0:T(8,128)(2,1)S(1)}, bf16[2,4,4,3,16,512]{5,4,3,2,1,0:T(8,128)(2,1)S(1)}, u32[]{:S(2)}, u32[]{:S(2)}) collective-permute-start(bf16[2,4,4,3,16,512]{5,4,3,2,1,0:T(8,128)(2,1)S(1)} %pad_maximum_fusion.1.refs_4_), channel_id=1, source_target_pairs={{0,1},{1,0},{2,3},{3,2},{4,5},{5,4},{6,7},{7,6},{8,9},{9,8},{10,11... | collective-permute-start | bytes 4718600 | tf_op jit(solution)/shard_map/ppermute | solution.py:22
  75.7 3.0 %collective-permute-start.22 = (bf16[3,4,3,16,512]{4,3,2,1,0:T(8,128)(2,1)S(1)}, bf16[3,4,3,16,512]{4,3,2,1,0:T(8,128)(2,1)S(1)}, u32[]{:S(2)}, u32[]{:S(2)}) collective-permute-start(bf16[3,4,3,16,512]{4,3,2,1,0:T(8,128)(2,1)S(1)} %pad_maximum_fusion.4), channel_id=1, source_target_pairs={{0,8},{1,25},{8,16},{9,1},{16,24},{17,9},{24,0},{25,17},{2,10},{3,... | collective-permute-start | bytes 1769480 | tf_op jit(solution)/shard_map/ppermute | solution.py:31
  78.7 1.3 %shard_map.30 = f32[528,512]{1,0:T(8,128)S(1)} custom-call(s32[1]{0:T(128)} %bitcast.core, bf16[3,512,256]{2,1,0:T(8,128)(2,1)S(1)} %collective-permute-done.19.refs_0_.refs_3_, bf16[3,4,4,3,16,512]{5,4,3,2,1,0:T(8,128)(2,1)S(1)} %pad_maximum_fusion.refs_3_.refs_1_, bf16[4,4,3,16,512]{4,3,2,1,0:T(8,128)(2,1)S(1)} %get-tuple-element.102.refs_4_.refs_2_, ...), custom_call_target="tpu_custom_call" | custom-call | flops 402653184 | bytes 8388608 | tf_op jit(solution)/shard_map/pallas_call | solution.py:168
  80.3 2.8 %shard_map.31 = f32[528,512]{1,0:T(8,128)S(1)} custom-call(s32[1]{0:T(128)} %bitcast.core, bf16[3,512,256]{2,1,0:T(8,128)(2,1)S(1)} %shard_map.28.refs_0_, bf16[3,512,256]{2,1,0:T(8,128)(2,1)S(1)} %collective-permute-done.8.refs_1_, bf16[3,512,256]{2,1,0:T(8,128)(2,1)S(1)} %collective-permute-done.15.refs_2_, ...), custom_call_target="tpu_custom_call" | custom-call | flops 1610612736 | bytes 8388608 | tf_op jit(solution)/shard_map/pallas_call | solution.py:168
  83.1 10.7 %collective-permute-done.20 = f16[528,512]{1,0:T(8,128)(2,1)S(1)} collective-permute-done((f16[528,512]{1,0:T(8,128)(2,1)S(1)}, f16[528,512]{1,0:T(8,128)(2,1)S(1)}, u32[]{:S(2)}, u32[]{:S(2)}) %collective-permute-start.20) | collective-permute-done | bytes 540704 | tf_op jit(solution)/shard_map/ppermute | solution.py:22
  93.9 1.3 %collective-permute-start.27 = (bf16[9,4,3,16,512]{4,3,2,1,0:T(8,128)(2,1)S(1)}, bf16[9,4,3,16,512]{4,3,2,1,0:T(8,128)(2,1)S(1)}, u32[]{:S(2)}, u32[]{:S(2)}) collective-permute-start(bf16[9,4,3,16,512]{4,3,2,1,0:T(8,128)(2,1)S(1)} %slice_dynamic-update-slice_fusion.refs_5_), channel_id=1, source_target_pairs={{0,1},{1,0},{2,3},{3,2},{4,5},{5,4},{6,7},{7,6},{8,9},{9,8},{10,11... | collective-permute-start | bytes 5308424 | tf_op jit(solution)/shard_map/ppermute | solution.py:22
  95.2 2.2 %collective-permute-start.25 = (bf16[3,4,3,16,512]{4,3,2,1,0:T(8,128)(2,1)S(1)}, bf16[3,4,3,16,512]{4,3,2,1,0:T(8,128)(2,1)S(1)}, u32[]{:S(2)}, u32[]{:S(2)}) collective-permute-start(bf16[3,4,3,16,512]{4,3,2,1,0:T(8,128)(2,1)S(1)} %collective-permute-done.22), channel_id=1, source_target_pairs={{0,8},{1,25},{8,16},{9,1},{16,24},{17,9},{24,0},{25,17},{2,10},{3,... | collective-permute-start | bytes 1769480 | tf_op jit(solution)/shard_map/ppermute | solution.py:31
  97.7 6.6 %collective-permute-done.25.refs_6_ = bf16[3,4,3,16,512]{4,3,2,1,0:T(8,128)(2,1)S(1)} collective-permute-done((bf16[3,4,3,16,512]{4,3,2,1,0:T(8,128)(2,1)S(1)}, bf16[3,4,3,16,512]{4,3,2,1,0:T(8,128)(2,1)S(1)}, u32[]{:S(2)}, u32[]{:S(2)}) %collective-permute-start.25) | collective-permute-done | bytes 589856 | tf_op jit(solution)/shard_map/ppermute | solution.py:31
  104.3 2.1 %collective-permute-start.28 = (bf16[3,4,3,16,512]{4,3,2,1,0:T(8,128)(2,1)S(1)}, bf16[3,4,3,16,512]{4,3,2,1,0:T(8,128)(2,1)S(1)}, u32[]{:S(2)}, u32[]{:S(2)}) collective-permute-start(bf16[3,4,3,16,512]{4,3,2,1,0:T(8,128)(2,1)S(1)} %collective-permute-done.25.refs_6_), channel_id=1, source_target_pairs={{0,1},{1,0},{2,3},{3,2},{4,5},{5,4},{6,7},{7,6},{8,9},{9,8},{10,11... | collective-permute-start | bytes 1769480 | tf_op jit(solution)/shard_map/ppermute | solution.py:22
  106.5 3.4 %shard_map.32.given = f32[1024,512]{1,0:T(8,128)} custom-call(s32[1]{0:T(128)} %bitcast.core, bf16[3,512,256]{2,1,0:T(8,128)(2,1)S(1)} %shard_map.28.refs_0_, bf16[3,512,256]{2,1,0:T(8,128)(2,1)S(1)} %collective-permute-done.8.refs_1_, bf16[3,512,256]{2,1,0:T(8,128)(2,1)S(1)} %collective-permute-done.15.refs_2_, ...), custom_call_target="tpu_custom_call" | custom-call | flops 1610612736 | bytes 8388608 | tf_op jit(solution)/shard_map/pallas_call | solution.py:168
  110.1 2.4 %shard_map.33.given_total = f32[512,512]{1,0:T(8,128)S(1)} custom-call(s32[1]{0:T(128)} %bitcast.core, bf16[3,512,256]{2,1,0:T(8,128)(2,1)S(1)} %shard_map.28.refs_0_, bf16[3,512,256]{2,1,0:T(8,128)(2,1)S(1)} %collective-permute-done.8.refs_1_, bf16[3,512,256]{2,1,0:T(8,128)(2,1)S(1)} %collective-permute-done.15.refs_2_, ...), custom_call_target="tpu_custom_call" | custom-call | flops 1610612736 | bytes 8388608 | tf_op jit(solution)/shard_map/pallas_call | solution.py:168
  112.6 1.1 %shard_map.34 = f32[1024,512]{1,0:T(8,128)} custom-call(s32[1]{0:T(128)} %bitcast.core, f32[512,512]{1,0:T(8,128)S(1)} %shard_map.33.given_total, f32[528,512]{1,0:T(8,128)S(1)} %convert_element_type.19.before, f32[16,128]{1,0:T(8,128)S(1)} %collective-permute-done.26.token, f32[1024,512]{1,0:T(8,128)} %shard_map.32.given), custom_call_target="tpu_custom_call", output_to_operand_aliasing={{}: (4, {})} | custom-call | tf_op jit(solution)/shard_map/pallas_call | solution.py:190
  (66 shorter events, 8.4 us)
Async XLA Ops:
  0.0 9.5 %copy-start = (bf16[3,256,512]{2,1,0:T(8,128)(2,1)S(1)}, bf16[3,256,512]{2,1,0:T(8,128)(2,1)}, u32[]{:S(2)}) copy-start(bf16[3,256,512]{2,1,0:T(8,128)(2,1)} %acts.1) | copy-start | bytes 2359300
  1.1 4.4 %collective-permute-start = (bf16[4,2,3,8,512]{4,3,2,0,1:T(8,128)(2,1)S(1)}, bf16[4,2,3,8,512]{4,3,2,0,1:T(8,128)(2,1)S(1)}, u32[]{:S(2)}, u32[]{:S(2)}) collective-permute-start(bf16[4,2,3,8,512]{4,3,2,0,1:T(8,128)(2,1)S(1)} %bitcast.74), channel_id=1, source_target_pairs={{0,1},{1,0},{2,3},{3,2},{4,5},{5,4},{6,7},{7,6},{8,9},{9,8},{10,11... | collective-permute-start | bytes 589832 | tf_op jit(solution)/shard_map/ppermute | solution.py:22
  5.6 5.6 %collective-permute-start.3 = (bf16[2,3,16,512]{3,2,1,0:T(8,128)(2,1)S(1)}, bf16[2,3,16,512]{3,2,1,0:T(8,128)(2,1)S(1)}, u32[]{:S(2)}, u32[]{:S(2)}) collective-permute-start(bf16[2,3,16,512]{3,2,1,0:T(8,128)(2,1)S(1)} %get-tuple-element.111), channel_id=1, source_target_pairs={{0,64},{1,65},{32,96},{33,97},{64,0},{65,1},{96,32},{97,33},{2,66}... | collective-permute-start | bytes 294920 | tf_op jit(solution)/shard_map/ppermute | solution.py:31
  6.7 6.5 %collective-permute-start.2 = (bf16[2,3,16,512]{3,2,1,0:T(8,128)(2,1)S(1)}, bf16[2,3,16,512]{3,2,1,0:T(8,128)(2,1)S(1)}, u32[]{:S(2)}, u32[]{:S(2)}) collective-permute-start(bf16[2,3,16,512]{3,2,1,0:T(8,128)(2,1)S(1)} %get-tuple-element.110), channel_id=1, source_target_pairs={{0,96},{1,33},{32,0},{33,65},{64,32},{65,97},{96,64},{97,1},{2,98}... | collective-permute-start | bytes 294920 | tf_op jit(solution)/shard_map/ppermute | solution.py:31
  7.0 6.2 %collective-permute-start.1 = (bf16[2,3,16,512]{3,2,1,0:T(8,128)(2,1)S(1)}, bf16[2,3,16,512]{3,2,1,0:T(8,128)(2,1)S(1)}, u32[]{:S(2)}, u32[]{:S(2)}) collective-permute-start(bf16[2,3,16,512]{3,2,1,0:T(8,128)(2,1)S(1)} %get-tuple-element.109), channel_id=1, source_target_pairs={{0,32},{1,97},{32,64},{33,1},{64,96},{65,33},{96,0},{97,65},{2,34}... | collective-permute-start | bytes 294920 | tf_op jit(solution)/shard_map/ppermute | solution.py:31
  13.4 18.8 %collective-permute-start.8 = (bf16[3,512,256]{2,1,0:T(8,128)(2,1)S(1)}, bf16[3,512,256]{2,1,0:T(8,128)(2,1)S(1)}, u32[]{:S(2)}, u32[]{:S(2)}) collective-permute-start(bf16[3,512,256]{2,1,0:T(8,128)(2,1)S(1)} %shard_map.28.refs_0_), channel_id=1, source_target_pairs={{0,32},{1,97},{32,64},{33,1},{64,96},{65,33},{96,0},{97,65},{2,34}... | collective-permute-start | bytes 2359304 | tf_op jit(solution)/shard_map/ppermute | solution.py:31
  15.1 17.1 %collective-permute-start.6 = (bf16[2,4,3,16,512]{4,3,2,1,0:T(8,128)(2,1)S(1)}, bf16[2,4,3,16,512]{4,3,2,1,0:T(8,128)(2,1)S(1)}, u32[]{:S(2)}, u32[]{:S(2)}) collective-permute-start(bf16[2,4,3,16,512]{4,3,2,1,0:T(8,128)(2,1)S(1)} %pad_maximum_fusion.6), channel_id=1, source_target_pairs={{0,8},{1,25},{8,16},{9,1},{16,24},{17,9},{24,0},{25,17},{2,10},{3,... | collective-permute-start | bytes 1179656 | tf_op jit(solution)/shard_map/ppermute | solution.py:31
  17.8 14.4 %collective-permute-start.7 = (bf16[2,4,3,16,512]{4,3,2,1,0:T(8,128)(2,1)S(1)}, bf16[2,4,3,16,512]{4,3,2,1,0:T(8,128)(2,1)S(1)}, u32[]{:S(2)}, u32[]{:S(2)}) collective-permute-start(bf16[2,4,3,16,512]{4,3,2,1,0:T(8,128)(2,1)S(1)} %pad_maximum_fusion.6), channel_id=1, source_target_pairs={{0,24},{1,9},{8,0},{9,17},{16,8},{17,25},{24,16},{25,1},{2,26},{3,... | collective-permute-start | bytes 1179656 | tf_op jit(solution)/shard_map/ppermute | solution.py:31
  17.8 14.3 %collective-permute-start.4 = (bf16[4,3,16,512]{3,2,1,0:T(8,128)(2,1)S(1)}, bf16[4,3,16,512]{3,2,1,0:T(8,128)(2,1)S(1)}, u32[]{:S(2)}, u32[]{:S(2)}) collective-permute-start(bf16[4,3,16,512]{3,2,1,0:T(8,128)(2,1)S(1)} %slice_bitcast_fusion), channel_id=1, source_target_pairs={{0,2},{1,7},{2,4},{3,1},{4,6},{5,3},{6,0},{7,5},{8,10},{9,15},{10,... | collective-permute-start | bytes 589832 | tf_op jit(solution)/shard_map/ppermute | solution.py:31
  23.9 8.2 %collective-permute-start.5 = (bf16[4,3,16,512]{3,2,1,0:T(8,128)(2,1)S(1)}, bf16[4,3,16,512]{3,2,1,0:T(8,128)(2,1)S(1)}, u32[]{:S(2)}, u32[]{:S(2)}) collective-permute-start(bf16[4,3,16,512]{3,2,1,0:T(8,128)(2,1)S(1)} %slice_bitcast_fusion), channel_id=1, source_target_pairs={{0,6},{1,3},{2,0},{3,5},{4,2},{5,7},{6,4},{7,1},{8,14},{9,11},{10,... | collective-permute-start | bytes 589832 | tf_op jit(solution)/shard_map/ppermute | solution.py:31
  32.2 10.3 %collective-permute-start.10 = (bf16[2,4,3,16,512]{4,3,2,1,0:T(8,128)(2,1)S(1)}, bf16[2,4,3,16,512]{4,3,2,1,0:T(8,128)(2,1)S(1)}, u32[]{:S(2)}, u32[]{:S(2)}) collective-permute-start(bf16[2,4,3,16,512]{4,3,2,1,0:T(8,128)(2,1)S(1)} %collective-permute-done.6), channel_id=1, source_target_pairs={{0,8},{1,25},{8,16},{9,1},{16,24},{17,9},{24,0},{25,17},{2,10},{3,... | collective-permute-start | bytes 1179656 | tf_op jit(solution)/shard_map/ppermute | solution.py:31
  36.7 5.8 %collective-permute-start.9 = (bf16[4,3,16,512]{3,2,1,0:T(8,128)(2,1)S(1)}, bf16[4,3,16,512]{3,2,1,0:T(8,128)(2,1)S(1)}, u32[]{:S(2)}, u32[]{:S(2)}) collective-permute-start(bf16[4,3,16,512]{3,2,1,0:T(8,128)(2,1)S(1)} %collective-permute-done.4), channel_id=1, source_target_pairs={{0,2},{1,7},{2,4},{3,1},{4,6},{5,3},{6,0},{7,5},{8,10},{9,15},{10,... | collective-permute-start | bytes 589832 | tf_op jit(solution)/shard_map/ppermute | solution.py:31
  39.1 19.8 %collective-permute-start.15 = (bf16[3,512,256]{2,1,0:T(8,128)(2,1)S(1)}, bf16[3,512,256]{2,1,0:T(8,128)(2,1)S(1)}, u32[]{:S(2)}, u32[]{:S(2)}) collective-permute-start(bf16[3,512,256]{2,1,0:T(8,128)(2,1)S(1)} %shard_map.28.refs_0_), channel_id=1, source_target_pairs={{0,96},{1,33},{32,0},{33,65},{64,32},{65,97},{96,64},{97,1},{2,98}... | collective-permute-start | bytes 2359304 | tf_op jit(solution)/shard_map/ppermute | solution.py:31
  42.5 16.5 %collective-permute-start.11 = (bf16[3,4,3,16,512]{4,3,2,1,0:T(8,128)(2,1)S(1)}, bf16[3,4,3,16,512]{4,3,2,1,0:T(8,128)(2,1)S(1)}, u32[]{:S(2)}, u32[]{:S(2)}) collective-permute-start(bf16[3,4,3,16,512]{4,3,2,1,0:T(8,128)(2,1)S(1)} %pad_maximum_fusion.3), channel_id=1, source_target_pairs={{0,8},{1,25},{8,16},{9,1},{16,24},{17,9},{24,0},{25,17},{2,10},{3,... | collective-permute-start | bytes 1769480 | tf_op jit(solution)/shard_map/ppermute | solution.py:31
  45.0 15.9 %collective-permute-start.12 = (bf16[3,4,3,16,512]{4,3,2,1,0:T(8,128)(2,1)S(1)}, bf16[3,4,3,16,512]{4,3,2,1,0:T(8,128)(2,1)S(1)}, u32[]{:S(2)}, u32[]{:S(2)}) collective-permute-start(bf16[3,4,3,16,512]{4,3,2,1,0:T(8,128)(2,1)S(1)} %pad_maximum_fusion.3), channel_id=1, source_target_pairs={{0,24},{1,9},{8,0},{9,17},{16,8},{17,25},{24,16},{25,1},{2,26},{3,... | collective-permute-start | bytes 1769480 | tf_op jit(solution)/shard_map/ppermute | solution.py:31
  45.1 7.5 %collective-permute-start.13 = (bf16[4,3,16,512]{3,2,1,0:T(8,128)(2,1)S(1)}, bf16[4,3,16,512]{3,2,1,0:T(8,128)(2,1)S(1)}, u32[]{:S(2)}, u32[]{:S(2)}) collective-permute-start(bf16[4,3,16,512]{3,2,1,0:T(8,128)(2,1)S(1)} %get-tuple-element.104), channel_id=1, source_target_pairs={{0,2},{1,7},{2,4},{3,1},{4,6},{5,3},{6,0},{7,5},{8,10},{9,15},{10,... | collective-permute-start | bytes 589832 | tf_op jit(solution)/shard_map/ppermute | solution.py:31
  48.9 10.0 %collective-permute-start.14 = (bf16[4,3,16,512]{3,2,1,0:T(8,128)(2,1)S(1)}, bf16[4,3,16,512]{3,2,1,0:T(8,128)(2,1)S(1)}, u32[]{:S(2)}, u32[]{:S(2)}) collective-permute-start(bf16[4,3,16,512]{3,2,1,0:T(8,128)(2,1)S(1)} %get-tuple-element.104), channel_id=1, source_target_pairs={{0,6},{1,3},{2,0},{3,5},{4,2},{5,7},{6,4},{7,1},{8,14},{9,11},{10,... | collective-permute-start | bytes 589832 | tf_op jit(solution)/shard_map/ppermute | solution.py:31
  61.4 12.3 %collective-permute-start.17 = (bf16[3,4,4,3,16,512]{5,4,3,2,1,0:T(8,128)(2,1)S(1)}, bf16[3,4,4,3,16,512]{5,4,3,2,1,0:T(8,128)(2,1)S(1)}, u32[]{:S(2)}, u32[]{:S(2)}) collective-permute-start(bf16[3,4,4,3,16,512]{5,4,3,2,1,0:T(8,128)(2,1)S(1)} %pad_maximum_fusion.refs_3_.refs_1_), channel_id=1, source_target_pairs={{0,1},{1,0},{2,3},{3,2},{4,5},{5,4},{6,7},{7,6},{8,9},{9,8},{10,11... | collective-permute-start | bytes 7077896 | tf_op jit(solution)/shard_map/ppermute | solution.py:22
  61.9 9.0 %collective-permute-start.18 = (bf16[3,4,3,16,512]{4,3,2,1,0:T(8,128)(2,1)S(1)}, bf16[3,4,3,16,512]{4,3,2,1,0:T(8,128)(2,1)S(1)}, u32[]{:S(2)}, u32[]{:S(2)}) collective-permute-start(bf16[3,4,3,16,512]{4,3,2,1,0:T(8,128)(2,1)S(1)} %collective-permute-done.11), channel_id=1, source_target_pairs={{0,8},{1,25},{8,16},{9,1},{16,24},{17,9},{24,0},{25,17},{2,10},{3,... | collective-permute-start | bytes 1769480 | tf_op jit(solution)/shard_map/ppermute | solution.py:31
  62.6 11.1 %collective-permute-start.19 = (bf16[3,512,256]{2,1,0:T(8,128)(2,1)S(1)}, bf16[3,512,256]{2,1,0:T(8,128)(2,1)S(1)}, u32[]{:S(2)}, u32[]{:S(2)}) collective-permute-start(bf16[3,512,256]{2,1,0:T(8,128)(2,1)S(1)} %collective-permute-done.8.refs_1_), channel_id=1, source_target_pairs={{0,32},{1,97},{32,64},{33,1},{64,96},{65,33},{96,0},{97,65},{2,34}... | collective-permute-start | bytes 2359304 | tf_op jit(solution)/shard_map/ppermute | solution.py:31
  63.8 9.1 %collective-permute-start.16 = (bf16[4,3,16,512]{3,2,1,0:T(8,128)(2,1)S(1)}, bf16[4,3,16,512]{3,2,1,0:T(8,128)(2,1)S(1)}, u32[]{:S(2)}, u32[]{:S(2)}) collective-permute-start(bf16[4,3,16,512]{3,2,1,0:T(8,128)(2,1)S(1)} %collective-permute-done.13), channel_id=1, source_target_pairs={{0,2},{1,7},{2,4},{3,1},{4,6},{5,3},{6,0},{7,5},{8,10},{9,15},{10,... | collective-permute-start | bytes 589832 | tf_op jit(solution)/shard_map/ppermute | solution.py:31
  74.0 6.3 %collective-permute-start.21 = (bf16[2,4,4,3,16,512]{5,4,3,2,1,0:T(8,128)(2,1)S(1)}, bf16[2,4,4,3,16,512]{5,4,3,2,1,0:T(8,128)(2,1)S(1)}, u32[]{:S(2)}, u32[]{:S(2)}) collective-permute-start(bf16[2,4,4,3,16,512]{5,4,3,2,1,0:T(8,128)(2,1)S(1)} %pad_maximum_fusion.1.refs_4_), channel_id=1, source_target_pairs={{0,1},{1,0},{2,3},{3,2},{4,5},{5,4},{6,7},{7,6},{8,9},{9,8},{10,11... | collective-permute-start | bytes 4718600 | tf_op jit(solution)/shard_map/ppermute | solution.py:22
  75.7 18.0 %collective-permute-start.22 = (bf16[3,4,3,16,512]{4,3,2,1,0:T(8,128)(2,1)S(1)}, bf16[3,4,3,16,512]{4,3,2,1,0:T(8,128)(2,1)S(1)}, u32[]{:S(2)}, u32[]{:S(2)}) collective-permute-start(bf16[3,4,3,16,512]{4,3,2,1,0:T(8,128)(2,1)S(1)} %pad_maximum_fusion.4), channel_id=1, source_target_pairs={{0,8},{1,25},{8,16},{9,1},{16,24},{17,9},{24,0},{25,17},{2,10},{3,... | collective-permute-start | bytes 1769480 | tf_op jit(solution)/shard_map/ppermute | solution.py:31
  78.7 15.0 %collective-permute-start.23 = (bf16[3,4,3,16,512]{4,3,2,1,0:T(8,128)(2,1)S(1)}, bf16[3,4,3,16,512]{4,3,2,1,0:T(8,128)(2,1)S(1)}, u32[]{:S(2)}, u32[]{:S(2)}) collective-permute-start(bf16[3,4,3,16,512]{4,3,2,1,0:T(8,128)(2,1)S(1)} %pad_maximum_fusion.4), channel_id=1, source_target_pairs={{0,24},{1,9},{8,0},{9,17},{16,8},{17,25},{24,16},{25,1},{2,26},{3,... | collective-permute-start | bytes 1769480 | tf_op jit(solution)/shard_map/ppermute | solution.py:31
  80.2 13.6 %collective-permute-start.20 = (f16[528,512]{1,0:T(8,128)(2,1)S(1)}, f16[528,512]{1,0:T(8,128)(2,1)S(1)}, u32[]{:S(2)}, u32[]{:S(2)}) collective-permute-start(f16[528,512]{1,0:T(8,128)(2,1)S(1)} %convert_element_type.15), channel_id=1, source_target_pairs={{0,128},{128,0},{1,129},{129,1},{2,130},{130,2},{3,131},{131,3},{4... | collective-permute-start | bytes 1622024 | tf_op jit(solution)/shard_map/ppermute | solution.py:22
  93.9 16.2 %collective-permute-start.27 = (bf16[9,4,3,16,512]{4,3,2,1,0:T(8,128)(2,1)S(1)}, bf16[9,4,3,16,512]{4,3,2,1,0:T(8,128)(2,1)S(1)}, u32[]{:S(2)}, u32[]{:S(2)}) collective-permute-start(bf16[9,4,3,16,512]{4,3,2,1,0:T(8,128)(2,1)S(1)} %slice_dynamic-update-slice_fusion.refs_5_), channel_id=1, source_target_pairs={{0,1},{1,0},{2,3},{3,2},{4,5},{5,4},{6,7},{7,6},{8,9},{9,8},{10,11... | collective-permute-start | bytes 5308424 | tf_op jit(solution)/shard_map/ppermute | solution.py:22
  95.2 9.1 %collective-permute-start.25 = (bf16[3,4,3,16,512]{4,3,2,1,0:T(8,128)(2,1)S(1)}, bf16[3,4,3,16,512]{4,3,2,1,0:T(8,128)(2,1)S(1)}, u32[]{:S(2)}, u32[]{:S(2)}) collective-permute-start(bf16[3,4,3,16,512]{4,3,2,1,0:T(8,128)(2,1)S(1)} %collective-permute-done.22), channel_id=1, source_target_pairs={{0,8},{1,25},{8,16},{9,1},{16,24},{17,9},{24,0},{25,17},{2,10},{3,... | collective-permute-start | bytes 1769480 | tf_op jit(solution)/shard_map/ppermute | solution.py:31
  97.6 12.4 %collective-permute-start.24 = (f16[528,512]{1,0:T(8,128)(2,1)S(1)}, f16[528,512]{1,0:T(8,128)(2,1)S(1)}, u32[]{:S(2)}, u32[]{:S(2)}) collective-permute-start(f16[528,512]{1,0:T(8,128)(2,1)S(1)} %convert_element_type.16), channel_id=1, source_target_pairs={{0,128},{128,0},{1,129},{129,1},{2,130},{130,2},{3,131},{131,3},{4... | collective-permute-start | bytes 1622024 | tf_op jit(solution)/shard_map/ppermute | solution.py:22
  104.3 5.8 %collective-permute-start.28 = (bf16[3,4,3,16,512]{4,3,2,1,0:T(8,128)(2,1)S(1)}, bf16[3,4,3,16,512]{4,3,2,1,0:T(8,128)(2,1)S(1)}, u32[]{:S(2)}, u32[]{:S(2)}) collective-permute-start(bf16[3,4,3,16,512]{4,3,2,1,0:T(8,128)(2,1)S(1)} %collective-permute-done.25.refs_6_), channel_id=1, source_target_pairs={{0,1},{1,0},{2,3},{3,2},{4,5},{5,4},{6,7},{7,6},{8,9},{9,8},{10,11... | collective-permute-start | bytes 1769480 | tf_op jit(solution)/shard_map/ppermute | solution.py:22
  110.0 2.5 %collective-permute-start.26 = (f32[16,128]{1,0:T(8,128)S(1)}, f32[16,128]{1,0:T(8,128)S(1)}, u32[]{:S(2)}, u32[]{:S(2)}) collective-permute-start(f32[16,128]{1,0:T(8,128)S(1)} %slice_convert_fusion), channel_id=1, source_target_pairs={{0,1},{1,0},{2,3},{3,2},{4,5},{5,4},{6,7},{7,6},{8,9},{9,8},{10,11... | collective-permute-start | bytes 24584 | tf_op jit(solution)/shard_map/ppermute | solution.py:22

commit v6 on v5

--- a/solution.py
+++ b/solution.py
@@ -83,6 +83,7 @@
         grads, (before, *_, out, total, turned, sem) = refs[:3], refs[3:]
     else:
         grads, sent, total = refs[:count], *refs[-2:]
+        total = sent if more == "before" else total
     half = total.shape[1]
     if last:
         back = jnp.exp2(before[-8:, :][:1] - SCALE)
@@ -119,9 +120,7 @@
     if last:
         where = 1 - core[0] if swapped else core[0]
         write_out(total, turned, out, sem, where, seqs)
-    elif more == "before":
-        sent[...] = total[...]
-    else:
+    elif more != "before":
         peak = jnp.max(total[...], axis=(0, 1), keepdims=True)
         exponent = jnp.floor(jnp.log2(jnp.maximum(peak, jnp.float32(1e-30))))
         sent[: total.shape[0], :] = total[...] * jnp.exp2(SCALE - exponent)

time: 114 us -> 114 us (level)
  no operation moved by 1% of the time
where the time goes in v6:
time: 114 us
  waiting for transfers between devices  50.9 us (45%)
  starting transfers between devices  45.7 us (40%)
  Pallas kernels  13.7 us (12%)
  other arithmetic  1.59 us (1%)
  local copies, waits for them, and re-layouts  1.5 us (1%)
    ppermute x21, waiting for transfers between devices, send(): return lax.ppermute(value, (axis, 'core'), pairs)  39.1 us
    ppermute x21, starting transfers between devices, send(): return lax.ppermute(value, (axis, 'core'), pairs)  36.5 us
    ppermute x8, waiting for transfers between devices, swap(): return lax.ppermute(value, axis, [(0, 1), (1, 0)])  11.8 us
    pallas_call x5, Pallas kernels, add_side(): pl.pallas_call(functools.partial(square_sum, seqs, table, swapped, last,...  11.6 us
    ppermute x8, starting transfers between devices, swap(): return lax.ppermute(value, axis, [(0, 1), (1, 0)])  9.19 us
  transfers between devices with their start and end apart: 29, of which 12 were waited for; matrix products, arithmetic and copies ran while one was open for 1% of the time, Pallas kernels for 11%

profile of v6, /device:TPU:1, one launch (start us, length us, event | category | flops | bytes accessed | tf_op | source)
XLA Modules:
  0.0 113.9 jit_solution(11383054071003261992)
XLA Ops:
  0.0 1.1 constant_dynamic-slice_fusion.1
  1.1 3.3 %collective-permute-start = (bf16[4,2,3,8,512]{4,3,2,0,1:T(8,128)(2,1)S(1)}, bf16[4,2,3,8,512]{4,3,2,0,1:T(8,128)(2,1)S(1)}, u32[]{:S(2)}, u32[]{:S(2)}) collective-permute-start(bf16[4,2,3,8,512]{4,3,2,0,1:T(8,128)(2,1)S(1)} %bitcast.74), channel_id=1, source_target_pairs={{0,1},{1,0},{2,3},{3,2},{4,5},{5,4},{6,7},{7,6},{8,9},{9,8},{10,11... | collective-permute-start | bytes 589832 | tf_op jit(solution)/shard_map/ppermute | solution.py:22
  7.0 2.4 %collective-permute-start.1 = (bf16[2,3,16,512]{3,2,1,0:T(8,128)(2,1)S(1)}, bf16[2,3,16,512]{3,2,1,0:T(8,128)(2,1)S(1)}, u32[]{:S(2)}, u32[]{:S(2)}) collective-permute-start(bf16[2,3,16,512]{3,2,1,0:T(8,128)(2,1)S(1)} %get-tuple-element.109), channel_id=1, source_target_pairs={{0,32},{1,97},{32,64},{33,1},{64,96},{65,33},{96,0},{97,65},{2,34}... | collective-permute-start | bytes 294920 | tf_op jit(solution)/shard_map/ppermute | solution.py:31
  11.2 2.0 %collective-permute-done.2 = bf16[2,3,16,512]{3,2,1,0:T(8,128)(2,1)S(1)} collective-permute-done((bf16[2,3,16,512]{3,2,1,0:T(8,128)(2,1)S(1)}, bf16[2,3,16,512]{3,2,1,0:T(8,128)(2,1)S(1)}, u32[]{:S(2)}, u32[]{:S(2)}) %collective-permute-start.2) | collective-permute-done | bytes 98336 | tf_op jit(solution)/shard_map/ppermute | solution.py:31
  13.4 1.7 %collective-permute-start.8 = (bf16[3,512,256]{2,1,0:T(8,128)(2,1)S(1)}, bf16[3,512,256]{2,1,0:T(8,128)(2,1)S(1)}, u32[]{:S(2)}, u32[]{:S(2)}) collective-permute-start(bf16[3,512,256]{2,1,0:T(8,128)(2,1)S(1)} %shard_map.28.refs_0_), channel_id=1, source_target_pairs={{0,32},{1,97},{32,64},{33,1},{64,96},{65,33},{96,0},{97,65},{2,34}... | collective-permute-start | bytes 2359304 | tf_op jit(solution)/shard_map/ppermute | solution.py:31
  15.1 2.7 %collective-permute-start.6 = (bf16[2,4,3,16,512]{4,3,2,1,0:T(8,128)(2,1)S(1)}, bf16[2,4,3,16,512]{4,3,2,1,0:T(8,128)(2,1)S(1)}, u32[]{:S(2)}, u32[]{:S(2)}) collective-permute-start(bf16[2,4,3,16,512]{4,3,2,1,0:T(8,128)(2,1)S(1)} %pad_maximum_fusion.6), channel_id=1, source_target_pairs={{0,8},{1,25},{8,16},{9,1},{16,24},{17,9},{24,0},{25,17},{2,10},{3,... | collective-permute-start | bytes 1179656 | tf_op jit(solution)/shard_map/ppermute | solution.py:31
  17.8 6.1 %collective-permute-start.4 = (bf16[4,3,16,512]{3,2,1,0:T(8,128)(2,1)S(1)}, bf16[4,3,16,512]{3,2,1,0:T(8,128)(2,1)S(1)}, u32[]{:S(2)}, u32[]{:S(2)}) collective-permute-start(bf16[4,3,16,512]{3,2,1,0:T(8,128)(2,1)S(1)} %slice_bitcast_fusion), channel_id=1, source_target_pairs={{0,2},{1,7},{2,4},{3,1},{4,6},{5,3},{6,0},{7,5},{8,10},{9,15},{10,... | collective-permute-start | bytes 589832 | tf_op jit(solution)/shard_map/ppermute | solution.py:31
  23.9 8.2 %collective-permute-done.4 = bf16[4,3,16,512]{3,2,1,0:T(8,128)(2,1)S(1)} collective-permute-done((bf16[4,3,16,512]{3,2,1,0:T(8,128)(2,1)S(1)}, bf16[4,3,16,512]{3,2,1,0:T(8,128)(2,1)S(1)}, u32[]{:S(2)}, u32[]{:S(2)}) %collective-permute-start.4) | collective-permute-done | bytes 196640 | tf_op jit(solution)/shard_map/ppermute | solution.py:31
  32.2 4.5 %collective-permute-start.10 = (bf16[2,4,3,16,512]{4,3,2,1,0:T(8,128)(2,1)S(1)}, bf16[2,4,3,16,512]{4,3,2,1,0:T(8,128)(2,1)S(1)}, u32[]{:S(2)}, u32[]{:S(2)}) collective-permute-start(bf16[2,4,3,16,512]{4,3,2,1,0:T(8,128)(2,1)S(1)} %collective-permute-done.6), channel_id=1, source_target_pairs={{0,8},{1,25},{8,16},{9,1},{16,24},{17,9},{24,0},{25,17},{2,10},{3,... | collective-permute-start | bytes 1179656 | tf_op jit(solution)/shard_map/ppermute | solution.py:31
  36.7 2.4 %collective-permute-start.9 = (bf16[4,3,16,512]{3,2,1,0:T(8,128)(2,1)S(1)}, bf16[4,3,16,512]{3,2,1,0:T(8,128)(2,1)S(1)}, u32[]{:S(2)}, u32[]{:S(2)}) collective-permute-start(bf16[4,3,16,512]{3,2,1,0:T(8,128)(2,1)S(1)} %collective-permute-done.4), channel_id=1, source_target_pairs={{0,2},{1,7},{2,4},{3,1},{4,6},{5,3},{6,0},{7,5},{8,10},{9,15},{10,... | collective-permute-start | bytes 589832 | tf_op jit(solution)/shard_map/ppermute | solution.py:31
  39.1 3.3 %collective-permute-done.9 = bf16[4,3,16,512]{3,2,1,0:T(8,128)(2,1)S(1)} collective-permute-done((bf16[4,3,16,512]{3,2,1,0:T(8,128)(2,1)S(1)}, bf16[4,3,16,512]{3,2,1,0:T(8,128)(2,1)S(1)}, u32[]{:S(2)}, u32[]{:S(2)}) %collective-permute-start.9) | collective-permute-done | bytes 196640 | tf_op jit(solution)/shard_map/ppermute | solution.py:31
  42.5 2.4 %collective-permute-start.11 = (bf16[3,4,3,16,512]{4,3,2,1,0:T(8,128)(2,1)S(1)}, bf16[3,4,3,16,512]{4,3,2,1,0:T(8,128)(2,1)S(1)}, u32[]{:S(2)}, u32[]{:S(2)}) collective-permute-start(bf16[3,4,3,16,512]{4,3,2,1,0:T(8,128)(2,1)S(1)} %pad_maximum_fusion.3), channel_id=1, source_target_pairs={{0,8},{1,25},{8,16},{9,1},{16,24},{17,9},{24,0},{25,17},{2,10},{3,... | collective-permute-start | bytes 1769480 | tf_op jit(solution)/shard_map/ppermute | solution.py:31
  45.1 3.9 %collective-permute-start.13 = (bf16[4,3,16,512]{3,2,1,0:T(8,128)(2,1)S(1)}, bf16[4,3,16,512]{3,2,1,0:T(8,128)(2,1)S(1)}, u32[]{:S(2)}, u32[]{:S(2)}) collective-permute-start(bf16[4,3,16,512]{3,2,1,0:T(8,128)(2,1)S(1)} %get-tuple-element.104), channel_id=1, source_target_pairs={{0,2},{1,7},{2,4},{3,1},{4,6},{5,3},{6,0},{7,5},{8,10},{9,15},{10,... | collective-permute-start | bytes 589832 | tf_op jit(solution)/shard_map/ppermute | solution.py:31
  48.9 3.6 %collective-permute-done.13 = bf16[4,3,16,512]{3,2,1,0:T(8,128)(2,1)S(1)} collective-permute-done((bf16[4,3,16,512]{3,2,1,0:T(8,128)(2,1)S(1)}, bf16[4,3,16,512]{3,2,1,0:T(8,128)(2,1)S(1)}, u32[]{:S(2)}, u32[]{:S(2)}) %collective-permute-start.13) | collective-permute-done | bytes 196640 | tf_op jit(solution)/shard_map/ppermute | solution.py:31
  52.6 6.4 %collective-permute-done.14 = bf16[4,3,16,512]{3,2,1,0:T(8,128)(2,1)S(1)} collective-permute-done((bf16[4,3,16,512]{3,2,1,0:T(8,128)(2,1)S(1)}, bf16[4,3,16,512]{3,2,1,0:T(8,128)(2,1)S(1)}, u32[]{:S(2)}, u32[]{:S(2)}) %collective-permute-start.14) | collective-permute-done | bytes 196640 | tf_op jit(solution)/shard_map/ppermute | solution.py:31
  59.0 1.9 %collective-permute-done.12 = bf16[3,4,3,16,512]{4,3,2,1,0:T(8,128)(2,1)S(1)} collective-permute-done((bf16[3,4,3,16,512]{4,3,2,1,0:T(8,128)(2,1)S(1)}, bf16[3,4,3,16,512]{4,3,2,1,0:T(8,128)(2,1)S(1)}, u32[]{:S(2)}, u32[]{:S(2)}) %collective-permute-start.12) | collective-permute-done | bytes 589856 | tf_op jit(solution)/shard_map/ppermute | solution.py:31
  62.6 1.3 %collective-permute-start.19 = (bf16[3,512,256]{2,1,0:T(8,128)(2,1)S(1)}, bf16[3,512,256]{2,1,0:T(8,128)(2,1)S(1)}, u32[]{:S(2)}, u32[]{:S(2)}) collective-permute-start(bf16[3,512,256]{2,1,0:T(8,128)(2,1)S(1)} %collective-permute-done.8.refs_1_), channel_id=1, source_target_pairs={{0,32},{1,97},{32,64},{33,1},{64,96},{65,33},{96,0},{97,65},{2,34}... | collective-permute-start | bytes 2359304 | tf_op jit(solution)/shard_map/ppermute | solution.py:31
  63.8 1.8 %collective-permute-start.16 = (bf16[4,3,16,512]{3,2,1,0:T(8,128)(2,1)S(1)}, bf16[4,3,16,512]{3,2,1,0:T(8,128)(2,1)S(1)}, u32[]{:S(2)}, u32[]{:S(2)}) collective-permute-start(bf16[4,3,16,512]{3,2,1,0:T(8,128)(2,1)S(1)} %collective-permute-done.13), channel_id=1, source_target_pairs={{0,2},{1,7},{2,4},{3,1},{4,6},{5,3},{6,0},{7,5},{8,10},{9,15},{10,... | collective-permute-start | bytes 589832 | tf_op jit(solution)/shard_map/ppermute | solution.py:31
  65.6 5.3 %collective-permute-done.18 = bf16[3,4,3,16,512]{4,3,2,1,0:T(8,128)(2,1)S(1)} collective-permute-done((bf16[3,4,3,16,512]{4,3,2,1,0:T(8,128)(2,1)S(1)}, bf16[3,4,3,16,512]{4,3,2,1,0:T(8,128)(2,1)S(1)}, u32[]{:S(2)}, u32[]{:S(2)}) %collective-permute-start.18) | collective-permute-done | bytes 589856 | tf_op jit(solution)/shard_map/ppermute | solution.py:31
  71.1 1.7 %shard_map.29.refs_3_ = f32[512,512]{1,0:T(8,128)S(1)} custom-call(s32[1]{0:T(128)} %bitcast.core, bf16[3,512,256]{2,1,0:T(8,128)(2,1)S(1)} %shard_map.28.refs_0_, bf16[3,512,256]{2,1,0:T(8,128)(2,1)S(1)} %collective-permute-done.8.refs_1_, bf16[3,512,256]{2,1,0:T(8,128)(2,1)S(1)} %collective-permute-done.15.refs_2_, ...), custom_call_target="tpu_custom_call" | custom-call | flops 1207959552 | bytes 8388608 | tf_op jit(solution)/shard_map/pallas_call | solution.py:167
  74.0 1.7 %collective-permute-start.21 = (bf16[2,4,4,3,16,512]{5,4,3,2,1,0:T(8,128)(2,1)S(1)}, bf16[2,4,4,3,16,512]{5,4,3,2,1,0:T(8,128)(2,1)S(1)}, u32[]{:S(2)}, u32[]{:S(2)}) collective-permute-start(bf16[2,4,4,3,16,512]{5,4,3,2,1,0:T(8,128)(2,1)S(1)} %pad_maximum_fusion.1.refs_4_), channel_id=1, source_target_pairs={{0,1},{1,0},{2,3},{3,2},{4,5},{5,4},{6,7},{7,6},{8,9},{9,8},{10,11... | collective-permute-start | bytes 4718600 | tf_op jit(solution)/shard_map/ppermute | solution.py:22
  75.7 3.0 %collective-permute-start.22 = (bf16[3,4,3,16,512]{4,3,2,1,0:T(8,128)(2,1)S(1)}, bf16[3,4,3,16,512]{4,3,2,1,0:T(8,128)(2,1)S(1)}, u32[]{:S(2)}, u32[]{:S(2)}) collective-permute-start(bf16[3,4,3,16,512]{4,3,2,1,0:T(8,128)(2,1)S(1)} %pad_maximum_fusion.4), channel_id=1, source_target_pairs={{0,8},{1,25},{8,16},{9,1},{16,24},{17,9},{24,0},{25,17},{2,10},{3,... | collective-permute-start | bytes 1769480 | tf_op jit(solution)/shard_map/ppermute | solution.py:31
  78.7 1.3 %shard_map.30 = f32[528,512]{1,0:T(8,128)S(1)} custom-call(s32[1]{0:T(128)} %bitcast.core, bf16[3,512,256]{2,1,0:T(8,128)(2,1)S(1)} %collective-permute-done.19.refs_0_.refs_3_, bf16[3,4,4,3,16,512]{5,4,3,2,1,0:T(8,128)(2,1)S(1)} %pad_maximum_fusion.refs_3_.refs_1_, bf16[4,4,3,16,512]{4,3,2,1,0:T(8,128)(2,1)S(1)} %get-tuple-element.102.refs_4_.refs_2_, ...), custom_call_target="tpu_custom_call" | custom-call | flops 402653184 | bytes 8388608 | tf_op jit(solution)/shard_map/pallas_call | solution.py:167
  80.3 2.8 %shard_map.31 = f32[528,512]{1,0:T(8,128)S(1)} custom-call(s32[1]{0:T(128)} %bitcast.core, bf16[3,512,256]{2,1,0:T(8,128)(2,1)S(1)} %shard_map.28.refs_0_, bf16[3,512,256]{2,1,0:T(8,128)(2,1)S(1)} %collective-permute-done.8.refs_1_, bf16[3,512,256]{2,1,0:T(8,128)(2,1)S(1)} %collective-permute-done.15.refs_2_, ...), custom_call_target="tpu_custom_call" | custom-call | flops 1610612736 | bytes 8388608 | tf_op jit(solution)/shard_map/pallas_call | solution.py:167
  83.1 10.7 %collective-permute-done.20 = f16[528,512]{1,0:T(8,128)(2,1)S(1)} collective-permute-done((f16[528,512]{1,0:T(8,128)(2,1)S(1)}, f16[528,512]{1,0:T(8,128)(2,1)S(1)}, u32[]{:S(2)}, u32[]{:S(2)}) %collective-permute-start.20) | collective-permute-done | bytes 540704 | tf_op jit(solution)/shard_map/ppermute | solution.py:22
  93.9 1.3 %collective-permute-start.27 = (bf16[9,4,3,16,512]{4,3,2,1,0:T(8,128)(2,1)S(1)}, bf16[9,4,3,16,512]{4,3,2,1,0:T(8,128)(2,1)S(1)}, u32[]{:S(2)}, u32[]{:S(2)}) collective-permute-start(bf16[9,4,3,16,512]{4,3,2,1,0:T(8,128)(2,1)S(1)} %slice_dynamic-update-slice_fusion.refs_5_), channel_id=1, source_target_pairs={{0,1},{1,0},{2,3},{3,2},{4,5},{5,4},{6,7},{7,6},{8,9},{9,8},{10,11... | collective-permute-start | bytes 5308424 | tf_op jit(solution)/shard_map/ppermute | solution.py:22
  95.2 2.2 %collective-permute-start.25 = (bf16[3,4,3,16,512]{4,3,2,1,0:T(8,128)(2,1)S(1)}, bf16[3,4,3,16,512]{4,3,2,1,0:T(8,128)(2,1)S(1)}, u32[]{:S(2)}, u32[]{:S(2)}) collective-permute-start(bf16[3,4,3,16,512]{4,3,2,1,0:T(8,128)(2,1)S(1)} %collective-permute-done.22), channel_id=1, source_target_pairs={{0,8},{1,25},{8,16},{9,1},{16,24},{17,9},{24,0},{25,17},{2,10},{3,... | collective-permute-start | bytes 1769480 | tf_op jit(solution)/shard_map/ppermute | solution.py:31
  97.7 6.6 %collective-permute-done.25.refs_6_ = bf16[3,4,3,16,512]{4,3,2,1,0:T(8,128)(2,1)S(1)} collective-permute-done((bf16[3,4,3,16,512]{4,3,2,1,0:T(8,128)(2,1)S(1)}, bf16[3,4,3,16,512]{4,3,2,1,0:T(8,128)(2,1)S(1)}, u32[]{:S(2)}, u32[]{:S(2)}) %collective-permute-start.25) | collective-permute-done | bytes 589856 | tf_op jit(solution)/shard_map/ppermute | solution.py:31
  104.3 2.1 %collective-permute-start.28 = (bf16[3,4,3,16,512]{4,3,2,1,0:T(8,128)(2,1)S(1)}, bf16[3,4,3,16,512]{4,3,2,1,0:T(8,128)(2,1)S(1)}, u32[]{:S(2)}, u32[]{:S(2)}) collective-permute-start(bf16[3,4,3,16,512]{4,3,2,1,0:T(8,128)(2,1)S(1)} %collective-permute-done.25.refs_6_), channel_id=1, source_target_pairs={{0,1},{1,0},{2,3},{3,2},{4,5},{5,4},{6,7},{7,6},{8,9},{9,8},{10,11... | collective-permute-start | bytes 1769480 | tf_op jit(solution)/shard_map/ppermute | solution.py:22
  106.5 3.4 %shard_map.32.given = f32[1024,512]{1,0:T(8,128)} custom-call(s32[1]{0:T(128)} %bitcast.core, bf16[3,512,256]{2,1,0:T(8,128)(2,1)S(1)} %shard_map.28.refs_0_, bf16[3,512,256]{2,1,0:T(8,128)(2,1)S(1)} %collective-permute-done.8.refs_1_, bf16[3,512,256]{2,1,0:T(8,128)(2,1)S(1)} %collective-permute-done.15.refs_2_, ...), custom_call_target="tpu_custom_call" | custom-call | flops 1610612736 | bytes 8388608 | tf_op jit(solution)/shard_map/pallas_call | solution.py:167
  110.1 2.3 %shard_map.33.given_total = f32[512,512]{1,0:T(8,128)S(1)} custom-call(s32[1]{0:T(128)} %bitcast.core, bf16[3,512,256]{2,1,0:T(8,128)(2,1)S(1)} %shard_map.28.refs_0_, bf16[3,512,256]{2,1,0:T(8,128)(2,1)S(1)} %collective-permute-done.8.refs_1_, bf16[3,512,256]{2,1,0:T(8,128)(2,1)S(1)} %collective-permute-done.15.refs_2_, ...), custom_call_target="tpu_custom_call" | custom-call | flops 1610612736 | bytes 8388608 | tf_op jit(solution)/shard_map/pallas_call | solution.py:167
  112.6 1.1 %shard_map.34 = f32[1024,512]{1,0:T(8,128)} custom-call(s32[1]{0:T(128)} %bitcast.core, f32[512,512]{1,0:T(8,128)S(1)} %shard_map.33.given_total, f32[528,512]{1,0:T(8,128)S(1)} %convert_element_type.19.before, f32[16,128]{1,0:T(8,128)S(1)} %collective-permute-done.26.token, f32[1024,512]{1,0:T(8,128)} %shard_map.32.given), custom_call_target="tpu_custom_call", output_to_operand_aliasing={{}: (4, {})} | custom-call | tf_op jit(solution)/shard_map/pallas_call | solution.py:189
  (66 shorter events, 8.5 us)
Async XLA Ops:
  0.0 9.5 %copy-start = (bf16[3,256,512]{2,1,0:T(8,128)(2,1)S(1)}, bf16[3,256,512]{2,1,0:T(8,128)(2,1)}, u32[]{:S(2)}) copy-start(bf16[3,256,512]{2,1,0:T(8,128)(2,1)} %acts.1) | copy-start | bytes 2359300
  1.1 4.4 %collective-permute-start = (bf16[4,2,3,8,512]{4,3,2,0,1:T(8,128)(2,1)S(1)}, bf16[4,2,3,8,512]{4,3,2,0,1:T(8,128)(2,1)S(1)}, u32[]{:S(2)}, u32[]{:S(2)}) collective-permute-start(bf16[4,2,3,8,512]{4,3,2,0,1:T(8,128)(2,1)S(1)} %bitcast.74), channel_id=1, source_target_pairs={{0,1},{1,0},{2,3},{3,2},{4,5},{5,4},{6,7},{7,6},{8,9},{9,8},{10,11... | collective-permute-start | bytes 589832 | tf_op jit(solution)/shard_map/ppermute | solution.py:22
  5.6 5.6 %collective-permute-start.3 = (bf16[2,3,16,512]{3,2,1,0:T(8,128)(2,1)S(1)}, bf16[2,3,16,512]{3,2,1,0:T(8,128)(2,1)S(1)}, u32[]{:S(2)}, u32[]{:S(2)}) collective-permute-start(bf16[2,3,16,512]{3,2,1,0:T(8,128)(2,1)S(1)} %get-tuple-element.111), channel_id=1, source_target_pairs={{0,64},{1,65},{32,96},{33,97},{64,0},{65,1},{96,32},{97,33},{2,66}... | collective-permute-start | bytes 294920 | tf_op jit(solution)/shard_map/ppermute | solution.py:31
  6.7 6.5 %collective-permute-start.2 = (bf16[2,3,16,512]{3,2,1,0:T(8,128)(2,1)S(1)}, bf16[2,3,16,512]{3,2,1,0:T(8,128)(2,1)S(1)}, u32[]{:S(2)}, u32[]{:S(2)}) collective-permute-start(bf16[2,3,16,512]{3,2,1,0:T(8,128)(2,1)S(1)} %get-tuple-element.110), channel_id=1, source_target_pairs={{0,96},{1,33},{32,0},{33,65},{64,32},{65,97},{96,64},{97,1},{2,98}... | collective-permute-start | bytes 294920 | tf_op jit(solution)/shard_map/ppermute | solution.py:31
  7.0 6.2 %collective-permute-start.1 = (bf16[2,3,16,512]{3,2,1,0:T(8,128)(2,1)S(1)}, bf16[2,3,16,512]{3,2,1,0:T(8,128)(2,1)S(1)}, u32[]{:S(2)}, u32[]{:S(2)}) collective-permute-start(bf16[2,3,16,512]{3,2,1,0:T(8,128)(2,1)S(1)} %get-tuple-element.109), channel_id=1, source_target_pairs={{0,32},{1,97},{32,64},{33,1},{64,96},{65,33},{96,0},{97,65},{2,34}... | collective-permute-start | bytes 294920 | tf_op jit(solution)/shard_map/ppermute | solution.py:31
  13.4 18.8 %collective-permute-start.8 = (bf16[3,512,256]{2,1,0:T(8,128)(2,1)S(1)}, bf16[3,512,256]{2,1,0:T(8,128)(2,1)S(1)}, u32[]{:S(2)}, u32[]{:S(2)}) collective-permute-start(bf16[3,512,256]{2,1,0:T(8,128)(2,1)S(1)} %shard_map.28.refs_0_), channel_id=1, source_target_pairs={{0,32},{1,97},{32,64},{33,1},{64,96},{65,33},{96,0},{97,65},{2,34}... | collective-permute-start | bytes 2359304 | tf_op jit(solution)/shard_map/ppermute | solution.py:31
  15.1 17.1 %collective-permute-start.6 = (bf16[2,4,3,16,512]{4,3,2,1,0:T(8,128)(2,1)S(1)}, bf16[2,4,3,16,512]{4,3,2,1,0:T(8,128)(2,1)S(1)}, u32[]{:S(2)}, u32[]{:S(2)}) collective-permute-start(bf16[2,4,3,16,512]{4,3,2,1,0:T(8,128)(2,1)S(1)} %pad_maximum_fusion.6), channel_id=1, source_target_pairs={{0,8},{1,25},{8,16},{9,1},{16,24},{17,9},{24,0},{25,17},{2,10},{3,... | collective-permute-start | bytes 1179656 | tf_op jit(solution)/shard_map/ppermute | solution.py:31
  17.8 14.4 %collective-permute-start.7 = (bf16[2,4,3,16,512]{4,3,2,1,0:T(8,128)(2,1)S(1)}, bf16[2,4,3,16,512]{4,3,2,1,0:T(8,128)(2,1)S(1)}, u32[]{:S(2)}, u32[]{:S(2)}) collective-permute-start(bf16[2,4,3,16,512]{4,3,2,1,0:T(8,128)(2,1)S(1)} %pad_maximum_fusion.6), channel_id=1, source_target_pairs={{0,24},{1,9},{8,0},{9,17},{16,8},{17,25},{24,16},{25,1},{2,26},{3,... | collective-permute-start | bytes 1179656 | tf_op jit(solution)/shard_map/ppermute | solution.py:31
  17.8 14.3 %collective-permute-start.4 = (bf16[4,3,16,512]{3,2,1,0:T(8,128)(2,1)S(1)}, bf16[4,3,16,512]{3,2,1,0:T(8,128)(2,1)S(1)}, u32[]{:S(2)}, u32[]{:S(2)}) collective-permute-start(bf16[4,3,16,512]{3,2,1,0:T(8,128)(2,1)S(1)} %slice_bitcast_fusion), channel_id=1, source_target_pairs={{0,2},{1,7},{2,4},{3,1},{4,6},{5,3},{6,0},{7,5},{8,10},{9,15},{10,... | collective-permute-start | bytes 589832 | tf_op jit(solution)/shard_map/ppermute | solution.py:31
  23.9 8.2 %collective-permute-start.5 = (bf16[4,3,16,512]{3,2,1,0:T(8,128)(2,1)S(1)}, bf16[4,3,16,512]{3,2,1,0:T(8,128)(2,1)S(1)}, u32[]{:S(2)}, u32[]{:S(2)}) collective-permute-start(bf16[4,3,16,512]{3,2,1,0:T(8,128)(2,1)S(1)} %slice_bitcast_fusion), channel_id=1, source_target_pairs={{0,6},{1,3},{2,0},{3,5},{4,2},{5,7},{6,4},{7,1},{8,14},{9,11},{10,... | collective-permute-start | bytes 589832 | tf_op jit(solution)/shard_map/ppermute | solution.py:31
  32.2 10.3 %collective-permute-start.10 = (bf16[2,4,3,16,512]{4,3,2,1,0:T(8,128)(2,1)S(1)}, bf16[2,4,3,16,512]{4,3,2,1,0:T(8,128)(2,1)S(1)}, u32[]{:S(2)}, u32[]{:S(2)}) collective-permute-start(bf16[2,4,3,16,512]{4,3,2,1,0:T(8,128)(2,1)S(1)} %collective-permute-done.6), channel_id=1, source_target_pairs={{0,8},{1,25},{8,16},{9,1},{16,24},{17,9},{24,0},{25,17},{2,10},{3,... | collective-permute-start | bytes 1179656 | tf_op jit(solution)/shard_map/ppermute | solution.py:31
  36.7 5.8 %collective-permute-start.9 = (bf16[4,3,16,512]{3,2,1,0:T(8,128)(2,1)S(1)}, bf16[4,3,16,512]{3,2,1,0:T(8,128)(2,1)S(1)}, u32[]{:S(2)}, u32[]{:S(2)}) collective-permute-start(bf16[4,3,16,512]{3,2,1,0:T(8,128)(2,1)S(1)} %collective-permute-done.4), channel_id=1, source_target_pairs={{0,2},{1,7},{2,4},{3,1},{4,6},{5,3},{6,0},{7,5},{8,10},{9,15},{10,... | collective-permute-start | bytes 589832 | tf_op jit(solution)/shard_map/ppermute | solution.py:31
  39.1 19.8 %collective-permute-start.15 = (bf16[3,512,256]{2,1,0:T(8,128)(2,1)S(1)}, bf16[3,512,256]{2,1,0:T(8,128)(2,1)S(1)}, u32[]{:S(2)}, u32[]{:S(2)}) collective-permute-start(bf16[3,512,256]{2,1,0:T(8,128)(2,1)S(1)} %shard_map.28.refs_0_), channel_id=1, source_target_pairs={{0,96},{1,33},{32,0},{33,65},{64,32},{65,97},{96,64},{97,1},{2,98}... | collective-permute-start | bytes 2359304 | tf_op jit(solution)/shard_map/ppermute | solution.py:31
  42.5 16.5 %collective-permute-start.11 = (bf16[3,4,3,16,512]{4,3,2,1,0:T(8,128)(2,1)S(1)}, bf16[3,4,3,16,512]{4,3,2,1,0:T(8,128)(2,1)S(1)}, u32[]{:S(2)}, u32[]{:S(2)}) collective-permute-start(bf16[3,4,3,16,512]{4,3,2,1,0:T(8,128)(2,1)S(1)} %pad_maximum_fusion.3), channel_id=1, source_target_pairs={{0,8},{1,25},{8,16},{9,1},{16,24},{17,9},{24,0},{25,17},{2,10},{3,... | collective-permute-start | bytes 1769480 | tf_op jit(solution)/shard_map/ppermute | solution.py:31
  45.0 15.9 %collective-permute-start.12 = (bf16[3,4,3,16,512]{4,3,2,1,0:T(8,128)(2,1)S(1)}, bf16[3,4,3,16,512]{4,3,2,1,0:T(8,128)(2,1)S(1)}, u32[]{:S(2)}, u32[]{:S(2)}) collective-permute-start(bf16[3,4,3,16,512]{4,3,2,1,0:T(8,128)(2,1)S(1)} %pad_maximum_fusion.3), channel_id=1, source_target_pairs={{0,24},{1,9},{8,0},{9,17},{16,8},{17,25},{24,16},{25,1},{2,26},{3,... | collective-permute-start | bytes 1769480 | tf_op jit(solution)/shard_map/ppermute | solution.py:31
  45.1 7.5 %collective-permute-start.13 = (bf16[4,3,16,512]{3,2,1,0:T(8,128)(2,1)S(1)}, bf16[4,3,16,512]{3,2,1,0:T(8,128)(2,1)S(1)}, u32[]{:S(2)}, u32[]{:S(2)}) collective-permute-start(bf16[4,3,16,512]{3,2,1,0:T(8,128)(2,1)S(1)} %get-tuple-element.104), channel_id=1, source_target_pairs={{0,2},{1,7},{2,4},{3,1},{4,6},{5,3},{6,0},{7,5},{8,10},{9,15},{10,... | collective-permute-start | bytes 589832 | tf_op jit(solution)/shard_map/ppermute | solution.py:31
  48.9 10.0 %collective-permute-start.14 = (bf16[4,3,16,512]{3,2,1,0:T(8,128)(2,1)S(1)}, bf16[4,3,16,512]{3,2,1,0:T(8,128)(2,1)S(1)}, u32[]{:S(2)}, u32[]{:S(2)}) collective-permute-start(bf16[4,3,16,512]{3,2,1,0:T(8,128)(2,1)S(1)} %get-tuple-element.104), channel_id=1, source_target_pairs={{0,6},{1,3},{2,0},{3,5},{4,2},{5,7},{6,4},{7,1},{8,14},{9,11},{10,... | collective-permute-start | bytes 589832 | tf_op jit(solution)/shard_map/ppermute | solution.py:31
  61.4 12.3 %collective-permute-start.17 = (bf16[3,4,4,3,16,512]{5,4,3,2,1,0:T(8,128)(2,1)S(1)}, bf16[3,4,4,3,16,512]{5,4,3,2,1,0:T(8,128)(2,1)S(1)}, u32[]{:S(2)}, u32[]{:S(2)}) collective-permute-start(bf16[3,4,4,3,16,512]{5,4,3,2,1,0:T(8,128)(2,1)S(1)} %pad_maximum_fusion.refs_3_.refs_1_), channel_id=1, source_target_pairs={{0,1},{1,0},{2,3},{3,2},{4,5},{5,4},{6,7},{7,6},{8,9},{9,8},{10,11... | collective-permute-start | bytes 7077896 | tf_op jit(solution)/shard_map/ppermute | solution.py:22
  61.9 9.0 %collective-permute-start.18 = (bf16[3,4,3,16,512]{4,3,2,1,0:T(8,128)(2,1)S(1)}, bf16[3,4,3,16,512]{4,3,2,1,0:T(8,128)(2,1)S(1)}, u32[]{:S(2)}, u32[]{:S(2)}) collective-permute-start(bf16[3,4,3,16,512]{4,3,2,1,0:T(8,128)(2,1)S(1)} %collective-permute-done.11), channel_id=1, source_target_pairs={{0,8},{1,25},{8,16},{9,1},{16,24},{17,9},{24,0},{25,17},{2,10},{3,... | collective-permute-start | bytes 1769480 | tf_op jit(solution)/shard_map/ppermute | solution.py:31
  62.6 11.1 %collective-permute-start.19 = (bf16[3,512,256]{2,1,0:T(8,128)(2,1)S(1)}, bf16[3,512,256]{2,1,0:T(8,128)(2,1)S(1)}, u32[]{:S(2)}, u32[]{:S(2)}) collective-permute-start(bf16[3,512,256]{2,1,0:T(8,128)(2,1)S(1)} %collective-permute-done.8.refs_1_), channel_id=1, source_target_pairs={{0,32},{1,97},{32,64},{33,1},{64,96},{65,33},{96,0},{97,65},{2,34}... | collective-permute-start | bytes 2359304 | tf_op jit(solution)/shard_map/ppermute | solution.py:31
  63.8 9.0 %collective-permute-start.16 = (bf16[4,3,16,512]{3,2,1,0:T(8,128)(2,1)S(1)}, bf16[4,3,16,512]{3,2,1,0:T(8,128)(2,1)S(1)}, u32[]{:S(2)}, u32[]{:S(2)}) collective-permute-start(bf16[4,3,16,512]{3,2,1,0:T(8,128)(2,1)S(1)} %collective-permute-done.13), channel_id=1, source_target_pairs={{0,2},{1,7},{2,4},{3,1},{4,6},{5,3},{6,0},{7,5},{8,10},{9,15},{10,... | collective-permute-start | bytes 589832 | tf_op jit(solution)/shard_map/ppermute | solution.py:31
  74.0 6.3 %collective-permute-start.21 = (bf16[2,4,4,3,16,512]{5,4,3,2,1,0:T(8,128)(2,1)S(1)}, bf16[2,4,4,3,16,512]{5,4,3,2,1,0:T(8,128)(2,1)S(1)}, u32[]{:S(2)}, u32[]{:S(2)}) collective-permute-start(bf16[2,4,4,3,16,512]{5,4,3,2,1,0:T(8,128)(2,1)S(1)} %pad_maximum_fusion.1.refs_4_), channel_id=1, source_target_pairs={{0,1},{1,0},{2,3},{3,2},{4,5},{5,4},{6,7},{7,6},{8,9},{9,8},{10,11... | collective-permute-start | bytes 4718600 | tf_op jit(solution)/shard_map/ppermute | solution.py:22
  75.7 18.0 %collective-permute-start.22 = (bf16[3,4,3,16,512]{4,3,2,1,0:T(8,128)(2,1)S(1)}, bf16[3,4,3,16,512]{4,3,2,1,0:T(8,128)(2,1)S(1)}, u32[]{:S(2)}, u32[]{:S(2)}) collective-permute-start(bf16[3,4,3,16,512]{4,3,2,1,0:T(8,128)(2,1)S(1)} %pad_maximum_fusion.4), channel_id=1, source_target_pairs={{0,8},{1,25},{8,16},{9,1},{16,24},{17,9},{24,0},{25,17},{2,10},{3,... | collective-permute-start | bytes 1769480 | tf_op jit(solution)/shard_map/ppermute | solution.py:31
  78.7 15.0 %collective-permute-start.23 = (bf16[3,4,3,16,512]{4,3,2,1,0:T(8,128)(2,1)S(1)}, bf16[3,4,3,16,512]{4,3,2,1,0:T(8,128)(2,1)S(1)}, u32[]{:S(2)}, u32[]{:S(2)}) collective-permute-start(bf16[3,4,3,16,512]{4,3,2,1,0:T(8,128)(2,1)S(1)} %pad_maximum_fusion.4), channel_id=1, source_target_pairs={{0,24},{1,9},{8,0},{9,17},{16,8},{17,25},{24,16},{25,1},{2,26},{3,... | collective-permute-start | bytes 1769480 | tf_op jit(solution)/shard_map/ppermute | solution.py:31
  80.2 13.6 %collective-permute-start.20 = (f16[528,512]{1,0:T(8,128)(2,1)S(1)}, f16[528,512]{1,0:T(8,128)(2,1)S(1)}, u32[]{:S(2)}, u32[]{:S(2)}) collective-permute-start(f16[528,512]{1,0:T(8,128)(2,1)S(1)} %convert_element_type.15), channel_id=1, source_target_pairs={{0,128},{128,0},{1,129},{129,1},{2,130},{130,2},{3,131},{131,3},{4... | collective-permute-start | bytes 1622024 | tf_op jit(solution)/shard_map/ppermute | solution.py:22
  93.9 16.2 %collective-permute-start.27 = (bf16[9,4,3,16,512]{4,3,2,1,0:T(8,128)(2,1)S(1)}, bf16[9,4,3,16,512]{4,3,2,1,0:T(8,128)(2,1)S(1)}, u32[]{:S(2)}, u32[]{:S(2)}) collective-permute-start(bf16[9,4,3,16,512]{4,3,2,1,0:T(8,128)(2,1)S(1)} %slice_dynamic-update-slice_fusion.refs_5_), channel_id=1, source_target_pairs={{0,1},{1,0},{2,3},{3,2},{4,5},{5,4},{6,7},{7,6},{8,9},{9,8},{10,11... | collective-permute-start | bytes 5308424 | tf_op jit(solution)/shard_map/ppermute | solution.py:22
  95.2 9.1 %collective-permute-start.25 = (bf16[3,4,3,16,512]{4,3,2,1,0:T(8,128)(2,1)S(1)}, bf16[3,4,3,16,512]{4,3,2,1,0:T(8,128)(2,1)S(1)}, u32[]{:S(2)}, u32[]{:S(2)}) collective-permute-start(bf16[3,4,3,16,512]{4,3,2,1,0:T(8,128)(2,1)S(1)} %collective-permute-done.22), channel_id=1, source_target_pairs={{0,8},{1,25},{8,16},{9,1},{16,24},{17,9},{24,0},{25,17},{2,10},{3,... | collective-permute-start | bytes 1769480 | tf_op jit(solution)/shard_map/ppermute | solution.py:31
  97.6 12.4 %collective-permute-start.24 = (f16[528,512]{1,0:T(8,128)(2,1)S(1)}, f16[528,512]{1,0:T(8,128)(2,1)S(1)}, u32[]{:S(2)}, u32[]{:S(2)}) collective-permute-start(f16[528,512]{1,0:T(8,128)(2,1)S(1)} %convert_element_type.16), channel_id=1, source_target_pairs={{0,128},{128,0},{1,129},{129,1},{2,130},{130,2},{3,131},{131,3},{4... | collective-permute-start | bytes 1622024 | tf_op jit(solution)/shard_map/ppermute | solution.py:22
  104.3 5.8 %collective-permute-start.28 = (bf16[3,4,3,16,512]{4,3,2,1,0:T(8,128)(2,1)S(1)}, bf16[3,4,3,16,512]{4,3,2,1,0:T(8,128)(2,1)S(1)}, u32[]{:S(2)}, u32[]{:S(2)}) collective-permute-start(bf16[3,4,3,16,512]{4,3,2,1,0:T(8,128)(2,1)S(1)} %collective-permute-done.25.refs_6_), channel_id=1, source_target_pairs={{0,1},{1,0},{2,3},{3,2},{4,5},{5,4},{6,7},{7,6},{8,9},{9,8},{10,11... | collective-permute-start | bytes 1769480 | tf_op jit(solution)/shard_map/ppermute | solution.py:22
  110.0 2.4 %collective-permute-start.26 = (f32[16,128]{1,0:T(8,128)S(1)}, f32[16,128]{1,0:T(8,128)S(1)}, u32[]{:S(2)}, u32[]{:S(2)}) collective-permute-start(f32[16,128]{1,0:T(8,128)S(1)} %slice_convert_fusion), channel_id=1, source_target_pairs={{0,1},{1,0},{2,3},{3,2},{4,5},{5,4},{6,7},{7,6},{8,9},{9,8},{10,11... | collective-permute-start | bytes 24584 | tf_op jit(solution)/shard_map/ppermute | solution.py:22
